TPU v7x, 32 devices: a whole 2x2x4 slice. The times are simulated.
32 devices in a mesh: mod: 4 (over z), row: 8 (over y, x, core).
Axes of the slice: x: 2, y: 2, z: 4, core: 2. Of those that a mesh axis runs over, the one named last changes fastest.
Arguments:
- activations: bfloat16 [4, 8192, 4096], P('mod', 'row'), may hold values from -6 to 6
- out_grads: bfloat16 [4, 8192, 4096], P('mod', 'row'), may hold values from -0.3125 to 0.3125
- in_projection: bfloat16 [4, 64, 4096], P('mod'), may hold values from -0.09375 to 0.09375
- out_projection: bfloat16 [4, 64, 4096], P('mod'), may hold values from -0.09375 to 0.09375
- inv_curvature: bfloat16 [4, 4096, 4096], P('mod', 'row'), as said below
- store_grads: bfloat16 [4, 6144, 4096], P('mod', 'row'), may hold values from -0.046875 to 0.046875
- lengths: int32 [32], replicated, may hold values from 64 to 128, as said below
- owners: int32 [32], replicated, may hold values from 0 to 7, as said below
Outputs:
- scores: float32 [32, 6144], P('mod', 'row')
Inputs may be any that keep to these rules, and one draw needn't show every extreme that they name: `owners`: at most 8 query examples have the same owner, and some owner has exactly 8. `lengths`: the examples of one owner hold at most 1024 tokens together, and some owner holds exactly 1024. `inv_curvature`: each module's matrix is symmetric.
All inputs are finite; a program needn't handle non-finite values.
Results may differ from a plain program's by a relative error of at most 0.0041.
Values may be sent and summed in bfloat16 or wider, within the bound.
No kernel may reach another device: no remote copies, remote signals or barrier semaphores. Data moves between devices by JAX's collectives and lax.ppermute only.
A program may use at most 128 MiB of HBM per device.

v0:
```python
import jax
import jax.numpy as jnp
from jax import lax
from jax.sharding import PartitionSpec as P

exact_mode = lax.Precision.HIGHEST


def contract_last(left, right):
    return lax.dot_general(
        left, right, (((1,), (1,)), ((), ())), preferred_element_type=jnp.float32
    )


def on_device(
    activations,
    out_grads,
    in_projection,
    out_projection,
    inv_curvature,
    store_grads,
    lengths,
    owners,
):
    row_id = lax.axis_index("row")
    row_count = lax.axis_size("row")
    mod_count = lax.axis_size("mod")
    queries = lengths.shape[0]
    tok_rows = activations.shape[1]
    rank = in_projection.shape[1]
    width = rank * rank
    capacity = 2 * queries // row_count
    examples = jnp.arange(queries, dtype=jnp.int32)
    earlier = (owners[:, None] == owners[None, :]) & (examples[None, :] < examples[:, None])
    offsets = jnp.sum(jnp.where(earlier, lengths[None, :], 0), axis=1)
    slot_rank = jnp.sum(earlier.astype(jnp.int32), axis=1)
    owned_here = owners == row_id
    slot_ids = jnp.arange(capacity, dtype=jnp.int32)
    chosen = owned_here[None, :] & (slot_rank[None, :] == slot_ids[:, None])
    slot_start = jnp.sum(jnp.where(chosen, offsets[None, :], 0), axis=1)
    slot_length = jnp.sum(jnp.where(chosen, lengths[None, :], 0), axis=1)
    positions = jnp.arange(tok_rows, dtype=jnp.int32)
    slot_member = (
        (positions[None, :] >= slot_start[:, None])
        & (positions[None, :] < (slot_start + slot_length)[:, None])
    ).astype(jnp.float32)
    in_feat = contract_last(activations[0], in_projection[0])
    out_feat = contract_last(out_grads[0], out_projection[0])
    weighted = slot_member[:, None, :] * out_feat.T[None, :, :]
    per_slot = jnp.dot(
        weighted.reshape(capacity * rank, tok_rows), in_feat, precision=exact_mode
    ).reshape(capacity, width)
    store_rows = store_grads[0]
    curvature_rows = inv_curvature[0]
    all_slots = jnp.arange(row_count * capacity, dtype=jnp.int32)
    placer = (owners * capacity + slot_rank)[:, None] == all_slots[None, :]
    gathered = lax.all_gather(per_slot.astype(jnp.bfloat16), "row", axis=0, tiled=True)
    whole = jnp.dot(
        placer.astype(jnp.bfloat16), gathered, preferred_element_type=jnp.float32
    ).astype(jnp.bfloat16)
    column_part = contract_last(whole, curvature_rows).astype(jnp.bfloat16)
    scores = contract_last(lax.all_gather(column_part, "row", axis=1, tiled=True), store_rows)
    share = queries // mod_count
    everything = lax.psum(scores, "mod")
    total = lax.dynamic_slice_in_dim(everything, lax.axis_index("mod") * share, share, 0)
    return total


def solution(mesh):
    return jax.shard_map(
        on_device,
        mesh=mesh,
        in_specs=(
            P("mod", "row", None),
            P("mod", "row", None),
            P("mod", None, None),
            P("mod", None, None),
            P("mod", "row", None),
            P("mod", "row", None),
            P(),
            P(),
        ),
        out_specs=P("mod", "row"),
        check_vma=False,
    )
```

profile of v0, /device:TPU:0, one launch (start us, length us, event | category | flops | bytes accessed | tf_op | source)
XLA Modules:
  0.0 94.7 jit_solution(4259235042864467235)
XLA Ops:
  6.5 0.0 copy-start
  6.5 0.0 copy-start.2
  6.5 0.0 all-reduce.2.cloned.1.call-start
  6.5 1.0 %convert_reduce_fusion = (s32[32]{0:T(128)S(1)}, s32[32]{0:T(128)S(1)}) fusion(s32[32]{0:T(128)} %param.15, s32[32]{0:T(128)} %param.14), kind=kLoop, calls=%fused_computation.20 | loop fusion | flops 7104 | bytes 512 | tf_op jit(solution)/shard_map/reduce_sum | solution.py:36
  7.6 1.2 %broadcast_compare_fusion = pred[32]{0:T(512)(128)(4,1)S(1)} fusion(s32[32]{0:T(128)} %param.15, s32[]{:T(128)S(6)} %axis_index.22), kind=kLoop, calls=%fused_computation.29 | loop fusion | flops 32 | bytes 164 | tf_op jit(solution)/shard_map/eq | solution.py:37
  8.7 0.9 multiply_add_fusion
  9.6 0.8 select_reduce_fusion.1
  10.4 0.1 fusion.14
  10.5 0.0 copy-done
  10.5 6.0 %fusion.2 = f32[64,1024]{1,0:T(8,128)S(1)} fusion(bf16[1,1024,4096]{2,1,0:T(8,128)(2,1)} %param.9, bf16[1,64,4096]{2,1,0:T(8,128)(2,1)S(1)} %copy-done), kind=kOutput, calls=%fused_computation.2 | convolution fusion | flops 536870912 | bytes 9175040 | tf_op jit(solution)/shard_map/dot_general | solution.py:10
  16.6 0.3 broadcast_multiply_fusion
  16.9 0.0 copy-done.2
  16.9 0.0 copy-done.1
  16.9 2.7 %fusion = f32[1024,64]{0,1:T(8,128)S(1)} fusion(bf16[1,1024,4096]{2,1,0:T(8,128)(2,1)S(1)} %copy-done.1, bf16[1,64,4096]{2,1,0:T(8,128)(2,1)S(1)} %copy-done.2), kind=kOutput, calls=%fused_computation | convolution fusion | flops 536870912 | bytes 9175040 | tf_op jit(solution)/shard_map/dot_general | solution.py:10
  19.5 2.2 %convolution_convert_fusion.1 = bf16[512,64]{0,1:T(8,128)(2,1)S(1)} fusion(f32[512,1024]{1,0:T(8,128)S(1)} %bitcast.25, f32[1024,64]{0,1:T(8,128)S(1)} %fusion), kind=kOutput, calls=%fused_computation.9 | convolution fusion | flops 402685952 | bytes 2424832 | tf_op jit(solution)/shard_map/dot_general | solution.py:50
  21.7 0.1 copy.10
  21.8 0.2 convert_element_type.26
  22.0 11.3 %all_gather.6 = bf16[64,4096]{1,0:T(8,128)(2,1)S(1)} all-gather(bf16[8,4096]{1,0:T(8,128)(2,1)S(1)} %convert_element_type.26), channel_id=1, replica_groups=mesh['mod'=4,'row'=8] {'row'}, dimensions={0}, use_global_device_ids=true | all-gather | bytes 589824 | tf_op jit(solution)/shard_map/all_gather | solution.py:57
  33.3 3.7 %fusion.8 = bf16[32,512]{1,0:T(8,128)(2,1)S(1)} fusion(bf16[1,512,4096]{2,1,0:T(8,128)(2,1)} %param.12, bf16[64,4096]{1,0:T(8,128)(2,1)S(1)} %all_gather.6, s32[32]{0:T(128)S(1)} %multiply_add_fusion), kind=kOutput, calls=%fused_computation.10 | convolution fusion | flops 151144448 | bytes 4751488 | tf_op jit(solution)/shard_map/dot_general | solution.py:10
  37.0 9.3 %all_gather.7 = bf16[32,4096]{1,0:T(8,128)(2,1)S(1)} all-gather(bf16[32,512]{1,0:T(8,128)(2,1)S(1)} %fusion.8), channel_id=1, replica_groups=mesh['mod'=4,'row'=8] {'row'}, dimensions={1}, use_global_device_ids=true | all-gather | bytes 294912 | tf_op jit(solution)/shard_map/all_gather | solution.py:62
  46.3 5.4 %fusion.4 = f32[32,768]{1,0:T(8,128)} fusion(bf16[32,4096]{1,0:T(8,128)(2,1)S(1)} %all_gather.7, bf16[1,768,4096]{2,1,0:T(8,128)(2,1)} %param.13), kind=kOutput, calls=%fused_computation.4 | convolution fusion | flops 201326592 | bytes 6651904 | tf_op jit(solution)/shard_map/dot_general | solution.py:10
  51.7 0.0 all-reduce.2.cloned.1.call-update
  51.7 34.7 %all-reduce.2.cloned.1.call-done = f32[32,768]{1,0:T(8,128)} async-done(((f32[32,768]{1,0:T(8,128)}), f32[32,768]{1,0:T(8,128)}) %all-reduce.2.cloned.1.call-update) | async-done | bytes 98320 | tf_op jit(solution)/shard_map/psum | solution.py:64
  86.5 1.3 %constant_dynamic-slice_fusion = f32[8,768]{1,0:T(8,128)} fusion(f32[32,768]{1,0:T(8,128)} %all-reduce.2.cloned.1.call-done, s32[]{:T(128)S(6)} %select_n.17), kind=kLoop, calls=%fused_computation.30 | loop fusion | bytes 49156 | tf_op jit(solution)/shard_map/dynamic_slice | solution.py:65
  (2 shorter events, 0.0 us)
Async XLA Ops:
  6.5 4.0 %copy-start = (bf16[1,64,4096]{2,1,0:T(8,128)(2,1)S(1)}, bf16[1,64,4096]{2,1,0:T(8,128)(2,1)}, u32[]{:S(2)}) copy-start(bf16[1,64,4096]{2,1,0:T(8,128)(2,1)} %param.11) | copy-start | bytes 1572868
  6.5 10.3 %copy-start.2 = (bf16[1,64,4096]{2,1,0:T(8,128)(2,1)S(1)}, bf16[1,64,4096]{2,1,0:T(8,128)(2,1)}, u32[]{:S(2)}) copy-start(bf16[1,64,4096]{2,1,0:T(8,128)(2,1)} %param.10) | copy-start | bytes 1572868
  6.5 79.9 %all-reduce.2.cloned.1.call-start = ((), (), s32[]{:S(2)}) async-start(), calls=%async_computation | async-start | bytes 196608 | tf_op jit(solution)/shard_map/psum | solution.py:64
  6.5 10.3 %copy-start.1 = (bf16[1,1024,4096]{2,1,0:T(8,128)(2,1)S(1)}, bf16[1,1024,4096]{2,1,0:T(8,128)(2,1)}, u32[]{:S(2)}) copy-start(bf16[1,1024,4096]{2,1,0:T(8,128)(2,1)} %param.8) | copy-start | bytes 25165828
Sparse Core Ops, SparseCore 0:
  51.9 34.5 all-reduce.1
where the time goes:
time: 95 us; the launch traced here: 94.7 us
  waiting for transfers between devices  34.7 us (37%)
  blocking collectives  20.6 us (22%)
  matrix products  20 us (21%)
  between operations  13.4 us (14%)
  other arithmetic  4.24 us (4%)
  local copies, waits for them, and re-layouts  1.66 us (2%)
    psum x1, waiting for transfers between devices, on_device(): everything = lax.psum(scores, 'mod')  34.7 us
    dot_general x4, matrix products, contract_last(): lax.dot_general(left, right, (((1,), (1,)), ((), ())), preferred_element_...  17.8 us
    all_gather x1, blocking collectives, on_device(): lax.all_gather(per_slot.astype(jnp.bfloat16), 'row', axis=0, tiled=True)  11.3 us
    all_gather x1, blocking collectives, on_device(): lax.all_gather(column_part, 'row', axis=1, tiled=True)  9.3 us
    dot_general x1, matrix products, on_device(): jnp.dot(weighted.reshape(capacity * rank, tok_rows), in_feat, precision=e...  2.16 us
  transfers between devices with their start and end apart: 1, of which 1 were waited for; matrix products, arithmetic and copies ran while one was open for 0% of the time, Pallas kernels for 0%

commit v1 on v0

v1 whole, which is shorter than its diff:
```python
import functools

import jax
import jax.numpy as jnp
from jax import lax
from jax.experimental import pallas as pl
from jax.experimental.pallas import tpu as pltpu
from jax.sharding import PartitionSpec as P

MIB = 1024 * 1024


def contract_last(left, right):
    return lax.dot_general(
        left, right, (((1,), (1,)), ((), ())), preferred_element_type=jnp.float32
    )


def largest_tile(extent, most):
    tile = min(extent, most)
    while extent % tile:
        tile -= 1
    return tile


def split_two(values):
    high = values.astype(jnp.bfloat16).astype(jnp.float32)
    return high, values - high


def featurize_kernel(
    lengths_ref,
    owners_ref,
    act_ref,
    grad_ref,
    in_proj_ref,
    out_proj_ref,
    feature_ref,
    placer_ref,
    total,
    starts,
    stops,
    counts,
):
    step = pl.program_id(0)
    tile = act_ref.shape[0]
    rank = in_proj_ref.shape[0]
    capacity = feature_ref.shape[0]
    queries, slots = placer_ref.shape

    @pl.when(step == 0)
    def _():
        me = lax.axis_index("row")
        for slot in range(capacity):
            starts[slot] = 0
            stops[slot] = 0
        for owner in range(slots // capacity):
            counts[owner] = 0
        used = jnp.int32(0)
        lane = lax.broadcasted_iota(jnp.int32, (1, slots), 1)
        for example in range(queries):
            owner = owners_ref[example]
            length = lengths_ref[example]
            rank_here = counts[owner]
            counts[owner] = rank_here + 1
            mine = owner == me

            @pl.when(mine)
            def _():
                starts[rank_here] = used
                stops[rank_here] = used + length

            used = used + jnp.where(mine, length, 0)
            placer_ref[pl.ds(example, 1), :] = (
                lane == owner * capacity + rank_here
            ).astype(jnp.float32)
        total[...] = jnp.zeros_like(total)

    in_feat = contract_last(act_ref[...], in_proj_ref[...])
    out_feat = contract_last(grad_ref[...], out_proj_ref[...]).T
    slot_id = lax.broadcasted_iota(jnp.int32, (capacity, tile), 0)
    position = step * tile + lax.broadcasted_iota(jnp.int32, (capacity, tile), 1)
    start = jnp.zeros((capacity, tile), jnp.int32)
    stop = jnp.zeros((capacity, tile), jnp.int32)
    for slot in range(capacity):
        start = jnp.where(slot_id == slot, starts[slot], start)
        stop = jnp.where(slot_id == slot, stops[slot], stop)
    member = ((position >= start) & (position < stop)).astype(jnp.float32)
    in_high, in_low = (part.astype(jnp.bfloat16) for part in split_two(in_feat))
    out_high, out_low = (
        (part[:, None, :] * member[None, :, :])
        .reshape(rank * capacity, tile)
        .astype(jnp.bfloat16)
        for part in split_two(out_feat)
    )
    total[...] += (
        jnp.dot(out_high, in_high, preferred_element_type=jnp.float32)
        + jnp.dot(out_high, in_low, preferred_element_type=jnp.float32)
        + jnp.dot(out_low, in_high, preferred_element_type=jnp.float32)
    )

    @pl.when(step == pl.num_programs(0) - 1)
    def _():
        per_store = 2
        for first in range(0, rank, per_store):
            rows = [
                total[pl.ds((first + k) * capacity, capacity), :] for k in range(per_store)
            ]
            feature_ref[:, pl.ds(first * rank, per_store * rank)] = jnp.concatenate(
                rows, axis=1
            ).astype(jnp.bfloat16)


def featurize(activations, out_grads, in_projection, out_projection, lengths, owners, capacity, slots):
    tokens, width = activations.shape
    rank = in_projection.shape[0]
    queries = lengths.shape[0]
    tile = largest_tile(tokens, 256)
    whole = lambda step: (0, 0)
    return pl.pallas_call(
        featurize_kernel,
        grid=(tokens // tile,),
        in_specs=[
            pl.BlockSpec(memory_space=pltpu.SMEM),
            pl.BlockSpec(memory_space=pltpu.SMEM),
            pl.BlockSpec((tile, width), lambda step: (step, 0)),
            pl.BlockSpec((tile, width), lambda step: (step, 0)),
            pl.BlockSpec((rank, width), whole),
            pl.BlockSpec((rank, width), whole),
        ],
        out_specs=[
            pl.BlockSpec((capacity, rank * rank), whole),
            pl.BlockSpec((queries, slots), whole),
        ],
        out_shape=[
            jax.ShapeDtypeStruct((capacity, rank * rank), jnp.bfloat16),
            jax.ShapeDtypeStruct((queries, slots), jnp.float32),
        ],
        scratch_shapes=[
            pltpu.VMEM((rank * capacity, rank), jnp.float32),
            pltpu.SMEM((capacity,), jnp.int32),
            pltpu.SMEM((capacity,), jnp.int32),
            pltpu.SMEM((slots // capacity,), jnp.int32),
        ],
        compiler_params=pltpu.CompilerParams(vmem_limit_bytes=32 * MIB),
        name="featurize",
    )(lengths, owners, activations, out_grads, in_projection, out_projection)


def precondition_kernel(feature_ref, curvature_ref, placer_ref, out_ref, total):
    step = pl.program_id(0)

    @pl.when(step == 0)
    def _():
        total[...] = jnp.zeros_like(total)

    total[...] += contract_last(feature_ref[...], curvature_ref[...])

    @pl.when(step == pl.num_programs(0) - 1)
    def _():
        out_ref[...] = jnp.dot(
            placer_ref[...].astype(jnp.bfloat16),
            total[...].astype(jnp.bfloat16),
            preferred_element_type=jnp.float32,
        ).astype(jnp.bfloat16)


def precondition(gathered, curvature_rows, placer):
    slots, entries = gathered.shape
    columns = curvature_rows.shape[0]
    queries = placer.shape[0]
    depth = largest_tile(entries, 1024)
    return pl.pallas_call(
        precondition_kernel,
        grid=(entries // depth,),
        in_specs=[
            pl.BlockSpec((slots, depth), lambda step: (0, step)),
            pl.BlockSpec((columns, depth), lambda step: (0, step)),
            pl.BlockSpec((queries, slots), lambda step: (0, 0)),
        ],
        out_specs=pl.BlockSpec((queries, columns), lambda step: (0, 0)),
        out_shape=jax.ShapeDtypeStruct((queries, columns), jnp.bfloat16),
        scratch_shapes=[pltpu.VMEM((slots, columns), jnp.float32)],
        compiler_params=pltpu.CompilerParams(vmem_limit_bytes=32 * MIB),
        name="precondition",
    )(gathered, curvature_rows, placer)


def score_kernel(parts, part_ref, store_ref, keep_ref, send_ref, total):
    step = pl.program_id(0)
    share = keep_ref.shape[1]

    @pl.when(step == 0)
    def _():
        total[...] = jnp.zeros_like(total)

    total[...] += contract_last(part_ref[...], store_ref[...])

    @pl.when(step == pl.num_programs(0) - 1)
    def _():
        me = lax.axis_index("mod")
        for place in range(parts):
            row = pl.multiple_of((me ^ place) * share, share)
            block = total[pl.ds(row, share), :]
            if place % 2:
                send_ref[place // 2] = block
            else:
                keep_ref[place // 2] = block


def score(preconditioned, store_rows, queries, parts):
    stores, entries = store_rows.shape
    depth = preconditioned.shape[1]
    share = queries // parts
    half = jax.ShapeDtypeStruct((parts // 2, share, stores), jnp.float32)
    half_spec = pl.BlockSpec((parts // 2, share, stores), lambda step: (0, 0, 0))
    return pl.pallas_call(
        functools.partial(score_kernel, parts),
        grid=(entries // depth,),
        in_specs=[
            pl.BlockSpec((queries, depth), lambda step: (step, 0)),
            pl.BlockSpec((stores, depth), lambda step: (0, step)),
        ],
        out_specs=[half_spec, half_spec],
        out_shape=[half, half],
        scratch_shapes=[pltpu.VMEM((queries, stores), jnp.float32)],
        compiler_params=pltpu.CompilerParams(vmem_limit_bytes=32 * MIB),
        name="score",
    )(preconditioned, store_rows)


def on_device(
    activations,
    out_grads,
    in_projection,
    out_projection,
    inv_curvature,
    store_grads,
    lengths,
    owners,
):
    row_count = lax.axis_size("row")
    mod_count = lax.axis_size("mod")
    queries = lengths.shape[0]
    capacity = 2 * queries // row_count
    feature, placer = featurize(
        activations[0],
        out_grads[0],
        in_projection[0],
        out_projection[0],
        lengths,
        owners,
        capacity,
        row_count * capacity,
    )
    gathered = lax.all_gather(feature, "row", axis=0, tiled=True)
    column_part = precondition(gathered, inv_curvature[0], placer)
    preconditioned = lax.all_gather(column_part, "row", axis=0, tiled=True)
    keep, send = score(preconditioned, store_grads[0], queries, mod_count)
    distance = 1
    while True:
        arrived = lax.ppermute(
            send, "mod", [(i, i ^ distance) for i in range(mod_count)]
        )
        summed = keep + arrived
        distance *= 2
        if distance == mod_count:
            return summed[0]
        keep, send = summed[0::2], summed[1::2]


def solution(mesh):
    return jax.shard_map(
        on_device,
        mesh=mesh,
        in_specs=(
            P("mod", "row", None),
            P("mod", "row", None),
            P("mod", None, None),
            P("mod", None, None),
            P("mod", "row", None),
            P("mod", "row", None),
            P(),
            P(),
        ),
        out_specs=P("mod", "row"),
        check_vma=False,
    )
```

time: 95 us -> 54.1 us (0.57)
  waiting for transfers between devices: 34.7 us -> 4.66 us
  matrix products: 20 us -> 0 us
  Pallas kernels: 0 us -> 13.4 us
  between operations: 13.4 us -> 0.03 us
  local copies, waits for them, and re-layouts: 1.66 us -> 10.2 us
  starting transfers between devices: 0.01 us -> 4.28 us
  other arithmetic: 4.24 us -> 0.62 us
    psum x1 -> x0, waiting for transfers between devices: 34.7 us -> none  [on_device(): everything = lax.psum(scores, 'mod')]
    dot_general x5 -> x0, matrix products: 20 us -> none  [the longest x4 17.8 us: contract_last(): lax.dot_general(left, right, (((1,), (1,)), ((), ())), preferred_element_...]
    pallas_call x0 -> x3, Pallas kernels: none -> 13.4 us  [the longest x1 7.93 us: featurize(): pl.pallas_call(featurize_kernel, grid=(tokens // tile,), in_specs=[pl.Blo...]
    unnamed x6 -> x16, local copies, waits for them, and re-layouts: 0.01 us -> 10.2 us
    ppermute x0 -> x2, waiting for transfers between devices: none -> 4.66 us  [on_device(): lax.ppermute(send, 'mod', [(i, i ^ distance) for i in range(mod_count)])]
    ppermute x0 -> x2, starting transfers between devices: none -> 4.28 us  [on_device(): lax.ppermute(send, 'mod', [(i, i ^ distance) for i in range(mod_count)])]
    reduce_sum x2 -> x0, other arithmetic: 1.82 us -> none  [the longest x1 1.02 us: on_device(): slot_rank = jnp.sum(earlier.astype(jnp.int32), axis=1)]
    dynamic_slice x1 -> x0, local copies, waits for them, and re-layouts: 1.35 us -> none  [on_device(): lax.dynamic_slice_in_dim(everything, lax.axis_index('mod') * share, share...]
  transfers between devices with their start and end apart: 1 -> 2, of which waited for: 1 -> 2; matrix products, arithmetic and copies ran while one was open for 0% -> 0% of each run, Pallas kernels for 0% -> 0%
where the time goes in v1:
time: 54.1 us; the launch traced here: 53.8 us
  blocking collectives  20.6 us (38%)
  Pallas kernels  13.4 us (25%)
  local copies, waits for them, and re-layouts  10.2 us (19%)
  waiting for transfers between devices  4.66 us (9%)
  starting transfers between devices  4.28 us (8%)
  other arithmetic  0.62 us (1%)
    all_gather x1, blocking collectives, on_device(): gathered = lax.all_gather(feature, 'row', axis=0, tiled=True)  11.3 us
    unnamed x16, local copies, waits for them, and re-layouts  10.2 us
    all_gather x1, blocking collectives, on_device(): preconditioned = lax.all_gather(column_part, 'row', axis=0, tiled=True)  9.3 us
    pallas_call x1, Pallas kernels, featurize(): pl.pallas_call(featurize_kernel, grid=(tokens // tile,), in_specs=[pl.Blo...  7.93 us
    ppermute x2, waiting for transfers between devices, on_device(): lax.ppermute(send, 'mod', [(i, i ^ distance) for i in range(mod_count)])  4.66 us
    ppermute x2, starting transfers between devices, on_device(): lax.ppermute(send, 'mod', [(i, i ^ distance) for i in range(mod_count)])  4.28 us
    pallas_call x1, Pallas kernels, score(): pl.pallas_call(functools.partial(score_kernel, parts), grid=(entries // d...  3.25 us
    pallas_call x1, Pallas kernels, precondition(): pl.pallas_call(precondition_kernel, grid=(entries // depth,), in_specs=[p...  2.25 us
  transfers between devices with their start and end apart: 2, of which 2 were waited for; matrix products, arithmetic and copies ran while one was open for 0% of the time, Pallas kernels for 0%

profile of v1, /device:TPU:0, one launch (start us, length us, event | category | flops | bytes accessed | tf_op | source)
XLA Modules:
  0.0 53.8 jit_solution(8997573303532866672)
XLA Ops:
  0.0 0.0 copy-start
  0.0 3.4 %copy-done = bf16[1,1024,4096]{2,1,0:T(8,128)(2,1)S(1)} copy-done((bf16[1,1024,4096]{2,1,0:T(8,128)(2,1)S(1)}, bf16[1,1024,4096]{2,1,0:T(8,128)(2,1)}, u32[]{:S(2)}) %copy-start) | copy-done | bytes 8388632
  3.4 0.0 copy-start.1
  3.4 3.4 %copy-done.1 = bf16[1,1024,4096]{2,1,0:T(8,128)(2,1)S(1)} copy-done((bf16[1,1024,4096]{2,1,0:T(8,128)(2,1)S(1)}, bf16[1,1024,4096]{2,1,0:T(8,128)(2,1)}, u32[]{:S(2)}) %copy-start.1) | copy-done | bytes 8388632
  6.8 0.0 copy-start.4
  6.8 1.0 %copy-done.4 = bf16[1,64,4096]{2,1,0:T(8,128)(2,1)S(1)} copy-done((bf16[1,64,4096]{2,1,0:T(8,128)(2,1)S(1)}, bf16[1,64,4096]{2,1,0:T(8,128)(2,1)}, u32[]{:S(2)}) %copy-start.4) | copy-done | bytes 524312
  7.8 0.0 copy-start.5
  7.8 1.0 %copy-done.5 = bf16[1,64,4096]{2,1,0:T(8,128)(2,1)S(1)} copy-done((bf16[1,64,4096]{2,1,0:T(8,128)(2,1)S(1)}, bf16[1,64,4096]{2,1,0:T(8,128)(2,1)}, u32[]{:S(2)}) %copy-start.5) | copy-done | bytes 524312
  8.8 0.0 copy-start.6
  8.9 0.7 %copy-done.6 = s32[32]{0:T(128)S(1)} copy-done((s32[32]{0:T(128)S(1)}, s32[32]{0:T(128)}, u32[]{:S(2)}) %copy-start.6) | copy-done | bytes 152
  9.5 0.0 copy-start.7
  9.5 0.7 %copy-done.7 = s32[32]{0:T(128)S(1)} copy-done((s32[32]{0:T(128)S(1)}, s32[32]{0:T(128)}, u32[]{:S(2)}) %copy-start.7) | copy-done | bytes 152
  10.2 7.9 %featurize.1 = (bf16[8,4096]{1,0:T(8,128)(2,1)S(1)}, f32[32,64]{1,0:T(8,128)S(1)}) custom-call(s32[32]{0:T(128)S(1)} %copy-done.6, s32[32]{0:T(128)S(1)} %copy-done.7, bf16[1024,4096]{1,0:T(8,128)(2,1)S(1)} %bitcast.8, bf16[1024,4096]{1,0:T(8,128)(2,1)S(1)} %bitcast.9, bf16[64,4096]{1,0:T(8,128)(2,1)S(1)} %bitcast.12, bf16[64,4096]{1,0:T(8,128)(2,1)S(1)} %bitcast.13), custom_call_target="tpu_custom_call" | custom-call | tf_op jit(solution)/shard_map/featurize/pallas_call | solution.py:120
  18.1 11.3 %all_gather.6.feature_ref = bf16[64,4096]{1,0:T(8,128)(2,1)S(1)} all-gather(bf16[8,4096]{1,0:T(8,128)(2,1)S(1)} %get-tuple-element.9), channel_id=1, replica_groups=mesh['mod'=4,'row'=8] {'row'}, dimensions={0}, use_global_device_ids=true | all-gather | bytes 589824 | tf_op jit(solution)/shard_map/all_gather | solution.py:256
  29.4 0.0 copy-done.3
  29.4 2.3 %precondition.1 = bf16[32,512]{1,0:T(8,128)(2,1)S(1)} custom-call(bf16[64,4096]{1,0:T(8,128)(2,1)S(1)} %all_gather.6.feature_ref, bf16[512,4096]{1,0:T(8,128)(2,1)S(1)} %bitcast.11, f32[32,64]{1,0:T(8,128)S(1)} %get-tuple-element.10.placer_ref), custom_call_target="tpu_custom_call" | custom-call | tf_op jit(solution)/shard_map/precondition/pallas_call | solution.py:173
  31.7 9.3 %all_gather.7.part_ref = bf16[256,512]{1,0:T(8,128)(2,1)S(1)} all-gather(bf16[32,512]{1,0:T(8,128)(2,1)S(1)} %precondition.1), channel_id=1, replica_groups=mesh['mod'=4,'row'=8] {'row'}, dimensions={0}, use_global_device_ids=true | all-gather | bytes 294912 | tf_op jit(solution)/shard_map/all_gather | solution.py:258
  41.0 0.0 copy-done.2
  41.0 3.2 %score.1 = (f32[2,8,768]{2,1,0:T(8,128)S(1)}, f32[2,8,768]{2,1,0:T(8,128)S(1)}) custom-call(bf16[256,512]{1,0:T(8,128)(2,1)S(1)} %all_gather.7.part_ref, bf16[768,4096]{1,0:T(8,128)(2,1)S(1)} %bitcast.10), custom_call_target="tpu_custom_call" | custom-call | tf_op jit(solution)/shard_map/score/pallas_call | solution.py:217
  44.2 1.6 %collective-permute-start = (f32[2,8,768]{2,1,0:T(8,128)S(1)}, f32[2,8,768]{2,1,0:T(8,128)S(1)}, u32[]{:S(2)}, u32[]{:S(2)}) collective-permute-start(f32[2,8,768]{2,1,0:T(8,128)S(1)} %get-tuple-element.12), channel_id=1, source_target_pairs={{0,8},{8,0},{16,24},{24,16},{1,9},{9,1},{17,25},{25,17},{2,10},{10... | collective-permute-start | bytes 147464 | tf_op jit(solution)/shard_map/ppermute | solution.py:262
  45.9 2.5 %collective-permute-done = f32[2,8,768]{2,1,0:T(8,128)S(1)} collective-permute-done((f32[2,8,768]{2,1,0:T(8,128)S(1)}, f32[2,8,768]{2,1,0:T(8,128)S(1)}, u32[]{:S(2)}, u32[]{:S(2)}) %collective-permute-start) | collective-permute-done | bytes 49184 | tf_op jit(solution)/shard_map/ppermute | solution.py:262
  48.4 2.6 %collective-permute-start.1 = (f32[1,8,768]{2,1,0:T(8,128)S(1)}, f32[1,8,768]{2,1,0:T(8,128)S(1)}, u32[]{:S(2)}, u32[]{:S(2)}) collective-permute-start(f32[1,8,768]{2,1,0:T(8,128)S(1)} %slice.11), channel_id=1, source_target_pairs={{0,16},{8,24},{16,0},{24,8},{1,17},{9,25},{17,1},{25,9},{2,18},{10... | collective-permute-start | bytes 73736 | tf_op jit(solution)/shard_map/ppermute | solution.py:262
  51.0 2.1 %collective-permute-done.1 = f32[1,8,768]{2,1,0:T(8,128)S(1)} collective-permute-done((f32[1,8,768]{2,1,0:T(8,128)S(1)}, f32[1,8,768]{2,1,0:T(8,128)S(1)}, u32[]{:S(2)}, u32[]{:S(2)}) %collective-permute-start.1) | collective-permute-done | bytes 24608 | tf_op jit(solution)/shard_map/ppermute | solution.py:262
  53.2 0.6 %fusion = f32[8,768]{1,0:T(8,128)} fusion(f32[1,8,768]{2,1,0:T(8,128)S(1)} %collective-permute-done.1, f32[2,8,768]{2,1,0:T(8,128)S(1)} %add.6), kind=kLoop, calls=%fused_computation.1 | loop fusion | flops 6144 | bytes 73728 | tf_op jit(solution)/shard_map/squeeze | solution.py:268
  (4 shorter events, 0.0 us)
Async XLA Ops:
  0.0 3.4 %copy-start = (bf16[1,1024,4096]{2,1,0:T(8,128)(2,1)S(1)}, bf16[1,1024,4096]{2,1,0:T(8,128)(2,1)}, u32[]{:S(2)}) copy-start(bf16[1,1024,4096]{2,1,0:T(8,128)(2,1)} %param.8) | copy-start | bytes 25165828
  3.4 3.4 %copy-start.1 = (bf16[1,1024,4096]{2,1,0:T(8,128)(2,1)S(1)}, bf16[1,1024,4096]{2,1,0:T(8,128)(2,1)}, u32[]{:S(2)}) copy-start(bf16[1,1024,4096]{2,1,0:T(8,128)(2,1)} %param.9) | copy-start | bytes 25165828
  6.8 1.0 %copy-start.4 = (bf16[1,64,4096]{2,1,0:T(8,128)(2,1)S(1)}, bf16[1,64,4096]{2,1,0:T(8,128)(2,1)}, u32[]{:S(2)}) copy-start(bf16[1,64,4096]{2,1,0:T(8,128)(2,1)} %param.10) | copy-start | bytes 1572868
  7.8 1.0 %copy-start.5 = (bf16[1,64,4096]{2,1,0:T(8,128)(2,1)S(1)}, bf16[1,64,4096]{2,1,0:T(8,128)(2,1)}, u32[]{:S(2)}) copy-start(bf16[1,64,4096]{2,1,0:T(8,128)(2,1)} %param.11) | copy-start | bytes 1572868
  8.8 0.7 %copy-start.6 = (s32[32]{0:T(128)S(1)}, s32[32]{0:T(128)}, u32[]{:S(2)}) copy-start(s32[32]{0:T(128)} %lengths_ref.1) | copy-start | bytes 388
  9.5 0.7 %copy-start.7 = (s32[32]{0:T(128)S(1)}, s32[32]{0:T(128)}, u32[]{:S(2)}) copy-start(s32[32]{0:T(128)} %owners_ref.1) | copy-start | bytes 388
  10.2 19.3 %copy-start.3 = (bf16[1,512,4096]{2,1,0:T(8,128)(2,1)S(1)}, bf16[1,512,4096]{2,1,0:T(8,128)(2,1)}, u32[]{:S(2)}) copy-start(bf16[1,512,4096]{2,1,0:T(8,128)(2,1)} %param.12) | copy-start | bytes 12582916
  10.2 30.8 %copy-start.2 = (bf16[1,768,4096]{2,1,0:T(8,128)(2,1)S(1)}, bf16[1,768,4096]{2,1,0:T(8,128)(2,1)}, u32[]{:S(2)}) copy-start(bf16[1,768,4096]{2,1,0:T(8,128)(2,1)} %param.13) | copy-start | bytes 18874372
  44.2 4.2 %collective-permute-start = (f32[2,8,768]{2,1,0:T(8,128)S(1)}, f32[2,8,768]{2,1,0:T(8,128)S(1)}, u32[]{:S(2)}, u32[]{:S(2)}) collective-permute-start(f32[2,8,768]{2,1,0:T(8,128)S(1)} %get-tuple-element.12), channel_id=1, source_target_pairs={{0,8},{8,0},{16,24},{24,16},{1,9},{9,1},{17,25},{25,17},{2,10},{10... | collective-permute-start | bytes 147464 | tf_op jit(solution)/shard_map/ppermute | solution.py:262
  48.4 4.8 %collective-permute-start.1 = (f32[1,8,768]{2,1,0:T(8,128)S(1)}, f32[1,8,768]{2,1,0:T(8,128)S(1)}, u32[]{:S(2)}, u32[]{:S(2)}) collective-permute-start(f32[1,8,768]{2,1,0:T(8,128)S(1)} %slice.11), channel_id=1, source_target_pairs={{0,16},{8,24},{16,0},{24,8},{1,17},{9,25},{17,1},{25,9},{2,18},{10... | collective-permute-start | bytes 73736 | tf_op jit(solution)/shard_map/ppermute | solution.py:262

commit v2 on v1

--- a/solution.py
+++ b/solution.py
@@ -24,125 +24,168 @@
 
 
 def split_two(values):
-    high = values.astype(jnp.bfloat16).astype(jnp.float32)
-    return high, values - high
+    high = values.astype(jnp.bfloat16)
+    return high, (values - high.astype(jnp.float32)).astype(jnp.bfloat16)
+
+
+def dot(left, right):
+    return jnp.dot(left, right, preferred_element_type=jnp.float32)
+
+
+def chunks_of(units):
+    return [(first, min(2, units - first)) for first in range(0, units, 2)]
 
 
 def featurize_kernel(
+    lengths_hbm,
+    owners_hbm,
+    act_hbm,
+    grad_hbm,
+    in_proj_hbm,
+    out_proj_hbm,
+    feature_ref,
+    placer_ref,
+    act,
+    grad,
+    in_proj,
+    out_proj,
+    in_feat,
+    out_feat,
+    total,
     lengths_ref,
     owners_ref,
-    act_ref,
-    grad_ref,
-    in_proj_ref,
-    out_proj_ref,
-    feature_ref,
-    placer_ref,
-    total,
     starts,
     stops,
     counts,
+    act_sems,
+    grad_sems,
+    first_sems,
 ):
-    step = pl.program_id(0)
-    tile = act_ref.shape[0]
-    rank = in_proj_ref.shape[0]
+    tokens = act.shape[0]
+    rank = in_proj.shape[0]
     capacity = feature_ref.shape[0]
     queries, slots = placer_ref.shape
-
-    @pl.when(step == 0)
-    def _():
-        me = lax.axis_index("row")
-        for slot in range(capacity):
-            starts[slot] = 0
-            stops[slot] = 0
-        for owner in range(slots // capacity):
-            counts[owner] = 0
-        used = jnp.int32(0)
-        lane = lax.broadcasted_iota(jnp.int32, (1, slots), 1)
-        for example in range(queries):
-            owner = owners_ref[example]
-            length = lengths_ref[example]
-            rank_here = counts[owner]
-            counts[owner] = rank_here + 1
-            mine = owner == me
-
-            @pl.when(mine)
-            def _():
-                starts[rank_here] = used
-                stops[rank_here] = used + length
-
-            used = used + jnp.where(mine, length, 0)
-            placer_ref[pl.ds(example, 1), :] = (
-                lane == owner * capacity + rank_here
-            ).astype(jnp.float32)
-        total[...] = jnp.zeros_like(total)
-
-    in_feat = contract_last(act_ref[...], in_proj_ref[...])
-    out_feat = contract_last(grad_ref[...], out_proj_ref[...]).T
-    slot_id = lax.broadcasted_iota(jnp.int32, (capacity, tile), 0)
-    position = step * tile + lax.broadcasted_iota(jnp.int32, (capacity, tile), 1)
-    start = jnp.zeros((capacity, tile), jnp.int32)
-    stop = jnp.zeros((capacity, tile), jnp.int32)
+    unit = tokens // capacity
+    chunks = chunks_of(capacity)
+
+    def copies(index):
+        first, size = chunks[index]
+        rows = pl.ds(first * unit, size * unit)
+        return (
+            pltpu.make_async_copy(act_hbm.at[rows], act.at[rows], act_sems.at[index]),
+            pltpu.make_async_copy(grad_hbm.at[rows], grad.at[rows], grad_sems.at[index]),
+        )
+
+    first_copies = [
+        pltpu.make_async_copy(source, target, first_sems.at[place])
+        for place, (source, target) in enumerate(
+            (
+                (in_proj_hbm, in_proj),
+                (out_proj_hbm, out_proj),
+                (lengths_hbm, lengths_ref),
+                (owners_hbm, owners_ref),
+            )
+        )
+    ]
+    for copy in first_copies:
+        copy.start()
+    for index in range(len(chunks)):
+        for copy in copies(index):
+            copy.start()
+
+    for copy in first_copies[2:]:
+        copy.wait()
+    me = lax.axis_index("row")
     for slot in range(capacity):
-        start = jnp.where(slot_id == slot, starts[slot], start)
-        stop = jnp.where(slot_id == slot, stops[slot], stop)
-    member = ((position >= start) & (position < stop)).astype(jnp.float32)
-    in_high, in_low = (part.astype(jnp.bfloat16) for part in split_two(in_feat))
-    out_high, out_low = (
-        (part[:, None, :] * member[None, :, :])
-        .reshape(rank * capacity, tile)
-        .astype(jnp.bfloat16)
-        for part in split_two(out_feat)
-    )
-    total[...] += (
-        jnp.dot(out_high, in_high, preferred_element_type=jnp.float32)
-        + jnp.dot(out_high, in_low, preferred_element_type=jnp.float32)
-        + jnp.dot(out_low, in_high, preferred_element_type=jnp.float32)
-    )
-
-    @pl.when(step == pl.num_programs(0) - 1)
-    def _():
-        per_store = 2
-        for first in range(0, rank, per_store):
-            rows = [
-                total[pl.ds((first + k) * capacity, capacity), :] for k in range(per_store)
-            ]
-            feature_ref[:, pl.ds(first * rank, per_store * rank)] = jnp.concatenate(
-                rows, axis=1
-            ).astype(jnp.bfloat16)
+        starts[slot] = 0
+        stops[slot] = 0
+    for owner in range(slots // capacity):
+        counts[owner] = 0
+    used = jnp.int32(0)
+    lane = lax.broadcasted_iota(jnp.int32, (1, slots), 1)
+    for example in range(queries):
+        owner = owners_ref[example]
+        length = lengths_ref[example]
+        rank_here = counts[owner]
+        counts[owner] = rank_here + 1
+        mine = owner == me
+
+        @pl.when(mine)
+        def _():
+            starts[rank_here] = used
+            stops[rank_here] = used + length
+
+        used = used + jnp.where(mine, length, 0)
+        placer_ref[pl.ds(example, 1), :] = (
+            lane == owner * capacity + rank_here
+        ).astype(jnp.float32)
+    in_feat[pl.ds(0, unit), :] = jnp.zeros((unit, rank), jnp.float32)
+    out_feat[:, pl.ds(0, unit)] = jnp.zeros((rank, unit), jnp.float32)
+
+    for copy in first_copies[:2]:
+        copy.wait()
+    for index, (first, size) in enumerate(chunks):
+        for copy in copies(index):
+            copy.wait()
+        rows = pl.ds(first * unit, size * unit)
+        padded = pl.ds((first + 1) * unit, size * unit)
+        in_feat[padded, :] = contract_last(act[rows, :], in_proj[...])
+        out_feat[:, padded] = contract_last(grad[rows, :], out_proj[...]).T
+        for slot in range(first, first + size):
+            start, stop = starts[slot], stops[slot]
+            window = jnp.maximum((stop + unit - 1) // unit - 1, 0) * unit
+            window = pl.multiple_of(window, unit)
+            position = (
+                window - unit + lax.broadcasted_iota(jnp.int32, (rank, 2 * unit), 1)
+            )
+            member = (position >= start) & (position < stop)
+            out_high, out_low = split_two(
+                jnp.where(member, out_feat[:, pl.ds(window, 2 * unit)], 0.0)
+            )
+            in_high, in_low = split_two(in_feat[pl.ds(window, 2 * unit), :])
+            total[pl.ds(slot * rank, rank), :] = (
+                dot(out_high, in_high) + dot(out_high, in_low) + dot(out_low, in_high)
+            )
+    for first in range(0, rank, 2):
+        pair = [
+            total[pl.ds(first + k, capacity, stride=rank), :] for k in range(2)
+        ]
+        feature_ref[:, pl.ds(first * rank, 2 * rank)] = jnp.concatenate(
+            pair, axis=1
+        ).astype(jnp.bfloat16)
 
 
 def featurize(activations, out_grads, in_projection, out_projection, lengths, owners, capacity, slots):
     tokens, width = activations.shape
     rank = in_projection.shape[0]
     queries = lengths.shape[0]
-    tile = largest_tile(tokens, 256)
-    whole = lambda step: (0, 0)
+    unit = tokens // capacity
+    chunks = len(chunks_of(capacity))
     return pl.pallas_call(
         featurize_kernel,
-        grid=(tokens // tile,),
-        in_specs=[
-            pl.BlockSpec(memory_space=pltpu.SMEM),
-            pl.BlockSpec(memory_space=pltpu.SMEM),
-            pl.BlockSpec((tile, width), lambda step: (step, 0)),
-            pl.BlockSpec((tile, width), lambda step: (step, 0)),
-            pl.BlockSpec((rank, width), whole),
-            pl.BlockSpec((rank, width), whole),
-        ],
-        out_specs=[
-            pl.BlockSpec((capacity, rank * rank), whole),
-            pl.BlockSpec((queries, slots), whole),
-        ],
+        in_specs=[pl.BlockSpec(memory_space=pl.ANY)] * 6,
         out_shape=[
             jax.ShapeDtypeStruct((capacity, rank * rank), jnp.bfloat16),
             jax.ShapeDtypeStruct((queries, slots), jnp.float32),
         ],
         scratch_shapes=[
+            pltpu.VMEM((tokens, width), jnp.bfloat16),
+            pltpu.VMEM((tokens, width), jnp.bfloat16),
+            pltpu.VMEM((rank, width), jnp.bfloat16),
+            pltpu.VMEM((rank, width), jnp.bfloat16),
+            pltpu.VMEM((unit + tokens, rank), jnp.float32),
+            pltpu.VMEM((rank, unit + tokens), jnp.float32),
             pltpu.VMEM((rank * capacity, rank), jnp.float32),
+            pltpu.SMEM((queries,), jnp.int32),
+            pltpu.SMEM((queries,), jnp.int32),
             pltpu.SMEM((capacity,), jnp.int32),
             pltpu.SMEM((capacity,), jnp.int32),
             pltpu.SMEM((slots // capacity,), jnp.int32),
+            pltpu.SemaphoreType.DMA((chunks,)),
+            pltpu.SemaphoreType.DMA((chunks,)),
+            pltpu.SemaphoreType.DMA((4,)),
         ],
-        compiler_params=pltpu.CompilerParams(vmem_limit_bytes=32 * MIB),
+        compiler_params=pltpu.CompilerParams(vmem_limit_bytes=56 * MIB),
         name="featurize",
     )(lengths, owners, activations, out_grads, in_projection, out_projection)
 

time: 54.1 us -> 48.2 us (0.89)
  local copies, waits for them, and re-layouts: 10.2 us -> 2.92 us
  Pallas kernels: 13.4 us -> 14.8 us
    unnamed x16 -> x8, local copies, waits for them, and re-layouts: 10.2 us -> 2.91 us
    pallas_call x1, Pallas kernels: 7.93 us -> 9.32 us  [featurize(): pl.pallas_call(featurize_kernel, in_specs=[pl.BlockSpec(memory_space=pl.A...]
where the time goes in v2:
time: 48.2 us; the launch traced here: 47.9 us
  blocking collectives  20.6 us (43%)
  Pallas kernels  14.8 us (31%)
  waiting for transfers between devices  4.66 us (10%)
  starting transfers between devices  4.3 us (9%)
  local copies, waits for them, and re-layouts  2.92 us (6%)
  other arithmetic  0.62 us (1%)
    all_gather x1, blocking collectives, on_device(): gathered = lax.all_gather(feature, 'row', axis=0, tiled=True)  11.6 us
    pallas_call x1, Pallas kernels, featurize(): pl.pallas_call(featurize_kernel, in_specs=[pl.BlockSpec(memory_space=pl.A...  9.32 us
    all_gather x1, blocking collectives, on_device(): preconditioned = lax.all_gather(column_part, 'row', axis=0, tiled=True)  9 us
    ppermute x2, waiting for transfers between devices, on_device(): lax.ppermute(send, 'mod', [(i, i ^ distance) for i in range(mod_count)])  4.66 us
    ppermute x2, starting transfers between devices, on_device(): lax.ppermute(send, 'mod', [(i, i ^ distance) for i in range(mod_count)])  4.3 us
    pallas_call x1, Pallas kernels, score(): pl.pallas_call(functools.partial(score_kernel, parts), grid=(entries // d...  3.25 us
    unnamed x8, local copies, waits for them, and re-layouts  2.91 us
    pallas_call x1, Pallas kernels, precondition(): pl.pallas_call(precondition_kernel, grid=(entries // depth,), in_specs=[p...  2.25 us
  transfers between devices with their start and end apart: 2, of which 2 were waited for; matrix products, arithmetic and copies ran while one was open for 0% of the time, Pallas kernels for 0%

profile of v2, /device:TPU:0, one launch (start us, length us, event | category | flops | bytes accessed | tf_op | source)
XLA Modules:
  0.0 47.9 jit_solution(13861454363421033397)
XLA Ops:
  0.0 0.0 slice-start
  0.0 0.0 slice-start.1
  0.0 9.3 %featurize.1 = (bf16[8,4096]{1,0:T(8,128)(2,1)}, f32[32,64]{1,0:T(8,128)}) custom-call(s32[32]{0:T(128)} %lengths_hbm.1, s32[32]{0:T(128)} %owners_hbm.1, bf16[1024,4096]{1,0:T(8,128)(2,1)} %bitcast.12, bf16[1024,4096]{1,0:T(8,128)(2,1)} %bitcast.13, bf16[64,4096]{1,0:T(8,128)(2,1)} %bitcast.14, bf16[64,4096]{1,0:T(8,128)(2,1)} %bitcast.15), custom_call_target="tpu_custom_call" | custom-call | tf_op jit(solution)/shard_map/featurize/pallas_call | solution.py:164
  9.3 11.6 %all_gather.6.feature_ref = bf16[64,4096]{1,0:T(8,128)(2,1)S(1)} all-gather(bf16[8,4096]{1,0:T(8,128)(2,1)} %get-tuple-element.9), channel_id=1, replica_groups=mesh['mod'=4,'row'=8] {'row'}, dimensions={0}, use_global_device_ids=true | all-gather | bytes 589824 | tf_op jit(solution)/shard_map/all_gather | solution.py:299
  20.9 0.0 copy-start
  20.9 2.2 %copy-done = bf16[1,512,4096]{2,1,0:T(8,128)(2,1)S(1)} copy-done((bf16[1,512,4096]{2,1,0:T(8,128)(2,1)S(1)}, bf16[1,512,4096]{2,1,0:T(8,128)(2,1)}, u32[]{:S(2)}) %copy-start) | copy-done | bytes 4194328
  23.1 0.0 copy-start.1
  23.1 0.7 %copy-done.1 = f32[32,64]{1,0:T(8,128)S(1)} copy-done((f32[32,64]{1,0:T(8,128)S(1)}, f32[32,64]{1,0:T(8,128)}, u32[]{:S(2)}) %copy-start.1) | copy-done | bytes 8216
  23.8 2.3 %precondition.1 = bf16[32,512]{1,0:T(8,128)(2,1)S(1)} custom-call(bf16[64,4096]{1,0:T(8,128)(2,1)S(1)} %all_gather.6.feature_ref, bf16[512,4096]{1,0:T(8,128)(2,1)S(1)} %bitcast.11, f32[32,64]{1,0:T(8,128)S(1)} %copy-done.1), custom_call_target="tpu_custom_call" | custom-call | tf_op jit(solution)/shard_map/precondition/pallas_call | solution.py:216
  26.1 9.0 %all_gather.7.part_ref = bf16[256,512]{1,0:T(8,128)(2,1)S(1)} all-gather(bf16[32,512]{1,0:T(8,128)(2,1)S(1)} %precondition.1), channel_id=1, replica_groups=mesh['mod'=4,'row'=8] {'row'}, dimensions={0}, use_global_device_ids=true | all-gather | bytes 294912 | tf_op jit(solution)/shard_map/all_gather | solution.py:301
  35.1 0.0 slice-done
  35.1 0.0 slice-done.1
  35.1 3.2 %score.1 = (f32[2,8,768]{2,1,0:T(8,128)S(1)}, f32[2,8,768]{2,1,0:T(8,128)S(1)}) custom-call(bf16[256,512]{1,0:T(8,128)(2,1)S(1)} %all_gather.7.part_ref, bf16[768,4096]{1,0:T(8,128)(2,1)S(1)} %bitcast.10), custom_call_target="tpu_custom_call" | custom-call | tf_op jit(solution)/shard_map/score/pallas_call | solution.py:260
  38.4 1.7 %collective-permute-start = (f32[2,8,768]{2,1,0:T(8,128)S(1)}, f32[2,8,768]{2,1,0:T(8,128)S(1)}, u32[]{:S(2)}, u32[]{:S(2)}) collective-permute-start(f32[2,8,768]{2,1,0:T(8,128)S(1)} %get-tuple-element.12), channel_id=1, source_target_pairs={{0,8},{8,0},{16,24},{24,16},{1,9},{9,1},{17,25},{25,17},{2,10},{10... | collective-permute-start | bytes 147464 | tf_op jit(solution)/shard_map/ppermute | solution.py:305
  40.0 2.5 %collective-permute-done = f32[2,8,768]{2,1,0:T(8,128)S(1)} collective-permute-done((f32[2,8,768]{2,1,0:T(8,128)S(1)}, f32[2,8,768]{2,1,0:T(8,128)S(1)}, u32[]{:S(2)}, u32[]{:S(2)}) %collective-permute-start) | collective-permute-done | bytes 49184 | tf_op jit(solution)/shard_map/ppermute | solution.py:305
  42.5 2.6 %collective-permute-start.1 = (f32[1,8,768]{2,1,0:T(8,128)S(1)}, f32[1,8,768]{2,1,0:T(8,128)S(1)}, u32[]{:S(2)}, u32[]{:S(2)}) collective-permute-start(f32[1,8,768]{2,1,0:T(8,128)S(1)} %slice.11), channel_id=1, source_target_pairs={{0,16},{8,24},{16,0},{24,8},{1,17},{9,25},{17,1},{25,9},{2,18},{10... | collective-permute-start | bytes 73736 | tf_op jit(solution)/shard_map/ppermute | solution.py:305
  45.2 2.1 %collective-permute-done.1 = f32[1,8,768]{2,1,0:T(8,128)S(1)} collective-permute-done((f32[1,8,768]{2,1,0:T(8,128)S(1)}, f32[1,8,768]{2,1,0:T(8,128)S(1)}, u32[]{:S(2)}, u32[]{:S(2)}) %collective-permute-start.1) | collective-permute-done | bytes 24608 | tf_op jit(solution)/shard_map/ppermute | solution.py:305
  47.3 0.6 %fusion = f32[8,768]{1,0:T(8,128)} fusion(f32[1,8,768]{2,1,0:T(8,128)S(1)} %collective-permute-done.1, f32[2,8,768]{2,1,0:T(8,128)S(1)} %add.6), kind=kLoop, calls=%fused_computation.1 | loop fusion | flops 6144 | bytes 73728 | tf_op jit(solution)/shard_map/squeeze | solution.py:311
  (3 shorter events, 0.0 us)
Async XLA Ops:
  0.0 35.1 %slice-start = ((s8[6291456]{0:T(1024)(128)(4,1)}), s8[4194304]{0:T(1024)(128)(4,1)S(1)}, s32[]{:S(2)}) async-start(s8[6291456]{0:T(1024)(128)(4,1)} %bitcast.8), calls=%async_computation | async-start | bytes 8388608
  0.0 35.1 %slice-start.1 = ((s8[6291456]{0:T(1024)(128)(4,1)}), s8[2097152]{0:T(1024)(128)(4,1)S(1)}, s32[]{:S(2)}) async-start(s8[6291456]{0:T(1024)(128)(4,1)} %bitcast.8), calls=%async_computation.1 | async-start | bytes 4194304
  20.9 2.2 %copy-start = (bf16[1,512,4096]{2,1,0:T(8,128)(2,1)S(1)}, bf16[1,512,4096]{2,1,0:T(8,128)(2,1)}, u32[]{:S(2)}) copy-start(bf16[1,512,4096]{2,1,0:T(8,128)(2,1)} %param.12) | copy-start | bytes 12582916
  23.1 0.7 %copy-start.1 = (f32[32,64]{1,0:T(8,128)S(1)}, f32[32,64]{1,0:T(8,128)}, u32[]{:S(2)}) copy-start(f32[32,64]{1,0:T(8,128)} %get-tuple-element.10.placer_ref) | copy-start | bytes 24580
  38.4 4.2 %collective-permute-start = (f32[2,8,768]{2,1,0:T(8,128)S(1)}, f32[2,8,768]{2,1,0:T(8,128)S(1)}, u32[]{:S(2)}, u32[]{:S(2)}) collective-permute-start(f32[2,8,768]{2,1,0:T(8,128)S(1)} %get-tuple-element.12), channel_id=1, source_target_pairs={{0,8},{8,0},{16,24},{24,16},{1,9},{9,1},{17,25},{25,17},{2,10},{10... | collective-permute-start | bytes 147464 | tf_op jit(solution)/shard_map/ppermute | solution.py:305
  42.5 4.8 %collective-permute-start.1 = (f32[1,8,768]{2,1,0:T(8,128)S(1)}, f32[1,8,768]{2,1,0:T(8,128)S(1)}, u32[]{:S(2)}, u32[]{:S(2)}) collective-permute-start(f32[1,8,768]{2,1,0:T(8,128)S(1)} %slice.11), channel_id=1, source_target_pairs={{0,16},{8,24},{16,0},{24,8},{1,17},{9,25},{17,1},{25,9},{2,18},{10... | collective-permute-start | bytes 73736 | tf_op jit(solution)/shard_map/ppermute | solution.py:305

commit v3 on v2

v3 whole, which is shorter than its diff:
```python
import functools

import jax
import jax.numpy as jnp
from jax import lax
from jax.experimental import pallas as pl
from jax.experimental.pallas import tpu as pltpu
from jax.sharding import PartitionSpec as P

MIB = 1024 * 1024


def contract_last(left, right):
    return lax.dot_general(
        left, right, (((1,), (1,)), ((), ())), preferred_element_type=jnp.float32
    )


def split_two(values):
    high = values.astype(jnp.bfloat16)
    return high, (values - high.astype(jnp.float32)).astype(jnp.bfloat16)


def dot(left, right):
    return jnp.dot(left, right, preferred_element_type=jnp.float32)


def chunks_of(units):
    return [(first, min(2, units - first)) for first in range(0, units, 2)]


def featurize_kernel(
    lengths_hbm,
    owners_hbm,
    curvature_hbm,
    act_hbm,
    grad_hbm,
    in_proj_hbm,
    out_proj_hbm,
    feature_ref,
    placer_ref,
    curvature_ref,
    act,
    grad,
    in_proj,
    out_proj,
    in_feat,
    out_feat,
    total,
    lengths_ref,
    owners_ref,
    starts,
    stops,
    counts,
    act_sems,
    grad_sems,
    first_sems,
):
    tokens = act.shape[0]
    rank = in_proj.shape[0]
    capacity = feature_ref.shape[0]
    queries, slots = placer_ref.shape
    unit = tokens // capacity
    chunks = chunks_of(capacity)

    def copies(index):
        first, size = chunks[index]
        rows = pl.ds(first * unit, size * unit)
        return (
            pltpu.make_async_copy(act_hbm.at[rows], act.at[rows], act_sems.at[index]),
            pltpu.make_async_copy(grad_hbm.at[rows], grad.at[rows], grad_sems.at[index]),
        )

    first_copies = [
        pltpu.make_async_copy(source, target, first_sems.at[place])
        for place, (source, target) in enumerate(
            (
                (in_proj_hbm, in_proj),
                (out_proj_hbm, out_proj),
                (lengths_hbm, lengths_ref),
                (owners_hbm, owners_ref),
            )
        )
    ]
    for copy in first_copies:
        copy.start()
    for index in range(len(chunks)):
        for copy in copies(index):
            copy.start()

    curvature_copy = pltpu.make_async_copy(curvature_hbm, curvature_ref, first_sems.at[4])
    curvature_copy.start()

    for copy in first_copies[2:]:
        copy.wait()
    me = lax.axis_index("row")
    for slot in range(capacity):
        starts[slot] = 0
        stops[slot] = 0
    for owner in range(slots // capacity):
        counts[owner] = 0
    used = jnp.int32(0)
    lane = lax.broadcasted_iota(jnp.int32, (1, slots), 1)
    for example in range(queries):
        owner = owners_ref[example]
        length = lengths_ref[example]
        rank_here = counts[owner]
        counts[owner] = rank_here + 1
        mine = owner == me

        @pl.when(mine)
        def _():
            starts[rank_here] = used
            stops[rank_here] = used + length

        used = used + jnp.where(mine, length, 0)
        placer_ref[pl.ds(example, 1), :] = (
            lane == owner * capacity + rank_here
        ).astype(jnp.float32)
    in_feat[pl.ds(0, unit), :] = jnp.zeros((unit, rank), jnp.float32)
    out_feat[:, pl.ds(0, unit)] = jnp.zeros((rank, unit), jnp.float32)

    for copy in first_copies[:2]:
        copy.wait()
    for index, (first, size) in enumerate(chunks):
        for copy in copies(index):
            copy.wait()
        rows = pl.ds(first * unit, size * unit)
        padded = pl.ds((first + 1) * unit, size * unit)
        in_feat[padded, :] = contract_last(act[rows, :], in_proj[...])
        out_feat[:, padded] = contract_last(grad[rows, :], out_proj[...]).T
    for slot in range(capacity):
        start, stop = starts[slot], stops[slot]
        window = jnp.maximum((stop + unit - 1) // unit - 1, 0) * unit
        window = pl.multiple_of(window, unit)
        position = (
            window - unit + lax.broadcasted_iota(jnp.int32, (rank, 2 * unit), 1)
        )
        member = (position >= start) & (position < stop)
        out_high, out_low = split_two(
            jnp.where(member, out_feat[:, pl.ds(window, 2 * unit)], 0.0)
        )
        in_high, in_low = split_two(in_feat[pl.ds(window, 2 * unit), :])
        total[pl.ds(slot * rank, rank), :] = (
            dot(out_high, in_high) + dot(out_high, in_low) + dot(out_low, in_high)
        )
    for first in range(0, rank, 2):
        pair = [
            total[pl.ds(first + k, capacity, stride=rank), :] for k in range(2)
        ]
        feature_ref[:, pl.ds(first * rank, 2 * rank)] = jnp.concatenate(
            pair, axis=1
        ).astype(jnp.bfloat16)
    curvature_copy.wait()


def featurize(
    activations, out_grads, in_projection, out_projection, curvature, lengths, owners, capacity, slots
):
    tokens, width = activations.shape
    rank = in_projection.shape[0]
    queries = lengths.shape[0]
    unit = tokens // capacity
    chunks = len(chunks_of(capacity))
    return pl.pallas_call(
        featurize_kernel,
        in_specs=[pl.BlockSpec(memory_space=pl.ANY)] * 7,
        out_shape=[
            pltpu.VMEM((capacity, rank * rank), jnp.bfloat16),
            pltpu.VMEM((queries, slots), jnp.float32),
            pltpu.VMEM(curvature.shape, curvature.dtype),
        ],
        out_specs=[pl.BlockSpec(memory_space=pltpu.VMEM)] * 3,
        scratch_shapes=[
            pltpu.VMEM((tokens, width), jnp.bfloat16),
            pltpu.VMEM((tokens, width), jnp.bfloat16),
            pltpu.VMEM((rank, width), jnp.bfloat16),
            pltpu.VMEM((rank, width), jnp.bfloat16),
            pltpu.VMEM((unit + tokens, rank), jnp.float32),
            pltpu.VMEM((rank, unit + tokens), jnp.float32),
            pltpu.VMEM((rank * capacity, rank), jnp.float32),
            pltpu.SMEM((queries,), jnp.int32),
            pltpu.SMEM((queries,), jnp.int32),
            pltpu.SMEM((capacity,), jnp.int32),
            pltpu.SMEM((capacity,), jnp.int32),
            pltpu.SMEM((slots // capacity,), jnp.int32),
            pltpu.SemaphoreType.DMA((chunks,)),
            pltpu.SemaphoreType.DMA((chunks,)),
            pltpu.SemaphoreType.DMA((5,)),
        ],
        compiler_params=pltpu.CompilerParams(vmem_limit_bytes=51 * MIB),
        name="featurize",
    )(lengths, owners, curvature, activations, out_grads, in_projection, out_projection)


def precondition_kernel(feature_ref, curvature_ref, placer_ref, out_ref):
    by_slot = contract_last(feature_ref[...], curvature_ref[...]).astype(jnp.bfloat16)
    out_ref[...] = dot(placer_ref[...].astype(jnp.bfloat16), by_slot).astype(jnp.bfloat16)


def precondition(gathered, curvature_rows, placer):
    return pl.pallas_call(
        precondition_kernel,
        in_specs=[pl.BlockSpec(memory_space=pltpu.VMEM)] * 3,
        out_specs=pl.BlockSpec(memory_space=pltpu.VMEM),
        out_shape=jax.ShapeDtypeStruct((placer.shape[0], curvature_rows.shape[0]), jnp.bfloat16),
        compiler_params=pltpu.CompilerParams(vmem_limit_bytes=16 * MIB),
        name="precondition",
    )(gathered, curvature_rows, placer)


def score_kernel(parts, part_ref, store_ref, keep_ref, send_ref, total):
    share = keep_ref.shape[1]
    queries, stores = total.shape
    depth = part_ref.shape[1]
    scores = jnp.zeros((queries, stores), jnp.float32)
    for block in range(part_ref.shape[0] // queries):
        scores += contract_last(
            part_ref[pl.ds(block * queries, queries), :],
            store_ref[:, pl.ds(block * depth, depth)],
        )
    total[...] = scores
    me = lax.axis_index("mod")
    for place in range(parts):
        row = pl.multiple_of((me ^ place) * share, share)
        block = total[pl.ds(row, share), :]
        if place % 2:
            send_ref[place // 2] = block
        else:
            keep_ref[place // 2] = block


def score(preconditioned, store_rows, queries, parts):
    stores = store_rows.shape[0]
    half = jax.ShapeDtypeStruct((parts // 2, queries // parts, stores), jnp.float32)
    return pl.pallas_call(
        functools.partial(score_kernel, parts),
        in_specs=[pl.BlockSpec(memory_space=pltpu.VMEM)] * 2,
        out_specs=[pl.BlockSpec(memory_space=pltpu.VMEM)] * 2,
        out_shape=[half, half],
        scratch_shapes=[pltpu.VMEM((queries, stores), jnp.float32)],
        compiler_params=pltpu.CompilerParams(vmem_limit_bytes=16 * MIB),
        name="score",
    )(preconditioned, store_rows)


def on_device(
    activations,
    out_grads,
    in_projection,
    out_projection,
    inv_curvature,
    store_grads,
    lengths,
    owners,
):
    row_count = lax.axis_size("row")
    mod_count = lax.axis_size("mod")
    queries = lengths.shape[0]
    capacity = 2 * queries // row_count
    feature, placer, curvature = featurize(
        activations[0],
        out_grads[0],
        in_projection[0],
        out_projection[0],
        inv_curvature[0],
        lengths,
        owners,
        capacity,
        row_count * capacity,
    )
    gathered = lax.all_gather(feature, "row", axis=0, tiled=True)
    column_part = precondition(gathered, curvature, placer)
    preconditioned = lax.all_gather(column_part, "row", axis=0, tiled=True)
    keep, send = score(preconditioned, store_grads[0], queries, mod_count)
    distance = 1
    while True:
        arrived = lax.ppermute(
            send, "mod", [(i, i ^ distance) for i in range(mod_count)]
        )
        summed = keep + arrived
        distance *= 2
        if distance == mod_count:
            return summed[0]
        keep, send = summed[0::2], summed[1::2]


def solution(mesh):
    return jax.shard_map(
        on_device,
        mesh=mesh,
        in_specs=(
            P("mod", "row", None),
            P("mod", "row", None),
            P("mod", None, None),
            P("mod", None, None),
            P("mod", "row", None),
            P("mod", "row", None),
            P(),
            P(),
        ),
        out_specs=P("mod", "row"),
        check_vma=False,
    )
```

time: 48.2 us -> 42.2 us (0.88)
  Pallas kernels: 14.8 us -> 11.8 us
  local copies, waits for them, and re-layouts: 2.92 us -> 0.01 us
    unnamed x8 -> x4, local copies, waits for them, and re-layouts: 2.91 us -> 0.01 us
    pallas_call x2, Pallas kernels: 5.5 us -> 3.43 us  [the longest x1 1.92 us: score(): pl.pallas_call(functools.partial(score_kernel, parts), in_specs=[pl.Block...]
    pallas_call x1, Pallas kernels: 9.32 us -> 8.41 us  [featurize(): pl.pallas_call(featurize_kernel, in_specs=[pl.BlockSpec(memory_space=pl.A...]
where the time goes in v3:
time: 42.2 us; the launch traced here: 42.1 us
  blocking collectives  20.6 us (49%)
  Pallas kernels  11.8 us (28%)
  waiting for transfers between devices  4.67 us (11%)
  starting transfers between devices  4.29 us (10%)
  other arithmetic  0.62 us (1%)
    all_gather x1, blocking collectives, on_device(): gathered = lax.all_gather(feature, 'row', axis=0, tiled=True)  11.3 us
    all_gather x1, blocking collectives, on_device(): preconditioned = lax.all_gather(column_part, 'row', axis=0, tiled=True)  9.31 us
    pallas_call x1, Pallas kernels, featurize(): pl.pallas_call(featurize_kernel, in_specs=[pl.BlockSpec(memory_space=pl.A...  8.41 us
    ppermute x2, waiting for transfers between devices, on_device(): lax.ppermute(send, 'mod', [(i, i ^ distance) for i in range(mod_count)])  4.67 us
    ppermute x2, starting transfers between devices, on_device(): lax.ppermute(send, 'mod', [(i, i ^ distance) for i in range(mod_count)])  4.29 us
    pallas_call x1, Pallas kernels, score(): pl.pallas_call(functools.partial(score_kernel, parts), in_specs=[pl.Block...  1.92 us
    pallas_call x1, Pallas kernels, precondition(): pl.pallas_call(precondition_kernel, in_specs=[pl.BlockSpec(memory_space=p...  1.51 us
  transfers between devices with their start and end apart: 2, of which 2 were waited for; matrix products, arithmetic and copies ran while one was open for 0% of the time, Pallas kernels for 0%

profile of v3, /device:TPU:0, one launch (start us, length us, event | category | flops | bytes accessed | tf_op | source)
XLA Modules:
  0.0 42.1 jit_solution(77420921619515230)
XLA Ops:
  0.0 0.0 slice-start
  0.0 0.0 slice-start.1
  0.0 8.4 %featurize.1 = (bf16[8,4096]{1,0:T(8,128)(2,1)S(1)}, f32[32,64]{1,0:T(8,128)S(1)}, bf16[512,4096]{1,0:T(8,128)(2,1)S(1)}) custom-call(s32[32]{0:T(128)} %lengths_hbm.1, s32[32]{0:T(128)} %owners_hbm.1, bf16[512,4096]{1,0:T(8,128)(2,1)} %bitcast.13, bf16[1024,4096]{1,0:T(8,128)(2,1)} %bitcast.11, bf16[1024,4096]{1,0:T(8,128)(2,1)} %bitcast.12, ...), custom_call_target="tpu_custom_call" | custom-call | tf_op jit(solution)/shard_map/featurize/pallas_call | solution.py:165
  8.4 11.3 %all_gather.6.feature_ref = bf16[64,4096]{1,0:T(8,128)(2,1)S(1)} all-gather(bf16[8,4096]{1,0:T(8,128)(2,1)S(1)} %get-tuple-element.10), channel_id=1, replica_groups=mesh['mod'=4,'row'=8] {'row'}, dimensions={0}, use_global_device_ids=true | all-gather | bytes 589824 | tf_op jit(solution)/shard_map/all_gather | solution.py:272
  19.7 1.5 %precondition.1 = bf16[32,512]{1,0:T(8,128)(2,1)S(1)} custom-call(bf16[64,4096]{1,0:T(8,128)(2,1)S(1)} %all_gather.6.feature_ref, bf16[512,4096]{1,0:T(8,128)(2,1)S(1)} %get-tuple-element.11.curvature_ref, f32[32,64]{1,0:T(8,128)S(1)} %get-tuple-element.12.placer_ref), custom_call_target="tpu_custom_call" | custom-call | tf_op jit(solution)/shard_map/precondition/pallas_call | solution.py:202
  21.2 9.3 %all_gather.7.part_ref = bf16[256,512]{1,0:T(8,128)(2,1)S(1)} all-gather(bf16[32,512]{1,0:T(8,128)(2,1)S(1)} %precondition.1), channel_id=1, replica_groups=mesh['mod'=4,'row'=8] {'row'}, dimensions={0}, use_global_device_ids=true | all-gather | bytes 294912 | tf_op jit(solution)/shard_map/all_gather | solution.py:274
  30.6 0.0 slice-done
  30.6 0.0 slice-done.1
  30.6 1.9 %score.1 = (f32[2,8,768]{2,1,0:T(8,128)S(1)}, f32[2,8,768]{2,1,0:T(8,128)S(1)}) custom-call(bf16[256,512]{1,0:T(8,128)(2,1)S(1)} %all_gather.7.part_ref, bf16[768,4096]{1,0:T(8,128)(2,1)S(1)} %bitcast.10), custom_call_target="tpu_custom_call" | custom-call | tf_op jit(solution)/shard_map/score/pallas_call | solution.py:236
  32.5 1.6 %collective-permute-start = (f32[2,8,768]{2,1,0:T(8,128)S(1)}, f32[2,8,768]{2,1,0:T(8,128)S(1)}, u32[]{:S(2)}, u32[]{:S(2)}) collective-permute-start(f32[2,8,768]{2,1,0:T(8,128)S(1)} %get-tuple-element.14), channel_id=1, source_target_pairs={{0,8},{8,0},{16,24},{24,16},{1,9},{9,1},{17,25},{25,17},{2,10},{10... | collective-permute-start | bytes 147464 | tf_op jit(solution)/shard_map/ppermute | solution.py:278
  34.1 2.5 %collective-permute-done = f32[2,8,768]{2,1,0:T(8,128)S(1)} collective-permute-done((f32[2,8,768]{2,1,0:T(8,128)S(1)}, f32[2,8,768]{2,1,0:T(8,128)S(1)}, u32[]{:S(2)}, u32[]{:S(2)}) %collective-permute-start) | collective-permute-done | bytes 49184 | tf_op jit(solution)/shard_map/ppermute | solution.py:278
  36.7 2.6 %collective-permute-start.1 = (f32[1,8,768]{2,1,0:T(8,128)S(1)}, f32[1,8,768]{2,1,0:T(8,128)S(1)}, u32[]{:S(2)}, u32[]{:S(2)}) collective-permute-start(f32[1,8,768]{2,1,0:T(8,128)S(1)} %slice.11), channel_id=1, source_target_pairs={{0,16},{8,24},{16,0},{24,8},{1,17},{9,25},{17,1},{25,9},{2,18},{10... | collective-permute-start | bytes 73736 | tf_op jit(solution)/shard_map/ppermute | solution.py:278
  39.3 2.1 %collective-permute-done.1 = f32[1,8,768]{2,1,0:T(8,128)S(1)} collective-permute-done((f32[1,8,768]{2,1,0:T(8,128)S(1)}, f32[1,8,768]{2,1,0:T(8,128)S(1)}, u32[]{:S(2)}, u32[]{:S(2)}) %collective-permute-start.1) | collective-permute-done | bytes 24608 | tf_op jit(solution)/shard_map/ppermute | solution.py:278
  41.5 0.6 %fusion = f32[8,768]{1,0:T(8,128)} fusion(f32[1,8,768]{2,1,0:T(8,128)S(1)} %collective-permute-done.1, f32[2,8,768]{2,1,0:T(8,128)S(1)} %add.6), kind=kLoop, calls=%fused_computation.1 | loop fusion | flops 6144 | bytes 73728 | tf_op jit(solution)/shard_map/squeeze | solution.py:284
  (3 shorter events, 0.0 us)
Async XLA Ops:
  0.0 30.6 %slice-start = ((s8[6291456]{0:T(1024)(128)(4,1)}), s8[4194304]{0:T(1024)(128)(4,1)S(1)}, s32[]{:S(2)}) async-start(s8[6291456]{0:T(1024)(128)(4,1)} %bitcast.8), calls=%async_computation | async-start | bytes 8388608
  0.0 30.6 %slice-start.1 = ((s8[6291456]{0:T(1024)(128)(4,1)}), s8[2097152]{0:T(1024)(128)(4,1)S(1)}, s32[]{:S(2)}) async-start(s8[6291456]{0:T(1024)(128)(4,1)} %bitcast.8), calls=%async_computation.1 | async-start | bytes 4194304
  32.5 4.2 %collective-permute-start = (f32[2,8,768]{2,1,0:T(8,128)S(1)}, f32[2,8,768]{2,1,0:T(8,128)S(1)}, u32[]{:S(2)}, u32[]{:S(2)}) collective-permute-start(f32[2,8,768]{2,1,0:T(8,128)S(1)} %get-tuple-element.14), channel_id=1, source_target_pairs={{0,8},{8,0},{16,24},{24,16},{1,9},{9,1},{17,25},{25,17},{2,10},{10... | collective-permute-start | bytes 147464 | tf_op jit(solution)/shard_map/ppermute | solution.py:278
  36.7 4.8 %collective-permute-start.1 = (f32[1,8,768]{2,1,0:T(8,128)S(1)}, f32[1,8,768]{2,1,0:T(8,128)S(1)}, u32[]{:S(2)}, u32[]{:S(2)}) collective-permute-start(f32[1,8,768]{2,1,0:T(8,128)S(1)} %slice.11), channel_id=1, source_target_pairs={{0,16},{8,24},{16,0},{24,8},{1,17},{9,25},{17,1},{25,9},{2,18},{10... | collective-permute-start | bytes 73736 | tf_op jit(solution)/shard_map/ppermute | solution.py:278

commit v4 on v3

--- a/solution.py
+++ b/solution.py
@@ -115,7 +115,7 @@
 
         used = used + jnp.where(mine, length, 0)
         placer_ref[pl.ds(example, 1), :] = (
-            lane == owner * capacity + rank_here
+            lane == (owner ^ me) * capacity + rank_here
         ).astype(jnp.float32)
     in_feat[pl.ds(0, unit), :] = jnp.zeros((unit, rank), jnp.float32)
     out_feat[:, pl.ds(0, unit)] = jnp.zeros((rank, unit), jnp.float32)
@@ -193,55 +193,74 @@
     )(lengths, owners, curvature, activations, out_grads, in_projection, out_projection)
 
 
-def precondition_kernel(feature_ref, curvature_ref, placer_ref, out_ref):
-    by_slot = contract_last(feature_ref[...], curvature_ref[...]).astype(jnp.bfloat16)
+def precondition_kernel(curvature_ref, placer_ref, *rest):
+    piece_refs, out_ref, feature = rest[:-2], rest[-2], rest[-1]
+    capacity = piece_refs[0].shape[0]
+    for place, piece_ref in enumerate(piece_refs):
+        feature[pl.ds(place * capacity, capacity), :] = piece_ref[...]
+    by_slot = contract_last(feature[...], curvature_ref[...]).astype(jnp.bfloat16)
     out_ref[...] = dot(placer_ref[...].astype(jnp.bfloat16), by_slot).astype(jnp.bfloat16)
 
 
-def precondition(gathered, curvature_rows, placer):
+def precondition(pieces, curvature_rows, placer):
+    capacity, entries = pieces[0].shape
     return pl.pallas_call(
         precondition_kernel,
-        in_specs=[pl.BlockSpec(memory_space=pltpu.VMEM)] * 3,
+        in_specs=[pl.BlockSpec(memory_space=pltpu.VMEM)] * (2 + len(pieces)),
         out_specs=pl.BlockSpec(memory_space=pltpu.VMEM),
-        out_shape=jax.ShapeDtypeStruct((placer.shape[0], curvature_rows.shape[0]), jnp.bfloat16),
+        out_shape=pltpu.VMEM((placer.shape[0], curvature_rows.shape[0]), jnp.bfloat16),
+        scratch_shapes=[pltpu.VMEM((len(pieces) * capacity, entries), jnp.bfloat16)],
         compiler_params=pltpu.CompilerParams(vmem_limit_bytes=16 * MIB),
         name="precondition",
-    )(gathered, curvature_rows, placer)
-
-
-def score_kernel(parts, part_ref, store_ref, keep_ref, send_ref, total):
-    share = keep_ref.shape[1]
+    )(curvature_rows, placer, *pieces)
+
+
+def score_kernel(parts, store_ref, *rest):
+    piece_refs = rest[: -parts - 1]
+    share_refs, total = rest[-parts - 1 : -1], rest[-1]
+    share = share_refs[0].shape[0]
     queries, stores = total.shape
-    depth = part_ref.shape[1]
+    depth = piece_refs[0].shape[1]
+    column = lax.axis_index("row")
     scores = jnp.zeros((queries, stores), jnp.float32)
-    for block in range(part_ref.shape[0] // queries):
-        scores += contract_last(
-            part_ref[pl.ds(block * queries, queries), :],
-            store_ref[:, pl.ds(block * depth, depth)],
-        )
+    for place, piece_ref in enumerate(piece_refs):
+        first = pl.multiple_of((column ^ place) * depth, depth)
+        scores += contract_last(piece_ref[...], store_ref[:, pl.ds(first, depth)])
     total[...] = scores
     me = lax.axis_index("mod")
     for place in range(parts):
         row = pl.multiple_of((me ^ place) * share, share)
-        block = total[pl.ds(row, share), :]
-        if place % 2:
-            send_ref[place // 2] = block
-        else:
-            keep_ref[place // 2] = block
-
-
-def score(preconditioned, store_rows, queries, parts):
+        share_refs[place][...] = total[pl.ds(row, share), :]
+
+
+def score(pieces, store_rows, queries, parts):
     stores = store_rows.shape[0]
-    half = jax.ShapeDtypeStruct((parts // 2, queries // parts, stores), jnp.float32)
+    one = pltpu.VMEM((queries // parts, stores), jnp.float32)
     return pl.pallas_call(
         functools.partial(score_kernel, parts),
-        in_specs=[pl.BlockSpec(memory_space=pltpu.VMEM)] * 2,
-        out_specs=[pl.BlockSpec(memory_space=pltpu.VMEM)] * 2,
-        out_shape=[half, half],
+        in_specs=[pl.BlockSpec(memory_space=pltpu.VMEM)] * (1 + len(pieces)),
+        out_specs=[pl.BlockSpec(memory_space=pltpu.VMEM)] * parts,
+        out_shape=[one] * parts,
         scratch_shapes=[pltpu.VMEM((queries, stores), jnp.float32)],
         compiler_params=pltpu.CompilerParams(vmem_limit_bytes=16 * MIB),
         name="score",
-    )(preconditioned, store_rows)
+    )(store_rows, *pieces)
+
+
+def exchange(array, axis, distance):
+    count = lax.axis_size(axis)
+    return lax.ppermute(array, axis, [(i, i ^ distance) for i in range(count)])
+
+
+def pieces_of_all(mine, axis):
+    count = lax.axis_size(axis)
+    far = {0: mine}
+    for d in sorted(range(2, count, 2), key=lambda d: -bin(d).count("1")):
+        far[d] = exchange(mine, axis, d)
+    pieces = []
+    for d in range(0, count, 2):
+        pieces += [far[d], exchange(far[d], axis, 1)]
+    return pieces
 
 
 def on_device(
@@ -269,20 +288,12 @@
         capacity,
         row_count * capacity,
     )
-    gathered = lax.all_gather(feature, "row", axis=0, tiled=True)
-    column_part = precondition(gathered, curvature, placer)
-    preconditioned = lax.all_gather(column_part, "row", axis=0, tiled=True)
-    keep, send = score(preconditioned, store_grads[0], queries, mod_count)
-    distance = 1
-    while True:
-        arrived = lax.ppermute(
-            send, "mod", [(i, i ^ distance) for i in range(mod_count)]
-        )
-        summed = keep + arrived
-        distance *= 2
-        if distance == mod_count:
-            return summed[0]
-        keep, send = summed[0::2], summed[1::2]
+    column_part = precondition(pieces_of_all(feature, "row"), curvature, placer)
+    shares = score(pieces_of_all(column_part, "row"), store_grads[0], queries, mod_count)
+    total = shares[0]
+    for d in reversed(range(1, mod_count)):
+        total = total + exchange(shares[d], "mod", d)
+    return total
 
 
 def solution(mesh):

time: 42.2 us -> 38.2 us (0.905)
  blocking collectives: 20.6 us -> 0 us
  starting transfers between devices: 4.29 us -> 12.6 us
  waiting for transfers between devices: 4.67 us -> 12.9 us
    all_gather x2 -> x0, blocking collectives: 20.6 us -> none  [the longest x1 11.3 us: on_device(): gathered = lax.all_gather(feature, 'row', axis=0, tiled=True)]
    ppermute x2 -> x17, starting transfers between devices: 4.29 us -> 12.6 us  [exchange(): return lax.ppermute(array, axis, [(i, i ^ distance) for i in range(count)])]
    ppermute x2 -> x17, waiting for transfers between devices: 4.67 us -> 12.9 us  [exchange(): return lax.ppermute(array, axis, [(i, i ^ distance) for i in range(count)])]
    squeeze x1 -> x0, other arithmetic: 0.61 us -> none  [on_device(): return summed[0]]
    add x1, other arithmetic: 0.01 us -> 0.62 us  [on_device(): total = total + exchange(shares[d], 'mod', d)]
  transfers between devices with their start and end apart: 2 -> 17, of which waited for: 2 -> 13; matrix products, arithmetic and copies ran while one was open for 0% -> 0% of each run, Pallas kernels for 0% -> 0%
where the time goes in v4:
time: 38.2 us; the launch traced here: 38.1 us
  waiting for transfers between devices  12.9 us (34%)
  starting transfers between devices  12.6 us (33%)
  Pallas kernels  11.9 us (31%)
  other arithmetic  0.62 us (2%)
    ppermute x17, waiting for transfers between devices, exchange(): return lax.ppermute(array, axis, [(i, i ^ distance) for i in range(count)])  12.9 us
    ppermute x17, starting transfers between devices, exchange(): return lax.ppermute(array, axis, [(i, i ^ distance) for i in range(count)])  12.6 us
    pallas_call x1, Pallas kernels, featurize(): pl.pallas_call(featurize_kernel, in_specs=[pl.BlockSpec(memory_space=pl.A...  8.42 us
    pallas_call x1, Pallas kernels, score(): pl.pallas_call(functools.partial(score_kernel, parts), in_specs=[pl.Block...  1.95 us
    pallas_call x1, Pallas kernels, precondition(): pl.pallas_call(precondition_kernel, in_specs=[pl.BlockSpec(memory_space=p...  1.5 us
  transfers between devices with their start and end apart: 17, of which 13 were waited for; matrix products, arithmetic and copies ran while one was open for 0% of the time, Pallas kernels for 0%

profile of v4, /device:TPU:0, one launch (start us, length us, event | category | flops | bytes accessed | tf_op | source)
XLA Modules:
  0.0 38.1 jit_solution(17118072411015809130)
XLA Ops:
  0.0 8.4 %featurize.1 = (bf16[8,4096]{1,0:T(8,128)(2,1)S(1)}, f32[32,64]{1,0:T(8,128)S(1)}, bf16[512,4096]{1,0:T(8,128)(2,1)S(1)}) custom-call(s32[32]{0:T(128)} %lengths_hbm.1, s32[32]{0:T(128)} %owners_hbm.1, bf16[512,4096]{1,0:T(8,128)(2,1)} %bitcast.11, bf16[1024,4096]{1,0:T(8,128)(2,1)} %bitcast.9, bf16[1024,4096]{1,0:T(8,128)(2,1)} %bitcast.10, ...), custom_call_target="tpu_custom_call" | custom-call | tf_op jit(solution)/shard_map/featurize/pallas_call | solution.py:165
  8.4 4.0 %collective-permute-start.5 = (bf16[8,4096]{1,0:T(8,128)(2,1)S(1)}, bf16[8,4096]{1,0:T(8,128)(2,1)S(1)}, u32[]{:S(2)}, u32[]{:S(2)}) collective-permute-start(bf16[8,4096]{1,0:T(8,128)(2,1)S(1)} %get-tuple-element.14.rest_0_), channel_id=1, source_target_pairs={{0,6},{1,7},{2,4},{3,5},{4,2},{5,3},{6,0},{7,1},{8,14},{9,15},{10,... | collective-permute-start | bytes 196616 | tf_op jit(solution)/shard_map/ppermute | solution.py:252
  12.4 0.5 %collective-permute-start.3 = (bf16[8,4096]{1,0:T(8,128)(2,1)S(1)}, bf16[8,4096]{1,0:T(8,128)(2,1)S(1)}, u32[]{:S(2)}, u32[]{:S(2)}) collective-permute-start(bf16[8,4096]{1,0:T(8,128)(2,1)S(1)} %get-tuple-element.14.rest_0_), channel_id=1, source_target_pairs={{0,4},{1,5},{2,6},{3,7},{4,0},{5,1},{6,2},{7,3},{8,12},{9,13},{10,... | collective-permute-start | bytes 196616 | tf_op jit(solution)/shard_map/ppermute | solution.py:252
  12.9 0.1 collective-permute-start.1
  13.1 1.6 %collective-permute-done.5.rest_6_ = bf16[8,4096]{1,0:T(8,128)(2,1)S(1)} collective-permute-done((bf16[8,4096]{1,0:T(8,128)(2,1)S(1)}, bf16[8,4096]{1,0:T(8,128)(2,1)S(1)}, u32[]{:S(2)}, u32[]{:S(2)}) %collective-permute-start.5) | collective-permute-done | bytes 65568 | tf_op jit(solution)/shard_map/ppermute | solution.py:252
  14.7 2.0 %collective-permute-done.3.rest_4_ = bf16[8,4096]{1,0:T(8,128)(2,1)S(1)} collective-permute-done((bf16[8,4096]{1,0:T(8,128)(2,1)S(1)}, bf16[8,4096]{1,0:T(8,128)(2,1)S(1)}, u32[]{:S(2)}, u32[]{:S(2)}) %collective-permute-start.3) | collective-permute-done | bytes 65568 | tf_op jit(solution)/shard_map/ppermute | solution.py:252
  16.7 0.5 %collective-permute-done.1.rest_2_ = bf16[8,4096]{1,0:T(8,128)(2,1)S(1)} collective-permute-done((bf16[8,4096]{1,0:T(8,128)(2,1)S(1)}, bf16[8,4096]{1,0:T(8,128)(2,1)S(1)}, u32[]{:S(2)}, u32[]{:S(2)}) %collective-permute-start.1) | collective-permute-done | bytes 65568 | tf_op jit(solution)/shard_map/ppermute | solution.py:252
  17.2 0.7 %collective-permute-done.4.rest_5_ = bf16[8,4096]{1,0:T(8,128)(2,1)S(1)} collective-permute-done((bf16[8,4096]{1,0:T(8,128)(2,1)S(1)}, bf16[8,4096]{1,0:T(8,128)(2,1)S(1)}, u32[]{:S(2)}, u32[]{:S(2)}) %collective-permute-start.4) | collective-permute-done | bytes 65568 | tf_op jit(solution)/shard_map/ppermute | solution.py:252
  17.9 0.5 %collective-permute-done.2.rest_3_ = bf16[8,4096]{1,0:T(8,128)(2,1)S(1)} collective-permute-done((bf16[8,4096]{1,0:T(8,128)(2,1)S(1)}, bf16[8,4096]{1,0:T(8,128)(2,1)S(1)}, u32[]{:S(2)}, u32[]{:S(2)}) %collective-permute-start.2) | collective-permute-done | bytes 65568 | tf_op jit(solution)/shard_map/ppermute | solution.py:252
  18.4 1.5 %precondition.1.rest_0_ = bf16[32,512]{1,0:T(8,128)(2,1)S(1)} custom-call(bf16[512,4096]{1,0:T(8,128)(2,1)S(1)} %get-tuple-element.12.curvature_ref, f32[32,64]{1,0:T(8,128)S(1)} %get-tuple-element.13.placer_ref, bf16[8,4096]{1,0:T(8,128)(2,1)S(1)} %get-tuple-element.14.rest_0_, bf16[8,4096]{1,0:T(8,128)(2,1)S(1)} %collective-permute-done.rest_1_, ...), custom_call_target="tpu_custom_call" | custom-call | tf_op jit(solution)/shard_map/precondition/pallas_call | solution.py:207
  19.9 1.5 %collective-permute-start.12 = (bf16[32,512]{1,0:T(8,128)(2,1)S(1)}, bf16[32,512]{1,0:T(8,128)(2,1)S(1)}, u32[]{:S(2)}, u32[]{:S(2)}) collective-permute-start(bf16[32,512]{1,0:T(8,128)(2,1)S(1)} %precondition.1.rest_0_), channel_id=1, source_target_pairs={{0,6},{1,7},{2,4},{3,5},{4,2},{5,3},{6,0},{7,1},{8,14},{9,15},{10,... | collective-permute-start | bytes 98312 | tf_op jit(solution)/shard_map/ppermute | solution.py:252
  21.4 0.6 %collective-permute-start.10 = (bf16[32,512]{1,0:T(8,128)(2,1)S(1)}, bf16[32,512]{1,0:T(8,128)(2,1)S(1)}, u32[]{:S(2)}, u32[]{:S(2)}) collective-permute-start(bf16[32,512]{1,0:T(8,128)(2,1)S(1)} %precondition.1.rest_0_), channel_id=1, source_target_pairs={{0,4},{1,5},{2,6},{3,7},{4,0},{5,1},{6,2},{7,3},{8,12},{9,13},{10,... | collective-permute-start | bytes 98312 | tf_op jit(solution)/shard_map/ppermute | solution.py:252
  22.0 1.4 %collective-permute-start.8 = (bf16[32,512]{1,0:T(8,128)(2,1)S(1)}, bf16[32,512]{1,0:T(8,128)(2,1)S(1)}, u32[]{:S(2)}, u32[]{:S(2)}) collective-permute-start(bf16[32,512]{1,0:T(8,128)(2,1)S(1)} %precondition.1.rest_0_), channel_id=1, source_target_pairs={{0,2},{1,3},{2,0},{3,1},{4,6},{5,7},{6,4},{7,5},{8,10},{9,11},{10,... | collective-permute-start | bytes 98312 | tf_op jit(solution)/shard_map/ppermute | solution.py:252
  23.4 1.3 %collective-permute-done.12.rest_6_ = bf16[32,512]{1,0:T(8,128)(2,1)S(1)} collective-permute-done((bf16[32,512]{1,0:T(8,128)(2,1)S(1)}, bf16[32,512]{1,0:T(8,128)(2,1)S(1)}, u32[]{:S(2)}, u32[]{:S(2)}) %collective-permute-start.12) | collective-permute-done | bytes 32800 | tf_op jit(solution)/shard_map/ppermute | solution.py:252
  24.8 0.6 %collective-permute-done.10.rest_4_ = bf16[32,512]{1,0:T(8,128)(2,1)S(1)} collective-permute-done((bf16[32,512]{1,0:T(8,128)(2,1)S(1)}, bf16[32,512]{1,0:T(8,128)(2,1)S(1)}, u32[]{:S(2)}, u32[]{:S(2)}) %collective-permute-start.10) | collective-permute-done | bytes 32800 | tf_op jit(solution)/shard_map/ppermute | solution.py:252
  25.3 0.6 %collective-permute-done.8.rest_2_ = bf16[32,512]{1,0:T(8,128)(2,1)S(1)} collective-permute-done((bf16[32,512]{1,0:T(8,128)(2,1)S(1)}, bf16[32,512]{1,0:T(8,128)(2,1)S(1)}, u32[]{:S(2)}, u32[]{:S(2)}) %collective-permute-start.8) | collective-permute-done | bytes 32800 | tf_op jit(solution)/shard_map/ppermute | solution.py:252
  26.0 0.6 %collective-permute-done.11.rest_5_ = bf16[32,512]{1,0:T(8,128)(2,1)S(1)} collective-permute-done((bf16[32,512]{1,0:T(8,128)(2,1)S(1)}, bf16[32,512]{1,0:T(8,128)(2,1)S(1)}, u32[]{:S(2)}, u32[]{:S(2)}) %collective-permute-start.11) | collective-permute-done | bytes 32800 | tf_op jit(solution)/shard_map/ppermute | solution.py:252
  26.5 0.6 %collective-permute-done.9.rest_3_ = bf16[32,512]{1,0:T(8,128)(2,1)S(1)} collective-permute-done((bf16[32,512]{1,0:T(8,128)(2,1)S(1)}, bf16[32,512]{1,0:T(8,128)(2,1)S(1)}, u32[]{:S(2)}, u32[]{:S(2)}) %collective-permute-start.9) | collective-permute-done | bytes 32800 | tf_op jit(solution)/shard_map/ppermute | solution.py:252
  27.1 1.9 %score.1 = (f32[8,768]{1,0:T(8,128)S(1)}, f32[8,768]{1,0:T(8,128)S(1)}, f32[8,768]{1,0:T(8,128)S(1)}, f32[8,768]{1,0:T(8,128)S(1)}) custom-call(bf16[768,4096]{1,0:T(8,128)(2,1)S(1)} %bitcast.8, bf16[32,512]{1,0:T(8,128)(2,1)S(1)} %precondition.1.rest_0_, bf16[32,512]{1,0:T(8,128)(2,1)S(1)} %collective-permute-done.7.rest_1_, ...), custom_call_target="tpu_custom_call" | custom-call | tf_op jit(solution)/shard_map/score/pallas_call | solution.py:239
  29.1 3.7 %collective-permute-start.14 = (f32[8,768]{1,0:T(8,128)S(1)}, f32[8,768]{1,0:T(8,128)S(1)}, u32[]{:S(2)}, u32[]{:S(2)}) collective-permute-start(f32[8,768]{1,0:T(8,128)S(1)} %get-tuple-element.16), channel_id=1, source_target_pairs={{0,24},{8,16},{16,8},{24,0},{1,25},{9,17},{17,9},{25,1},{2,26},{10... | collective-permute-start | bytes 73736 | tf_op jit(solution)/shard_map/ppermute | solution.py:252
  32.7 0.8 %collective-permute-start.16 = (f32[8,768]{1,0:T(8,128)S(1)}, f32[8,768]{1,0:T(8,128)S(1)}, u32[]{:S(2)}, u32[]{:S(2)}) collective-permute-start(f32[8,768]{1,0:T(8,128)S(1)} %get-tuple-element.18), channel_id=1, source_target_pairs={{0,8},{8,0},{16,24},{24,16},{1,9},{9,1},{17,25},{25,17},{2,10},{10... | collective-permute-start | bytes 73736 | tf_op jit(solution)/shard_map/ppermute | solution.py:252
  33.5 1.2 %collective-permute-done.14 = f32[8,768]{1,0:T(8,128)S(1)} collective-permute-done((f32[8,768]{1,0:T(8,128)S(1)}, f32[8,768]{1,0:T(8,128)S(1)}, u32[]{:S(2)}, u32[]{:S(2)}) %collective-permute-start.14) | collective-permute-done | bytes 24608 | tf_op jit(solution)/shard_map/ppermute | solution.py:252
  34.8 2.7 %collective-permute-done.15 = f32[8,768]{1,0:T(8,128)S(1)} collective-permute-done((f32[8,768]{1,0:T(8,128)S(1)}, f32[8,768]{1,0:T(8,128)S(1)}, u32[]{:S(2)}, u32[]{:S(2)}) %collective-permute-start.15) | collective-permute-done | bytes 24608 | tf_op jit(solution)/shard_map/ppermute | solution.py:252
  37.5 0.6 %add_add_fusion = f32[8,768]{1,0:T(8,128)} fusion(f32[8,768]{1,0:T(8,128)S(1)} %collective-permute-done.16, f32[8,768]{1,0:T(8,128)S(1)} %collective-permute-done.15, f32[8,768]{1,0:T(8,128)S(1)} %get-tuple-element.15, f32[8,768]{1,0:T(8,128)S(1)} %collective-permute-done.14), kind=kLoop, calls=%fused_computation | loop fusion | flops 18432 | bytes 122880 | tf_op jit(solution)/shard_map/add | solution.py:295
  (19 shorter events, 0.1 us)
Async XLA Ops:
  0.0 27.1 %slice-start = ((s8[6291456]{0:T(1024)(128)(4,1)}), s8[4194304]{0:T(1024)(128)(4,1)S(1)}, s32[]{:S(2)}) async-start(s8[6291456]{0:T(1024)(128)(4,1)} %bitcast.6), calls=%async_computation | async-start | bytes 8388608
  0.0 27.1 %slice-start.1 = ((s8[6291456]{0:T(1024)(128)(4,1)}), s8[2097152]{0:T(1024)(128)(4,1)S(1)}, s32[]{:S(2)}) async-start(s8[6291456]{0:T(1024)(128)(4,1)} %bitcast.6), calls=%async_computation.1 | async-start | bytes 4194304
  8.4 6.2 %collective-permute-start.5 = (bf16[8,4096]{1,0:T(8,128)(2,1)S(1)}, bf16[8,4096]{1,0:T(8,128)(2,1)S(1)}, u32[]{:S(2)}, u32[]{:S(2)}) collective-permute-start(bf16[8,4096]{1,0:T(8,128)(2,1)S(1)} %get-tuple-element.14.rest_0_), channel_id=1, source_target_pairs={{0,6},{1,7},{2,4},{3,5},{4,2},{5,3},{6,0},{7,1},{8,14},{9,15},{10,... | collective-permute-start | bytes 196616 | tf_op jit(solution)/shard_map/ppermute | solution.py:252
  12.4 4.3 %collective-permute-start.3 = (bf16[8,4096]{1,0:T(8,128)(2,1)S(1)}, bf16[8,4096]{1,0:T(8,128)(2,1)S(1)}, u32[]{:S(2)}, u32[]{:S(2)}) collective-permute-start(bf16[8,4096]{1,0:T(8,128)(2,1)S(1)} %get-tuple-element.14.rest_0_), channel_id=1, source_target_pairs={{0,4},{1,5},{2,6},{3,7},{4,0},{5,1},{6,2},{7,3},{8,12},{9,13},{10,... | collective-permute-start | bytes 196616 | tf_op jit(solution)/shard_map/ppermute | solution.py:252
  12.9 4.3 %collective-permute-start.1 = (bf16[8,4096]{1,0:T(8,128)(2,1)S(1)}, bf16[8,4096]{1,0:T(8,128)(2,1)S(1)}, u32[]{:S(2)}, u32[]{:S(2)}) collective-permute-start(bf16[8,4096]{1,0:T(8,128)(2,1)S(1)} %get-tuple-element.14.rest_0_), channel_id=1, source_target_pairs={{0,2},{1,3},{2,0},{3,1},{4,6},{5,7},{6,4},{7,5},{8,10},{9,11},{10,... | collective-permute-start | bytes 196616 | tf_op jit(solution)/shard_map/ppermute | solution.py:252
  13.0 4.1 %collective-permute-start = (bf16[8,4096]{1,0:T(8,128)(2,1)S(1)}, bf16[8,4096]{1,0:T(8,128)(2,1)S(1)}, u32[]{:S(2)}, u32[]{:S(2)}) collective-permute-start(bf16[8,4096]{1,0:T(8,128)(2,1)S(1)} %get-tuple-element.14.rest_0_), channel_id=1, source_target_pairs={{0,1},{1,0},{2,3},{3,2},{4,5},{5,4},{6,7},{7,6},{8,9},{9,8},{10,11... | collective-permute-start | bytes 196616 | tf_op jit(solution)/shard_map/ppermute | solution.py:252
  14.7 2.5 %collective-permute-start.6 = (bf16[8,4096]{1,0:T(8,128)(2,1)S(1)}, bf16[8,4096]{1,0:T(8,128)(2,1)S(1)}, u32[]{:S(2)}, u32[]{:S(2)}) collective-permute-start(bf16[8,4096]{1,0:T(8,128)(2,1)S(1)} %collective-permute-done.5.rest_6_), channel_id=1, source_target_pairs={{0,1},{1,0},{2,3},{3,2},{4,5},{5,4},{6,7},{7,6},{8,9},{9,8},{10,11... | collective-permute-start | bytes 196616 | tf_op jit(solution)/shard_map/ppermute | solution.py:252
  16.7 1.3 %collective-permute-start.4 = (bf16[8,4096]{1,0:T(8,128)(2,1)S(1)}, bf16[8,4096]{1,0:T(8,128)(2,1)S(1)}, u32[]{:S(2)}, u32[]{:S(2)}) collective-permute-start(bf16[8,4096]{1,0:T(8,128)(2,1)S(1)} %collective-permute-done.3.rest_4_), channel_id=1, source_target_pairs={{0,1},{1,0},{2,3},{3,2},{4,5},{5,4},{6,7},{7,6},{8,9},{9,8},{10,11... | collective-permute-start | bytes 196616 | tf_op jit(solution)/shard_map/ppermute | solution.py:252
  17.2 1.3 %collective-permute-start.2 = (bf16[8,4096]{1,0:T(8,128)(2,1)S(1)}, bf16[8,4096]{1,0:T(8,128)(2,1)S(1)}, u32[]{:S(2)}, u32[]{:S(2)}) collective-permute-start(bf16[8,4096]{1,0:T(8,128)(2,1)S(1)} %collective-permute-done.1.rest_2_), channel_id=1, source_target_pairs={{0,1},{1,0},{2,3},{3,2},{4,5},{5,4},{6,7},{7,6},{8,9},{9,8},{10,11... | collective-permute-start | bytes 196616 | tf_op jit(solution)/shard_map/ppermute | solution.py:252
  19.9 4.8 %collective-permute-start.12 = (bf16[32,512]{1,0:T(8,128)(2,1)S(1)}, bf16[32,512]{1,0:T(8,128)(2,1)S(1)}, u32[]{:S(2)}, u32[]{:S(2)}) collective-permute-start(bf16[32,512]{1,0:T(8,128)(2,1)S(1)} %precondition.1.rest_0_), channel_id=1, source_target_pairs={{0,6},{1,7},{2,4},{3,5},{4,2},{5,3},{6,0},{7,1},{8,14},{9,15},{10,... | collective-permute-start | bytes 98312 | tf_op jit(solution)/shard_map/ppermute | solution.py:252
  21.4 3.9 %collective-permute-start.10 = (bf16[32,512]{1,0:T(8,128)(2,1)S(1)}, bf16[32,512]{1,0:T(8,128)(2,1)S(1)}, u32[]{:S(2)}, u32[]{:S(2)}) collective-permute-start(bf16[32,512]{1,0:T(8,128)(2,1)S(1)} %precondition.1.rest_0_), channel_id=1, source_target_pairs={{0,4},{1,5},{2,6},{3,7},{4,0},{5,1},{6,2},{7,3},{8,12},{9,13},{10,... | collective-permute-start | bytes 98312 | tf_op jit(solution)/shard_map/ppermute | solution.py:252
  22.0 3.9 %collective-permute-start.8 = (bf16[32,512]{1,0:T(8,128)(2,1)S(1)}, bf16[32,512]{1,0:T(8,128)(2,1)S(1)}, u32[]{:S(2)}, u32[]{:S(2)}) collective-permute-start(bf16[32,512]{1,0:T(8,128)(2,1)S(1)} %precondition.1.rest_0_), channel_id=1, source_target_pairs={{0,2},{1,3},{2,0},{3,1},{4,6},{5,7},{6,4},{7,5},{8,10},{9,11},{10,... | collective-permute-start | bytes 98312 | tf_op jit(solution)/shard_map/ppermute | solution.py:252
  23.4 2.5 %collective-permute-start.7 = (bf16[32,512]{1,0:T(8,128)(2,1)S(1)}, bf16[32,512]{1,0:T(8,128)(2,1)S(1)}, u32[]{:S(2)}, u32[]{:S(2)}) collective-permute-start(bf16[32,512]{1,0:T(8,128)(2,1)S(1)} %precondition.1.rest_0_), channel_id=1, source_target_pairs={{0,1},{1,0},{2,3},{3,2},{4,5},{5,4},{6,7},{7,6},{8,9},{9,8},{10,11... | collective-permute-start | bytes 98312 | tf_op jit(solution)/shard_map/ppermute | solution.py:252
  24.8 1.2 %collective-permute-start.13 = (bf16[32,512]{1,0:T(8,128)(2,1)S(1)}, bf16[32,512]{1,0:T(8,128)(2,1)S(1)}, u32[]{:S(2)}, u32[]{:S(2)}) collective-permute-start(bf16[32,512]{1,0:T(8,128)(2,1)S(1)} %collective-permute-done.12.rest_6_), channel_id=1, source_target_pairs={{0,1},{1,0},{2,3},{3,2},{4,5},{5,4},{6,7},{7,6},{8,9},{9,8},{10,11... | collective-permute-start | bytes 98312 | tf_op jit(solution)/shard_map/ppermute | solution.py:252
  25.3 1.2 %collective-permute-start.11 = (bf16[32,512]{1,0:T(8,128)(2,1)S(1)}, bf16[32,512]{1,0:T(8,128)(2,1)S(1)}, u32[]{:S(2)}, u32[]{:S(2)}) collective-permute-start(bf16[32,512]{1,0:T(8,128)(2,1)S(1)} %collective-permute-done.10.rest_4_), channel_id=1, source_target_pairs={{0,1},{1,0},{2,3},{3,2},{4,5},{5,4},{6,7},{7,6},{8,9},{9,8},{10,11... | collective-permute-start | bytes 98312 | tf_op jit(solution)/shard_map/ppermute | solution.py:252
  25.9 1.2 %collective-permute-start.9 = (bf16[32,512]{1,0:T(8,128)(2,1)S(1)}, bf16[32,512]{1,0:T(8,128)(2,1)S(1)}, u32[]{:S(2)}, u32[]{:S(2)}) collective-permute-start(bf16[32,512]{1,0:T(8,128)(2,1)S(1)} %collective-permute-done.8.rest_2_), channel_id=1, source_target_pairs={{0,1},{1,0},{2,3},{3,2},{4,5},{5,4},{6,7},{7,6},{8,9},{9,8},{10,11... | collective-permute-start | bytes 98312 | tf_op jit(solution)/shard_map/ppermute | solution.py:252
  29.1 5.7 %collective-permute-start.14 = (f32[8,768]{1,0:T(8,128)S(1)}, f32[8,768]{1,0:T(8,128)S(1)}, u32[]{:S(2)}, u32[]{:S(2)}) collective-permute-start(f32[8,768]{1,0:T(8,128)S(1)} %get-tuple-element.16), channel_id=1, source_target_pairs={{0,24},{8,16},{16,8},{24,0},{1,25},{9,17},{17,9},{25,1},{2,26},{10... | collective-permute-start | bytes 73736 | tf_op jit(solution)/shard_map/ppermute | solution.py:252
  32.7 4.7 %collective-permute-start.15 = (f32[8,768]{1,0:T(8,128)S(1)}, f32[8,768]{1,0:T(8,128)S(1)}, u32[]{:S(2)}, u32[]{:S(2)}) collective-permute-start(f32[8,768]{1,0:T(8,128)S(1)} %get-tuple-element.17), channel_id=1, source_target_pairs={{0,16},{8,24},{16,0},{24,8},{1,17},{9,25},{17,1},{25,9},{2,18},{10... | collective-permute-start | bytes 73736 | tf_op jit(solution)/shard_map/ppermute | solution.py:252
  32.7 4.7 %collective-permute-start.16 = (f32[8,768]{1,0:T(8,128)S(1)}, f32[8,768]{1,0:T(8,128)S(1)}, u32[]{:S(2)}, u32[]{:S(2)}) collective-permute-start(f32[8,768]{1,0:T(8,128)S(1)} %get-tuple-element.18), channel_id=1, source_target_pairs={{0,8},{8,0},{16,24},{24,16},{1,9},{9,1},{17,25},{25,17},{2,10},{10... | collective-permute-start | bytes 73736 | tf_op jit(solution)/shard_map/ppermute | solution.py:252

commit v5 on v4

--- a/solution.py
+++ b/solution.py
@@ -14,6 +14,17 @@
     return lax.dot_general(
         left, right, (((1,), (1,)), ((), ())), preferred_element_type=jnp.float32
     )
+
+
+def ring_member(place):
+    return place ^ (place >> 1)
+
+
+def ring_place(member):
+    place = member
+    for shift in (1, 2, 4):
+        place = place ^ (place >> shift)
+    return place
 
 
 def split_two(values):
@@ -215,41 +226,66 @@
     )(curvature_rows, placer, *pieces)
 
 
-def score_kernel(parts, store_ref, *rest):
+def partial_scores(places, store_ref, piece_refs):
+    queries, depth = piece_refs[0].shape
+    column = lax.axis_index("row")
+    scores = jnp.zeros((store_ref.shape[0], queries), jnp.float32)
+    for place, piece_ref in zip(places, piece_refs):
+        first = pl.multiple_of((column ^ place) * depth, depth)
+        scores += contract_last(store_ref[:, pl.ds(first, depth)], piece_ref[...])
+    return scores
+
+
+def early_score_kernel(places, store_ref, *rest):
+    rest[-1][...] = partial_scores(places, store_ref, rest[:-1])
+
+
+def score_kernel(places, parts, early_ref, store_ref, *rest):
     piece_refs = rest[: -parts - 1]
     share_refs, total = rest[-parts - 1 : -1], rest[-1]
     share = share_refs[0].shape[0]
-    queries, stores = total.shape
-    depth = piece_refs[0].shape[1]
-    column = lax.axis_index("row")
-    scores = jnp.zeros((queries, stores), jnp.float32)
-    for place, piece_ref in enumerate(piece_refs):
-        first = pl.multiple_of((column ^ place) * depth, depth)
-        scores += contract_last(piece_ref[...], store_ref[:, pl.ds(first, depth)])
-    total[...] = scores
+    total[...] = (early_ref[...] + partial_scores(places, store_ref, piece_refs)).T
     me = lax.axis_index("mod")
     for place in range(parts):
-        row = pl.multiple_of((me ^ place) * share, share)
+        member = ring_member(lax.rem(ring_place(me) + place, parts))
+        row = pl.multiple_of(member * share, share)
         share_refs[place][...] = total[pl.ds(row, share), :]
 
 
-def score(pieces, store_rows, queries, parts):
+def score(pieces, store_rows, queries, parts, early_places):
     stores = store_rows.shape[0]
+    late_places = [d for d in range(len(pieces)) if d not in early_places]
+    early = pl.pallas_call(
+        functools.partial(early_score_kernel, early_places),
+        in_specs=[pl.BlockSpec(memory_space=pltpu.VMEM)] * (1 + len(early_places)),
+        out_specs=pl.BlockSpec(memory_space=pltpu.VMEM),
+        out_shape=pltpu.VMEM((stores, queries), jnp.float32),
+        compiler_params=pltpu.CompilerParams(vmem_limit_bytes=16 * MIB),
+        name="early_score",
+    )(store_rows, *[pieces[d] for d in early_places])
     one = pltpu.VMEM((queries // parts, stores), jnp.float32)
     return pl.pallas_call(
-        functools.partial(score_kernel, parts),
-        in_specs=[pl.BlockSpec(memory_space=pltpu.VMEM)] * (1 + len(pieces)),
+        functools.partial(score_kernel, late_places, parts),
+        in_specs=[pl.BlockSpec(memory_space=pltpu.VMEM)] * (2 + len(late_places)),
         out_specs=[pl.BlockSpec(memory_space=pltpu.VMEM)] * parts,
         out_shape=[one] * parts,
         scratch_shapes=[pltpu.VMEM((queries, stores), jnp.float32)],
         compiler_params=pltpu.CompilerParams(vmem_limit_bytes=16 * MIB),
         name="score",
-    )(store_rows, *pieces)
+    )(early, store_rows, *[pieces[d] for d in late_places])
 
 
 def exchange(array, axis, distance):
     count = lax.axis_size(axis)
     return lax.ppermute(array, axis, [(i, i ^ distance) for i in range(count)])
+
+
+def send_on(array, axis, places):
+    count = lax.axis_size(axis)
+    order = [ring_member(place) for place in range(count)]
+    return lax.ppermute(
+        array, axis, [(order[i], order[(i + places) % count]) for i in range(count)]
+    )
 
 
 def pieces_of_all(mine, axis):
@@ -289,10 +325,10 @@
         row_count * capacity,
     )
     column_part = precondition(pieces_of_all(feature, "row"), curvature, placer)
-    shares = score(pieces_of_all(column_part, "row"), store_grads[0], queries, mod_count)
+    shares = score(pieces_of_all(column_part, "row"), store_grads[0], queries, mod_count, [0, 1])
     total = shares[0]
-    for d in reversed(range(1, mod_count)):
-        total = total + exchange(shares[d], "mod", d)
+    for places in range(1, mod_count):
+        total = total + send_on(shares[places], "mod", places)
     return total
 
 

time: 38.2 us -> 37.2 us (0.974)
  waiting for transfers between devices: 12.9 us -> 10.6 us
  starting transfers between devices: 12.6 us -> 13.9 us
    ppermute x0 -> x3, starting transfers between devices: none -> 5.7 us  [send_on(): lax.ppermute(array, axis, [(order[i], order[(i + places) % count]) for i...]
    ppermute x17 -> x14, waiting for transfers between devices: 12.9 us -> 8.37 us  [exchange(): return lax.ppermute(array, axis, [(i, i ^ distance) for i in range(count)])]
    ppermute x17 -> x14, starting transfers between devices: 12.6 us -> 8.17 us  [exchange(): return lax.ppermute(array, axis, [(i, i ^ distance) for i in range(count)])]
    ppermute x0 -> x3, waiting for transfers between devices: none -> 2.22 us  [send_on(): lax.ppermute(array, axis, [(order[i], order[(i + places) % count]) for i...]
    pallas_call x1 -> x2, Pallas kernels: 1.95 us -> 1.98 us  [the longest x1 1.42 us: score(): pl.pallas_call(functools.partial(score_kernel, late_places, parts), in_sp...]
  transfers between devices with their start and end apart: 17 -> 17, of which waited for: 13 -> 12; matrix products, arithmetic and copies ran while one was open for 0% -> 0% of each run, Pallas kernels for 0% -> 1%
where the time goes in v5:
time: 37.2 us; the launch traced here: 37.1 us
  starting transfers between devices  13.9 us (37%)
  Pallas kernels  11.9 us (32%)
  waiting for transfers between devices  10.6 us (28%)
  other arithmetic  0.62 us (2%)
    pallas_call x1, Pallas kernels, featurize(): pl.pallas_call(featurize_kernel, in_specs=[pl.BlockSpec(memory_space=pl.A...  8.42 us
    ppermute x14, waiting for transfers between devices, exchange(): return lax.ppermute(array, axis, [(i, i ^ distance) for i in range(count)])  8.37 us
    ppermute x14, starting transfers between devices, exchange(): return lax.ppermute(array, axis, [(i, i ^ distance) for i in range(count)])  8.17 us
    ppermute x3, starting transfers between devices, send_on(): lax.ppermute(array, axis, [(order[i], order[(i + places) % count]) for i...  5.7 us
    ppermute x3, waiting for transfers between devices, send_on(): lax.ppermute(array, axis, [(order[i], order[(i + places) % count]) for i...  2.22 us
    pallas_call x1, Pallas kernels, precondition(): pl.pallas_call(precondition_kernel, in_specs=[pl.BlockSpec(memory_space=p...  1.5 us
    pallas_call x1, Pallas kernels, score(): pl.pallas_call(functools.partial(score_kernel, late_places, parts), in_sp...  1.42 us
  transfers between devices with their start and end apart: 17, of which 12 were waited for; matrix products, arithmetic and copies ran while one was open for 0% of the time, Pallas kernels for 1%

profile of v5, /device:TPU:0, one launch (start us, length us, event | category | flops | bytes accessed | tf_op | source)
XLA Modules:
  0.0 37.1 jit_solution(5756077333120224198)
XLA Ops:
  0.0 8.4 %featurize.1 = (bf16[8,4096]{1,0:T(8,128)(2,1)S(1)}, f32[32,64]{1,0:T(8,128)S(1)}, bf16[512,4096]{1,0:T(8,128)(2,1)S(1)}) custom-call(s32[32]{0:T(128)} %lengths_hbm.1, s32[32]{0:T(128)} %owners_hbm.1, bf16[512,4096]{1,0:T(8,128)(2,1)} %bitcast.12, bf16[1024,4096]{1,0:T(8,128)(2,1)} %bitcast.10, bf16[1024,4096]{1,0:T(8,128)(2,1)} %bitcast.11, ...), custom_call_target="tpu_custom_call" | custom-call | tf_op jit(solution)/shard_map/featurize/pallas_call | solution.py:176
  8.4 4.0 %collective-permute-start.5 = (bf16[8,4096]{1,0:T(8,128)(2,1)S(1)}, bf16[8,4096]{1,0:T(8,128)(2,1)S(1)}, u32[]{:S(2)}, u32[]{:S(2)}) collective-permute-start(bf16[8,4096]{1,0:T(8,128)(2,1)S(1)} %get-tuple-element.14.rest_0_), channel_id=1, source_target_pairs={{0,6},{1,7},{2,4},{3,5},{4,2},{5,3},{6,0},{7,1},{8,14},{9,15},{10,... | collective-permute-start | bytes 196616 | tf_op jit(solution)/shard_map/ppermute | solution.py:280
  12.4 0.5 %collective-permute-start.3 = (bf16[8,4096]{1,0:T(8,128)(2,1)S(1)}, bf16[8,4096]{1,0:T(8,128)(2,1)S(1)}, u32[]{:S(2)}, u32[]{:S(2)}) collective-permute-start(bf16[8,4096]{1,0:T(8,128)(2,1)S(1)} %get-tuple-element.14.rest_0_), channel_id=1, source_target_pairs={{0,4},{1,5},{2,6},{3,7},{4,0},{5,1},{6,2},{7,3},{8,12},{9,13},{10,... | collective-permute-start | bytes 196616 | tf_op jit(solution)/shard_map/ppermute | solution.py:280
  13.1 1.6 %collective-permute-done.5.rest_6_ = bf16[8,4096]{1,0:T(8,128)(2,1)S(1)} collective-permute-done((bf16[8,4096]{1,0:T(8,128)(2,1)S(1)}, bf16[8,4096]{1,0:T(8,128)(2,1)S(1)}, u32[]{:S(2)}, u32[]{:S(2)}) %collective-permute-start.5) | collective-permute-done | bytes 65568 | tf_op jit(solution)/shard_map/ppermute | solution.py:280
  14.7 2.0 %collective-permute-done.3.rest_4_ = bf16[8,4096]{1,0:T(8,128)(2,1)S(1)} collective-permute-done((bf16[8,4096]{1,0:T(8,128)(2,1)S(1)}, bf16[8,4096]{1,0:T(8,128)(2,1)S(1)}, u32[]{:S(2)}, u32[]{:S(2)}) %collective-permute-start.3) | collective-permute-done | bytes 65568 | tf_op jit(solution)/shard_map/ppermute | solution.py:280
  16.7 0.5 %collective-permute-done.1.rest_2_ = bf16[8,4096]{1,0:T(8,128)(2,1)S(1)} collective-permute-done((bf16[8,4096]{1,0:T(8,128)(2,1)S(1)}, bf16[8,4096]{1,0:T(8,128)(2,1)S(1)}, u32[]{:S(2)}, u32[]{:S(2)}) %collective-permute-start.1) | collective-permute-done | bytes 65568 | tf_op jit(solution)/shard_map/ppermute | solution.py:280
  17.2 0.7 %collective-permute-done.4.rest_5_ = bf16[8,4096]{1,0:T(8,128)(2,1)S(1)} collective-permute-done((bf16[8,4096]{1,0:T(8,128)(2,1)S(1)}, bf16[8,4096]{1,0:T(8,128)(2,1)S(1)}, u32[]{:S(2)}, u32[]{:S(2)}) %collective-permute-start.4) | collective-permute-done | bytes 65568 | tf_op jit(solution)/shard_map/ppermute | solution.py:280
  17.9 0.5 %collective-permute-done.2.rest_3_ = bf16[8,4096]{1,0:T(8,128)(2,1)S(1)} collective-permute-done((bf16[8,4096]{1,0:T(8,128)(2,1)S(1)}, bf16[8,4096]{1,0:T(8,128)(2,1)S(1)}, u32[]{:S(2)}, u32[]{:S(2)}) %collective-permute-start.2) | collective-permute-done | bytes 65568 | tf_op jit(solution)/shard_map/ppermute | solution.py:280
  18.4 1.5 %precondition.1.rest_0_ = bf16[32,512]{1,0:T(8,128)(2,1)S(1)} custom-call(bf16[512,4096]{1,0:T(8,128)(2,1)S(1)} %get-tuple-element.12.curvature_ref, f32[32,64]{1,0:T(8,128)S(1)} %get-tuple-element.13.placer_ref, bf16[8,4096]{1,0:T(8,128)(2,1)S(1)} %get-tuple-element.14.rest_0_, bf16[8,4096]{1,0:T(8,128)(2,1)S(1)} %collective-permute-done.rest_1_, ...), custom_call_target="tpu_custom_call" | custom-call | tf_op jit(solution)/shard_map/precondition/pallas_call | solution.py:218
  19.9 1.5 %collective-permute-start.12 = (bf16[32,512]{1,0:T(8,128)(2,1)S(1)}, bf16[32,512]{1,0:T(8,128)(2,1)S(1)}, u32[]{:S(2)}, u32[]{:S(2)}) collective-permute-start(bf16[32,512]{1,0:T(8,128)(2,1)S(1)} %precondition.1.rest_0_), channel_id=1, source_target_pairs={{0,6},{1,7},{2,4},{3,5},{4,2},{5,3},{6,0},{7,1},{8,14},{9,15},{10,... | collective-permute-start | bytes 98312 | tf_op jit(solution)/shard_map/ppermute | solution.py:280
  21.4 0.5 %collective-permute-start.10 = (bf16[32,512]{1,0:T(8,128)(2,1)S(1)}, bf16[32,512]{1,0:T(8,128)(2,1)S(1)}, u32[]{:S(2)}, u32[]{:S(2)}) collective-permute-start(bf16[32,512]{1,0:T(8,128)(2,1)S(1)} %precondition.1.rest_0_), channel_id=1, source_target_pairs={{0,4},{1,5},{2,6},{3,7},{4,0},{5,1},{6,2},{7,3},{8,12},{9,13},{10,... | collective-permute-start | bytes 98312 | tf_op jit(solution)/shard_map/ppermute | solution.py:280
  22.0 1.5 %collective-permute-start.8 = (bf16[32,512]{1,0:T(8,128)(2,1)S(1)}, bf16[32,512]{1,0:T(8,128)(2,1)S(1)}, u32[]{:S(2)}, u32[]{:S(2)}) collective-permute-start(bf16[32,512]{1,0:T(8,128)(2,1)S(1)} %precondition.1.rest_0_), channel_id=1, source_target_pairs={{0,2},{1,3},{2,0},{3,1},{4,6},{5,7},{6,4},{7,5},{8,10},{9,11},{10,... | collective-permute-start | bytes 98312 | tf_op jit(solution)/shard_map/ppermute | solution.py:280
  23.4 1.3 %collective-permute-done.12.rest_4_ = bf16[32,512]{1,0:T(8,128)(2,1)S(1)} collective-permute-done((bf16[32,512]{1,0:T(8,128)(2,1)S(1)}, bf16[32,512]{1,0:T(8,128)(2,1)S(1)}, u32[]{:S(2)}, u32[]{:S(2)}) %collective-permute-start.12) | collective-permute-done | bytes 32800 | tf_op jit(solution)/shard_map/ppermute | solution.py:280
  24.7 0.6 %collective-permute-done.10.rest_2_ = bf16[32,512]{1,0:T(8,128)(2,1)S(1)} collective-permute-done((bf16[32,512]{1,0:T(8,128)(2,1)S(1)}, bf16[32,512]{1,0:T(8,128)(2,1)S(1)}, u32[]{:S(2)}, u32[]{:S(2)}) %collective-permute-start.10) | collective-permute-done | bytes 32800 | tf_op jit(solution)/shard_map/ppermute | solution.py:280
  25.3 0.5 %collective-permute-done.8.rest_0_ = bf16[32,512]{1,0:T(8,128)(2,1)S(1)} collective-permute-done((bf16[32,512]{1,0:T(8,128)(2,1)S(1)}, bf16[32,512]{1,0:T(8,128)(2,1)S(1)}, u32[]{:S(2)}, u32[]{:S(2)}) %collective-permute-start.8) | collective-permute-done | bytes 32800 | tf_op jit(solution)/shard_map/ppermute | solution.py:280
  25.9 0.6 %early_score.1.early_ref = f32[768,32]{1,0:T(8,128)S(1)} custom-call(bf16[768,4096]{1,0:T(8,128)(2,1)S(1)} %bitcast.8, bf16[32,512]{1,0:T(8,128)(2,1)S(1)} %precondition.1.rest_0_, bf16[32,512]{1,0:T(8,128)(2,1)S(1)} %collective-permute-done.7.rest_1_), custom_call_target="tpu_custom_call" | custom-call | tf_op jit(solution)/shard_map/early_score/pallas_call | solution.py:258
  26.5 0.5 %collective-permute-done.9.rest_1_ = bf16[32,512]{1,0:T(8,128)(2,1)S(1)} collective-permute-done((bf16[32,512]{1,0:T(8,128)(2,1)S(1)}, bf16[32,512]{1,0:T(8,128)(2,1)S(1)}, u32[]{:S(2)}, u32[]{:S(2)}) %collective-permute-start.9) | collective-permute-done | bytes 32800 | tf_op jit(solution)/shard_map/ppermute | solution.py:280
  27.1 1.4 %score.1 = (f32[8,768]{1,0:T(8,128)S(1)}, f32[8,768]{1,0:T(8,128)S(1)}, f32[8,768]{1,0:T(8,128)S(1)}, f32[8,768]{1,0:T(8,128)S(1)}) custom-call(f32[768,32]{1,0:T(8,128)S(1)} %early_score.1.early_ref, bf16[768,4096]{1,0:T(8,128)(2,1)S(1)} %bitcast.9, bf16[32,512]{1,0:T(8,128)(2,1)S(1)} %collective-permute-done.8.rest_0_, ...), custom_call_target="tpu_custom_call" | custom-call | tf_op jit(solution)/shard_map/score/pallas_call | solution.py:267
  28.5 1.6 %collective-permute-start.14 = (f32[8,768]{1,0:T(8,128)S(1)}, f32[8,768]{1,0:T(8,128)S(1)}, u32[]{:S(2)}, u32[]{:S(2)}) collective-permute-start(f32[8,768]{1,0:T(8,128)S(1)} %get-tuple-element.16), channel_id=1, source_target_pairs={{0,8},{8,24},{24,16},{16,0},{1,9},{9,25},{25,17},{17,1},{2,10},{10... | collective-permute-start | bytes 73736 | tf_op jit(solution)/shard_map/ppermute | solution.py:286
  30.1 2.5 %collective-permute-start.15 = (f32[8,768]{1,0:T(8,128)S(1)}, f32[8,768]{1,0:T(8,128)S(1)}, u32[]{:S(2)}, u32[]{:S(2)}) collective-permute-start(f32[8,768]{1,0:T(8,128)S(1)} %get-tuple-element.17), channel_id=1, source_target_pairs={{0,24},{8,16},{24,0},{16,8},{1,25},{9,17},{25,1},{17,9},{2,26},{10... | collective-permute-start | bytes 73736 | tf_op jit(solution)/shard_map/ppermute | solution.py:286
  32.6 1.6 %collective-permute-start.16 = (f32[8,768]{1,0:T(8,128)S(1)}, f32[8,768]{1,0:T(8,128)S(1)}, u32[]{:S(2)}, u32[]{:S(2)}) collective-permute-start(f32[8,768]{1,0:T(8,128)S(1)} %get-tuple-element.18), channel_id=1, source_target_pairs={{0,16},{8,0},{24,8},{16,24},{1,17},{9,1},{25,9},{17,25},{2,18},{10... | collective-permute-start | bytes 73736 | tf_op jit(solution)/shard_map/ppermute | solution.py:286
  34.2 1.8 %collective-permute-done.15 = f32[8,768]{1,0:T(8,128)S(1)} collective-permute-done((f32[8,768]{1,0:T(8,128)S(1)}, f32[8,768]{1,0:T(8,128)S(1)}, u32[]{:S(2)}, u32[]{:S(2)}) %collective-permute-start.15) | collective-permute-done | bytes 24608 | tf_op jit(solution)/shard_map/ppermute | solution.py:286
  36.0 0.5 %collective-permute-done.16 = f32[8,768]{1,0:T(8,128)S(1)} collective-permute-done((f32[8,768]{1,0:T(8,128)S(1)}, f32[8,768]{1,0:T(8,128)S(1)}, u32[]{:S(2)}, u32[]{:S(2)}) %collective-permute-start.16) | collective-permute-done | bytes 24608 | tf_op jit(solution)/shard_map/ppermute | solution.py:286
  36.4 0.6 %add_add_fusion = f32[8,768]{1,0:T(8,128)} fusion(f32[8,768]{1,0:T(8,128)S(1)} %collective-permute-done.16, f32[8,768]{1,0:T(8,128)S(1)} %collective-permute-done.15, f32[8,768]{1,0:T(8,128)S(1)} %get-tuple-element.15, f32[8,768]{1,0:T(8,128)S(1)} %collective-permute-done.14), kind=kLoop, calls=%fused_computation | loop fusion | flops 18432 | bytes 122880 | tf_op jit(solution)/shard_map/add | solution.py:331
  (20 shorter events, 0.3 us)
Async XLA Ops:
  0.0 25.9 %slice-start = ((s8[6291456]{0:T(1024)(128)(4,1)}), s8[4194304]{0:T(1024)(128)(4,1)S(1)}, s32[]{:S(2)}) async-start(s8[6291456]{0:T(1024)(128)(4,1)} %bitcast.6), calls=%async_computation | async-start | bytes 8388608
  0.0 25.9 %slice-start.1 = ((s8[6291456]{0:T(1024)(128)(4,1)}), s8[2097152]{0:T(1024)(128)(4,1)S(1)}, s32[]{:S(2)}) async-start(s8[6291456]{0:T(1024)(128)(4,1)} %bitcast.6), calls=%async_computation.1 | async-start | bytes 4194304
  8.4 6.2 %collective-permute-start.5 = (bf16[8,4096]{1,0:T(8,128)(2,1)S(1)}, bf16[8,4096]{1,0:T(8,128)(2,1)S(1)}, u32[]{:S(2)}, u32[]{:S(2)}) collective-permute-start(bf16[8,4096]{1,0:T(8,128)(2,1)S(1)} %get-tuple-element.14.rest_0_), channel_id=1, source_target_pairs={{0,6},{1,7},{2,4},{3,5},{4,2},{5,3},{6,0},{7,1},{8,14},{9,15},{10,... | collective-permute-start | bytes 196616 | tf_op jit(solution)/shard_map/ppermute | solution.py:280
  12.4 4.3 %collective-permute-start.3 = (bf16[8,4096]{1,0:T(8,128)(2,1)S(1)}, bf16[8,4096]{1,0:T(8,128)(2,1)S(1)}, u32[]{:S(2)}, u32[]{:S(2)}) collective-permute-start(bf16[8,4096]{1,0:T(8,128)(2,1)S(1)} %get-tuple-element.14.rest_0_), channel_id=1, source_target_pairs={{0,4},{1,5},{2,6},{3,7},{4,0},{5,1},{6,2},{7,3},{8,12},{9,13},{10,... | collective-permute-start | bytes 196616 | tf_op jit(solution)/shard_map/ppermute | solution.py:280
  12.9 4.3 %collective-permute-start.1 = (bf16[8,4096]{1,0:T(8,128)(2,1)S(1)}, bf16[8,4096]{1,0:T(8,128)(2,1)S(1)}, u32[]{:S(2)}, u32[]{:S(2)}) collective-permute-start(bf16[8,4096]{1,0:T(8,128)(2,1)S(1)} %get-tuple-element.14.rest_0_), channel_id=1, source_target_pairs={{0,2},{1,3},{2,0},{3,1},{4,6},{5,7},{6,4},{7,5},{8,10},{9,11},{10,... | collective-permute-start | bytes 196616 | tf_op jit(solution)/shard_map/ppermute | solution.py:280
  13.1 4.1 %collective-permute-start = (bf16[8,4096]{1,0:T(8,128)(2,1)S(1)}, bf16[8,4096]{1,0:T(8,128)(2,1)S(1)}, u32[]{:S(2)}, u32[]{:S(2)}) collective-permute-start(bf16[8,4096]{1,0:T(8,128)(2,1)S(1)} %get-tuple-element.14.rest_0_), channel_id=1, source_target_pairs={{0,1},{1,0},{2,3},{3,2},{4,5},{5,4},{6,7},{7,6},{8,9},{9,8},{10,11... | collective-permute-start | bytes 196616 | tf_op jit(solution)/shard_map/ppermute | solution.py:280
  14.7 2.5 %collective-permute-start.6 = (bf16[8,4096]{1,0:T(8,128)(2,1)S(1)}, bf16[8,4096]{1,0:T(8,128)(2,1)S(1)}, u32[]{:S(2)}, u32[]{:S(2)}) collective-permute-start(bf16[8,4096]{1,0:T(8,128)(2,1)S(1)} %collective-permute-done.5.rest_6_), channel_id=1, source_target_pairs={{0,1},{1,0},{2,3},{3,2},{4,5},{5,4},{6,7},{7,6},{8,9},{9,8},{10,11... | collective-permute-start | bytes 196616 | tf_op jit(solution)/shard_map/ppermute | solution.py:280
  16.7 1.3 %collective-permute-start.4 = (bf16[8,4096]{1,0:T(8,128)(2,1)S(1)}, bf16[8,4096]{1,0:T(8,128)(2,1)S(1)}, u32[]{:S(2)}, u32[]{:S(2)}) collective-permute-start(bf16[8,4096]{1,0:T(8,128)(2,1)S(1)} %collective-permute-done.3.rest_4_), channel_id=1, source_target_pairs={{0,1},{1,0},{2,3},{3,2},{4,5},{5,4},{6,7},{7,6},{8,9},{9,8},{10,11... | collective-permute-start | bytes 196616 | tf_op jit(solution)/shard_map/ppermute | solution.py:280
  17.2 1.3 %collective-permute-start.2 = (bf16[8,4096]{1,0:T(8,128)(2,1)S(1)}, bf16[8,4096]{1,0:T(8,128)(2,1)S(1)}, u32[]{:S(2)}, u32[]{:S(2)}) collective-permute-start(bf16[8,4096]{1,0:T(8,128)(2,1)S(1)} %collective-permute-done.1.rest_2_), channel_id=1, source_target_pairs={{0,1},{1,0},{2,3},{3,2},{4,5},{5,4},{6,7},{7,6},{8,9},{9,8},{10,11... | collective-permute-start | bytes 196616 | tf_op jit(solution)/shard_map/ppermute | solution.py:280
  19.9 4.8 %collective-permute-start.12 = (bf16[32,512]{1,0:T(8,128)(2,1)S(1)}, bf16[32,512]{1,0:T(8,128)(2,1)S(1)}, u32[]{:S(2)}, u32[]{:S(2)}) collective-permute-start(bf16[32,512]{1,0:T(8,128)(2,1)S(1)} %precondition.1.rest_0_), channel_id=1, source_target_pairs={{0,6},{1,7},{2,4},{3,5},{4,2},{5,3},{6,0},{7,1},{8,14},{9,15},{10,... | collective-permute-start | bytes 98312 | tf_op jit(solution)/shard_map/ppermute | solution.py:280
  21.4 3.9 %collective-permute-start.10 = (bf16[32,512]{1,0:T(8,128)(2,1)S(1)}, bf16[32,512]{1,0:T(8,128)(2,1)S(1)}, u32[]{:S(2)}, u32[]{:S(2)}) collective-permute-start(bf16[32,512]{1,0:T(8,128)(2,1)S(1)} %precondition.1.rest_0_), channel_id=1, source_target_pairs={{0,4},{1,5},{2,6},{3,7},{4,0},{5,1},{6,2},{7,3},{8,12},{9,13},{10,... | collective-permute-start | bytes 98312 | tf_op jit(solution)/shard_map/ppermute | solution.py:280
  22.0 3.9 %collective-permute-start.8 = (bf16[32,512]{1,0:T(8,128)(2,1)S(1)}, bf16[32,512]{1,0:T(8,128)(2,1)S(1)}, u32[]{:S(2)}, u32[]{:S(2)}) collective-permute-start(bf16[32,512]{1,0:T(8,128)(2,1)S(1)} %precondition.1.rest_0_), channel_id=1, source_target_pairs={{0,2},{1,3},{2,0},{3,1},{4,6},{5,7},{6,4},{7,5},{8,10},{9,11},{10,... | collective-permute-start | bytes 98312 | tf_op jit(solution)/shard_map/ppermute | solution.py:280
  23.4 2.5 %collective-permute-start.7 = (bf16[32,512]{1,0:T(8,128)(2,1)S(1)}, bf16[32,512]{1,0:T(8,128)(2,1)S(1)}, u32[]{:S(2)}, u32[]{:S(2)}) collective-permute-start(bf16[32,512]{1,0:T(8,128)(2,1)S(1)} %precondition.1.rest_0_), channel_id=1, source_target_pairs={{0,1},{1,0},{2,3},{3,2},{4,5},{5,4},{6,7},{7,6},{8,9},{9,8},{10,11... | collective-permute-start | bytes 98312 | tf_op jit(solution)/shard_map/ppermute | solution.py:280
  24.7 1.7 %collective-permute-start.13 = (bf16[32,512]{1,0:T(8,128)(2,1)S(1)}, bf16[32,512]{1,0:T(8,128)(2,1)S(1)}, u32[]{:S(2)}, u32[]{:S(2)}) collective-permute-start(bf16[32,512]{1,0:T(8,128)(2,1)S(1)} %collective-permute-done.12.rest_4_), channel_id=1, source_target_pairs={{0,1},{1,0},{2,3},{3,2},{4,5},{5,4},{6,7},{7,6},{8,9},{9,8},{10,11... | collective-permute-start | bytes 98312 | tf_op jit(solution)/shard_map/ppermute | solution.py:280
  25.3 1.2 %collective-permute-start.11 = (bf16[32,512]{1,0:T(8,128)(2,1)S(1)}, bf16[32,512]{1,0:T(8,128)(2,1)S(1)}, u32[]{:S(2)}, u32[]{:S(2)}) collective-permute-start(bf16[32,512]{1,0:T(8,128)(2,1)S(1)} %collective-permute-done.10.rest_2_), channel_id=1, source_target_pairs={{0,1},{1,0},{2,3},{3,2},{4,5},{5,4},{6,7},{7,6},{8,9},{9,8},{10,11... | collective-permute-start | bytes 98312 | tf_op jit(solution)/shard_map/ppermute | solution.py:280
  25.9 1.2 %collective-permute-start.9 = (bf16[32,512]{1,0:T(8,128)(2,1)S(1)}, bf16[32,512]{1,0:T(8,128)(2,1)S(1)}, u32[]{:S(2)}, u32[]{:S(2)}) collective-permute-start(bf16[32,512]{1,0:T(8,128)(2,1)S(1)} %collective-permute-done.8.rest_0_), channel_id=1, source_target_pairs={{0,1},{1,0},{2,3},{3,2},{4,5},{5,4},{6,7},{7,6},{8,9},{9,8},{10,11... | collective-permute-start | bytes 98312 | tf_op jit(solution)/shard_map/ppermute | solution.py:280
  28.5 5.7 %collective-permute-start.14 = (f32[8,768]{1,0:T(8,128)S(1)}, f32[8,768]{1,0:T(8,128)S(1)}, u32[]{:S(2)}, u32[]{:S(2)}) collective-permute-start(f32[8,768]{1,0:T(8,128)S(1)} %get-tuple-element.16), channel_id=1, source_target_pairs={{0,8},{8,24},{24,16},{16,0},{1,9},{9,25},{25,17},{17,1},{2,10},{10... | collective-permute-start | bytes 73736 | tf_op jit(solution)/shard_map/ppermute | solution.py:286
  30.1 5.8 %collective-permute-start.15 = (f32[8,768]{1,0:T(8,128)S(1)}, f32[8,768]{1,0:T(8,128)S(1)}, u32[]{:S(2)}, u32[]{:S(2)}) collective-permute-start(f32[8,768]{1,0:T(8,128)S(1)} %get-tuple-element.17), channel_id=1, source_target_pairs={{0,24},{8,16},{24,0},{16,8},{1,25},{9,17},{25,1},{17,9},{2,26},{10... | collective-permute-start | bytes 73736 | tf_op jit(solution)/shard_map/ppermute | solution.py:286
  32.6 3.8 %collective-permute-start.16 = (f32[8,768]{1,0:T(8,128)S(1)}, f32[8,768]{1,0:T(8,128)S(1)}, u32[]{:S(2)}, u32[]{:S(2)}) collective-permute-start(f32[8,768]{1,0:T(8,128)S(1)} %get-tuple-element.18), channel_id=1, source_target_pairs={{0,16},{8,0},{24,8},{16,24},{1,17},{9,1},{25,9},{17,25},{2,18},{10... | collective-permute-start | bytes 73736 | tf_op jit(solution)/shard_map/ppermute | solution.py:286

commit v6 on v5

--- a/solution.py
+++ b/solution.py
@@ -252,9 +252,10 @@
         share_refs[place][...] = total[pl.ds(row, share), :]
 
 
-def score(pieces, store_rows, queries, parts, early_places):
+def score(pieces, store_rows, queries, parts):
     stores = store_rows.shape[0]
-    late_places = [d for d in range(len(pieces)) if d not in early_places]
+    early_places = range(0, len(pieces), 2)
+    late_places = range(1, len(pieces), 2)
     early = pl.pallas_call(
         functools.partial(early_score_kernel, early_places),
         in_specs=[pl.BlockSpec(memory_space=pltpu.VMEM)] * (1 + len(early_places)),
@@ -325,7 +326,7 @@
         row_count * capacity,
     )
     column_part = precondition(pieces_of_all(feature, "row"), curvature, placer)
-    shares = score(pieces_of_all(column_part, "row"), store_grads[0], queries, mod_count, [0, 1])
+    shares = score(pieces_of_all(column_part, "row"), store_grads[0], queries, mod_count)
     total = shares[0]
     for places in range(1, mod_count):
         total = total + send_on(shares[places], "mod", places)

time: 37.2 us -> 36.8 us (0.989)
  waiting for transfers between devices: 10.6 us -> 10.2 us
    pallas_call x1, Pallas kernels: 1.42 us -> 1.01 us  [score(): pl.pallas_call(functools.partial(score_kernel, late_places, parts), in_sp...]
    pallas_call x1, Pallas kernels: 0.56 us -> 0.96 us  [score(): pl.pallas_call(functools.partial(early_score_kernel, early_places), in_sp...]
    ppermute x14, waiting for transfers between devices: 8.37 us -> 7.98 us  [exchange(): return lax.ppermute(array, axis, [(i, i ^ distance) for i in range(count)])]
  transfers between devices with their start and end apart: 17 -> 17, of which waited for: 12 -> 11; matrix products, arithmetic and copies ran while one was open for 0% -> 0% of each run, Pallas kernels for 1% -> 3%
where the time goes in v6:
time: 36.8 us; the launch traced here: 36.6 us
  starting transfers between devices  13.8 us (38%)
  Pallas kernels  11.9 us (32%)
  waiting for transfers between devices  10.2 us (28%)
  other arithmetic  0.62 us (2%)
    pallas_call x1, Pallas kernels, featurize(): pl.pallas_call(featurize_kernel, in_specs=[pl.BlockSpec(memory_space=pl.A...  8.43 us
    ppermute x14, starting transfers between devices, exchange(): return lax.ppermute(array, axis, [(i, i ^ distance) for i in range(count)])  8.14 us
    ppermute x14, waiting for transfers between devices, exchange(): return lax.ppermute(array, axis, [(i, i ^ distance) for i in range(count)])  7.98 us
    ppermute x3, starting transfers between devices, send_on(): lax.ppermute(array, axis, [(order[i], order[(i + places) % count]) for i...  5.7 us
    ppermute x3, waiting for transfers between devices, send_on(): lax.ppermute(array, axis, [(order[i], order[(i + places) % count]) for i...  2.22 us
    pallas_call x1, Pallas kernels, precondition(): pl.pallas_call(precondition_kernel, in_specs=[pl.BlockSpec(memory_space=p...  1.5 us
    pallas_call x1, Pallas kernels, score(): pl.pallas_call(functools.partial(score_kernel, late_places, parts), in_sp...  1.01 us
    pallas_call x1, Pallas kernels, score(): pl.pallas_call(functools.partial(early_score_kernel, early_places), in_sp...  0.96 us
  transfers between devices with their start and end apart: 17, of which 11 were waited for; matrix products, arithmetic and copies ran while one was open for 0% of the time, Pallas kernels for 3%

profile of v6, /device:TPU:0, one launch (start us, length us, event | category | flops | bytes accessed | tf_op | source)
XLA Modules:
  0.0 36.6 jit_solution(5655555181571227330)
XLA Ops:
  0.0 8.4 %featurize.1 = (bf16[8,4096]{1,0:T(8,128)(2,1)S(1)}, f32[32,64]{1,0:T(8,128)S(1)}, bf16[512,4096]{1,0:T(8,128)(2,1)S(1)}) custom-call(s32[32]{0:T(128)} %lengths_hbm.1, s32[32]{0:T(128)} %owners_hbm.1, bf16[512,4096]{1,0:T(8,128)(2,1)} %bitcast.12, bf16[1024,4096]{1,0:T(8,128)(2,1)} %bitcast.10, bf16[1024,4096]{1,0:T(8,128)(2,1)} %bitcast.11, ...), custom_call_target="tpu_custom_call" | custom-call | tf_op jit(solution)/shard_map/featurize/pallas_call | solution.py:176
  8.4 4.0 %collective-permute-start.5 = (bf16[8,4096]{1,0:T(8,128)(2,1)S(1)}, bf16[8,4096]{1,0:T(8,128)(2,1)S(1)}, u32[]{:S(2)}, u32[]{:S(2)}) collective-permute-start(bf16[8,4096]{1,0:T(8,128)(2,1)S(1)} %get-tuple-element.14.rest_0_), channel_id=1, source_target_pairs={{0,6},{1,7},{2,4},{3,5},{4,2},{5,3},{6,0},{7,1},{8,14},{9,15},{10,... | collective-permute-start | bytes 196616 | tf_op jit(solution)/shard_map/ppermute | solution.py:281
  12.4 0.5 %collective-permute-start.3 = (bf16[8,4096]{1,0:T(8,128)(2,1)S(1)}, bf16[8,4096]{1,0:T(8,128)(2,1)S(1)}, u32[]{:S(2)}, u32[]{:S(2)}) collective-permute-start(bf16[8,4096]{1,0:T(8,128)(2,1)S(1)} %get-tuple-element.14.rest_0_), channel_id=1, source_target_pairs={{0,4},{1,5},{2,6},{3,7},{4,0},{5,1},{6,2},{7,3},{8,12},{9,13},{10,... | collective-permute-start | bytes 196616 | tf_op jit(solution)/shard_map/ppermute | solution.py:281
  13.1 1.6 %collective-permute-done.5.rest_6_ = bf16[8,4096]{1,0:T(8,128)(2,1)S(1)} collective-permute-done((bf16[8,4096]{1,0:T(8,128)(2,1)S(1)}, bf16[8,4096]{1,0:T(8,128)(2,1)S(1)}, u32[]{:S(2)}, u32[]{:S(2)}) %collective-permute-start.5) | collective-permute-done | bytes 65568 | tf_op jit(solution)/shard_map/ppermute | solution.py:281
  14.7 2.0 %collective-permute-done.3.rest_4_ = bf16[8,4096]{1,0:T(8,128)(2,1)S(1)} collective-permute-done((bf16[8,4096]{1,0:T(8,128)(2,1)S(1)}, bf16[8,4096]{1,0:T(8,128)(2,1)S(1)}, u32[]{:S(2)}, u32[]{:S(2)}) %collective-permute-start.3) | collective-permute-done | bytes 65568 | tf_op jit(solution)/shard_map/ppermute | solution.py:281
  16.7 0.5 %collective-permute-done.1.rest_2_ = bf16[8,4096]{1,0:T(8,128)(2,1)S(1)} collective-permute-done((bf16[8,4096]{1,0:T(8,128)(2,1)S(1)}, bf16[8,4096]{1,0:T(8,128)(2,1)S(1)}, u32[]{:S(2)}, u32[]{:S(2)}) %collective-permute-start.1) | collective-permute-done | bytes 65568 | tf_op jit(solution)/shard_map/ppermute | solution.py:281
  17.2 0.7 %collective-permute-done.4.rest_5_ = bf16[8,4096]{1,0:T(8,128)(2,1)S(1)} collective-permute-done((bf16[8,4096]{1,0:T(8,128)(2,1)S(1)}, bf16[8,4096]{1,0:T(8,128)(2,1)S(1)}, u32[]{:S(2)}, u32[]{:S(2)}) %collective-permute-start.4) | collective-permute-done | bytes 65568 | tf_op jit(solution)/shard_map/ppermute | solution.py:281
  17.9 0.5 %collective-permute-done.2.rest_3_ = bf16[8,4096]{1,0:T(8,128)(2,1)S(1)} collective-permute-done((bf16[8,4096]{1,0:T(8,128)(2,1)S(1)}, bf16[8,4096]{1,0:T(8,128)(2,1)S(1)}, u32[]{:S(2)}, u32[]{:S(2)}) %collective-permute-start.2) | collective-permute-done | bytes 65568 | tf_op jit(solution)/shard_map/ppermute | solution.py:281
  18.4 1.5 %precondition.1.rest_0_ = bf16[32,512]{1,0:T(8,128)(2,1)S(1)} custom-call(bf16[512,4096]{1,0:T(8,128)(2,1)S(1)} %get-tuple-element.12.curvature_ref, f32[32,64]{1,0:T(8,128)S(1)} %get-tuple-element.13.placer_ref, bf16[8,4096]{1,0:T(8,128)(2,1)S(1)} %get-tuple-element.14.rest_0_, bf16[8,4096]{1,0:T(8,128)(2,1)S(1)} %collective-permute-done.rest_1_, ...), custom_call_target="tpu_custom_call" | custom-call | tf_op jit(solution)/shard_map/precondition/pallas_call | solution.py:218
  19.9 1.5 %collective-permute-start.9 = (bf16[32,512]{1,0:T(8,128)(2,1)S(1)}, bf16[32,512]{1,0:T(8,128)(2,1)S(1)}, u32[]{:S(2)}, u32[]{:S(2)}) collective-permute-start(bf16[32,512]{1,0:T(8,128)(2,1)S(1)} %precondition.1.rest_0_), channel_id=1, source_target_pairs={{0,6},{1,7},{2,4},{3,5},{4,2},{5,3},{6,0},{7,1},{8,14},{9,15},{10,... | collective-permute-start | bytes 98312 | tf_op jit(solution)/shard_map/ppermute | solution.py:281
  21.4 0.5 %collective-permute-start.8 = (bf16[32,512]{1,0:T(8,128)(2,1)S(1)}, bf16[32,512]{1,0:T(8,128)(2,1)S(1)}, u32[]{:S(2)}, u32[]{:S(2)}) collective-permute-start(bf16[32,512]{1,0:T(8,128)(2,1)S(1)} %precondition.1.rest_0_), channel_id=1, source_target_pairs={{0,4},{1,5},{2,6},{3,7},{4,0},{5,1},{6,2},{7,3},{8,12},{9,13},{10,... | collective-permute-start | bytes 98312 | tf_op jit(solution)/shard_map/ppermute | solution.py:281
  22.0 1.5 %collective-permute-start.7 = (bf16[32,512]{1,0:T(8,128)(2,1)S(1)}, bf16[32,512]{1,0:T(8,128)(2,1)S(1)}, u32[]{:S(2)}, u32[]{:S(2)}) collective-permute-start(bf16[32,512]{1,0:T(8,128)(2,1)S(1)} %precondition.1.rest_0_), channel_id=1, source_target_pairs={{0,2},{1,3},{2,0},{3,1},{4,6},{5,7},{6,4},{7,5},{8,10},{9,11},{10,... | collective-permute-start | bytes 98312 | tf_op jit(solution)/shard_map/ppermute | solution.py:281
  23.4 1.3 %collective-permute-done.9.rest_3_ = bf16[32,512]{1,0:T(8,128)(2,1)S(1)} collective-permute-done((bf16[32,512]{1,0:T(8,128)(2,1)S(1)}, bf16[32,512]{1,0:T(8,128)(2,1)S(1)}, u32[]{:S(2)}, u32[]{:S(2)}) %collective-permute-start.9) | collective-permute-done | bytes 32800 | tf_op jit(solution)/shard_map/ppermute | solution.py:281
  24.7 0.6 %collective-permute-done.8.rest_2_ = bf16[32,512]{1,0:T(8,128)(2,1)S(1)} collective-permute-done((bf16[32,512]{1,0:T(8,128)(2,1)S(1)}, bf16[32,512]{1,0:T(8,128)(2,1)S(1)}, u32[]{:S(2)}, u32[]{:S(2)}) %collective-permute-start.8) | collective-permute-done | bytes 32800 | tf_op jit(solution)/shard_map/ppermute | solution.py:281
  25.3 0.5 %collective-permute-done.7.rest_1_ = bf16[32,512]{1,0:T(8,128)(2,1)S(1)} collective-permute-done((bf16[32,512]{1,0:T(8,128)(2,1)S(1)}, bf16[32,512]{1,0:T(8,128)(2,1)S(1)}, u32[]{:S(2)}, u32[]{:S(2)}) %collective-permute-start.7) | collective-permute-done | bytes 32800 | tf_op jit(solution)/shard_map/ppermute | solution.py:281
  25.9 1.0 %early_score.1.early_ref = f32[768,32]{1,0:T(8,128)S(1)} custom-call(bf16[768,4096]{1,0:T(8,128)(2,1)S(1)} %bitcast.8, bf16[32,512]{1,0:T(8,128)(2,1)S(1)} %precondition.1.rest_0_, bf16[32,512]{1,0:T(8,128)(2,1)S(1)} %collective-permute-done.7.rest_1_, bf16[32,512]{1,0:T(8,128)(2,1)S(1)} %collective-permute-done.8.rest_2_, ...), custom_call_target="tpu_custom_call" | custom-call | tf_op jit(solution)/shard_map/early_score/pallas_call | solution.py:259
  26.9 0.2 collective-permute-done.11.rest_1_
  27.1 1.0 %score.1 = (f32[8,768]{1,0:T(8,128)S(1)}, f32[8,768]{1,0:T(8,128)S(1)}, f32[8,768]{1,0:T(8,128)S(1)}, f32[8,768]{1,0:T(8,128)S(1)}) custom-call(f32[768,32]{1,0:T(8,128)S(1)} %early_score.1.early_ref, bf16[768,4096]{1,0:T(8,128)(2,1)S(1)} %bitcast.9, bf16[32,512]{1,0:T(8,128)(2,1)S(1)} %collective-permute-done.10.rest_0_, ...), custom_call_target="tpu_custom_call" | custom-call | tf_op jit(solution)/shard_map/score/pallas_call | solution.py:268
  28.1 1.6 %collective-permute-start.14 = (f32[8,768]{1,0:T(8,128)S(1)}, f32[8,768]{1,0:T(8,128)S(1)}, u32[]{:S(2)}, u32[]{:S(2)}) collective-permute-start(f32[8,768]{1,0:T(8,128)S(1)} %get-tuple-element.16), channel_id=1, source_target_pairs={{0,8},{8,24},{24,16},{16,0},{1,9},{9,25},{25,17},{17,1},{2,10},{10... | collective-permute-start | bytes 73736 | tf_op jit(solution)/shard_map/ppermute | solution.py:287
  29.7 2.5 %collective-permute-start.15 = (f32[8,768]{1,0:T(8,128)S(1)}, f32[8,768]{1,0:T(8,128)S(1)}, u32[]{:S(2)}, u32[]{:S(2)}) collective-permute-start(f32[8,768]{1,0:T(8,128)S(1)} %get-tuple-element.17), channel_id=1, source_target_pairs={{0,24},{8,16},{24,0},{16,8},{1,25},{9,17},{25,1},{17,9},{2,26},{10... | collective-permute-start | bytes 73736 | tf_op jit(solution)/shard_map/ppermute | solution.py:287
  32.2 1.6 %collective-permute-start.16 = (f32[8,768]{1,0:T(8,128)S(1)}, f32[8,768]{1,0:T(8,128)S(1)}, u32[]{:S(2)}, u32[]{:S(2)}) collective-permute-start(f32[8,768]{1,0:T(8,128)S(1)} %get-tuple-element.18), channel_id=1, source_target_pairs={{0,16},{8,0},{24,8},{16,24},{1,17},{9,1},{25,9},{17,25},{2,18},{10... | collective-permute-start | bytes 73736 | tf_op jit(solution)/shard_map/ppermute | solution.py:287
  33.8 1.6 %collective-permute-done.15 = f32[8,768]{1,0:T(8,128)S(1)} collective-permute-done((f32[8,768]{1,0:T(8,128)S(1)}, f32[8,768]{1,0:T(8,128)S(1)}, u32[]{:S(2)}, u32[]{:S(2)}) %collective-permute-start.15) | collective-permute-done | bytes 24608 | tf_op jit(solution)/shard_map/ppermute | solution.py:287
  35.4 0.6 %collective-permute-done.16 = f32[8,768]{1,0:T(8,128)S(1)} collective-permute-done((f32[8,768]{1,0:T(8,128)S(1)}, f32[8,768]{1,0:T(8,128)S(1)}, u32[]{:S(2)}, u32[]{:S(2)}) %collective-permute-start.16) | collective-permute-done | bytes 24608 | tf_op jit(solution)/shard_map/ppermute | solution.py:287
  36.0 0.6 %add_add_fusion = f32[8,768]{1,0:T(8,128)} fusion(f32[8,768]{1,0:T(8,128)S(1)} %collective-permute-done.16, f32[8,768]{1,0:T(8,128)S(1)} %collective-permute-done.15, f32[8,768]{1,0:T(8,128)S(1)} %get-tuple-element.15, f32[8,768]{1,0:T(8,128)S(1)} %collective-permute-done.14), kind=kLoop, calls=%fused_computation | loop fusion | flops 18432 | bytes 122880 | tf_op jit(solution)/shard_map/add | solution.py:332
  (20 shorter events, 0.2 us)
Async XLA Ops:
  0.0 25.9 %slice-start = ((s8[6291456]{0:T(1024)(128)(4,1)}), s8[4194304]{0:T(1024)(128)(4,1)S(1)}, s32[]{:S(2)}) async-start(s8[6291456]{0:T(1024)(128)(4,1)} %bitcast.6), calls=%async_computation | async-start | bytes 8388608
  0.0 25.9 %slice-start.1 = ((s8[6291456]{0:T(1024)(128)(4,1)}), s8[2097152]{0:T(1024)(128)(4,1)S(1)}, s32[]{:S(2)}) async-start(s8[6291456]{0:T(1024)(128)(4,1)} %bitcast.6), calls=%async_computation.1 | async-start | bytes 4194304
  8.4 6.2 %collective-permute-start.5 = (bf16[8,4096]{1,0:T(8,128)(2,1)S(1)}, bf16[8,4096]{1,0:T(8,128)(2,1)S(1)}, u32[]{:S(2)}, u32[]{:S(2)}) collective-permute-start(bf16[8,4096]{1,0:T(8,128)(2,1)S(1)} %get-tuple-element.14.rest_0_), channel_id=1, source_target_pairs={{0,6},{1,7},{2,4},{3,5},{4,2},{5,3},{6,0},{7,1},{8,14},{9,15},{10,... | collective-permute-start | bytes 196616 | tf_op jit(solution)/shard_map/ppermute | solution.py:281
  12.4 4.3 %collective-permute-start.3 = (bf16[8,4096]{1,0:T(8,128)(2,1)S(1)}, bf16[8,4096]{1,0:T(8,128)(2,1)S(1)}, u32[]{:S(2)}, u32[]{:S(2)}) collective-permute-start(bf16[8,4096]{1,0:T(8,128)(2,1)S(1)} %get-tuple-element.14.rest_0_), channel_id=1, source_target_pairs={{0,4},{1,5},{2,6},{3,7},{4,0},{5,1},{6,2},{7,3},{8,12},{9,13},{10,... | collective-permute-start | bytes 196616 | tf_op jit(solution)/shard_map/ppermute | solution.py:281
  12.9 4.3 %collective-permute-start.1 = (bf16[8,4096]{1,0:T(8,128)(2,1)S(1)}, bf16[8,4096]{1,0:T(8,128)(2,1)S(1)}, u32[]{:S(2)}, u32[]{:S(2)}) collective-permute-start(bf16[8,4096]{1,0:T(8,128)(2,1)S(1)} %get-tuple-element.14.rest_0_), channel_id=1, source_target_pairs={{0,2},{1,3},{2,0},{3,1},{4,6},{5,7},{6,4},{7,5},{8,10},{9,11},{10,... | collective-permute-start | bytes 196616 | tf_op jit(solution)/shard_map/ppermute | solution.py:281
  13.0 4.1 %collective-permute-start = (bf16[8,4096]{1,0:T(8,128)(2,1)S(1)}, bf16[8,4096]{1,0:T(8,128)(2,1)S(1)}, u32[]{:S(2)}, u32[]{:S(2)}) collective-permute-start(bf16[8,4096]{1,0:T(8,128)(2,1)S(1)} %get-tuple-element.14.rest_0_), channel_id=1, source_target_pairs={{0,1},{1,0},{2,3},{3,2},{4,5},{5,4},{6,7},{7,6},{8,9},{9,8},{10,11... | collective-permute-start | bytes 196616 | tf_op jit(solution)/shard_map/ppermute | solution.py:281
  14.7 2.5 %collective-permute-start.6 = (bf16[8,4096]{1,0:T(8,128)(2,1)S(1)}, bf16[8,4096]{1,0:T(8,128)(2,1)S(1)}, u32[]{:S(2)}, u32[]{:S(2)}) collective-permute-start(bf16[8,4096]{1,0:T(8,128)(2,1)S(1)} %collective-permute-done.5.rest_6_), channel_id=1, source_target_pairs={{0,1},{1,0},{2,3},{3,2},{4,5},{5,4},{6,7},{7,6},{8,9},{9,8},{10,11... | collective-permute-start | bytes 196616 | tf_op jit(solution)/shard_map/ppermute | solution.py:281
  16.7 1.3 %collective-permute-start.4 = (bf16[8,4096]{1,0:T(8,128)(2,1)S(1)}, bf16[8,4096]{1,0:T(8,128)(2,1)S(1)}, u32[]{:S(2)}, u32[]{:S(2)}) collective-permute-start(bf16[8,4096]{1,0:T(8,128)(2,1)S(1)} %collective-permute-done.3.rest_4_), channel_id=1, source_target_pairs={{0,1},{1,0},{2,3},{3,2},{4,5},{5,4},{6,7},{7,6},{8,9},{9,8},{10,11... | collective-permute-start | bytes 196616 | tf_op jit(solution)/shard_map/ppermute | solution.py:281
  17.2 1.3 %collective-permute-start.2 = (bf16[8,4096]{1,0:T(8,128)(2,1)S(1)}, bf16[8,4096]{1,0:T(8,128)(2,1)S(1)}, u32[]{:S(2)}, u32[]{:S(2)}) collective-permute-start(bf16[8,4096]{1,0:T(8,128)(2,1)S(1)} %collective-permute-done.1.rest_2_), channel_id=1, source_target_pairs={{0,1},{1,0},{2,3},{3,2},{4,5},{5,4},{6,7},{7,6},{8,9},{9,8},{10,11... | collective-permute-start | bytes 196616 | tf_op jit(solution)/shard_map/ppermute | solution.py:281
  19.9 4.8 %collective-permute-start.9 = (bf16[32,512]{1,0:T(8,128)(2,1)S(1)}, bf16[32,512]{1,0:T(8,128)(2,1)S(1)}, u32[]{:S(2)}, u32[]{:S(2)}) collective-permute-start(bf16[32,512]{1,0:T(8,128)(2,1)S(1)} %precondition.1.rest_0_), channel_id=1, source_target_pairs={{0,6},{1,7},{2,4},{3,5},{4,2},{5,3},{6,0},{7,1},{8,14},{9,15},{10,... | collective-permute-start | bytes 98312 | tf_op jit(solution)/shard_map/ppermute | solution.py:281
  21.4 3.9 %collective-permute-start.8 = (bf16[32,512]{1,0:T(8,128)(2,1)S(1)}, bf16[32,512]{1,0:T(8,128)(2,1)S(1)}, u32[]{:S(2)}, u32[]{:S(2)}) collective-permute-start(bf16[32,512]{1,0:T(8,128)(2,1)S(1)} %precondition.1.rest_0_), channel_id=1, source_target_pairs={{0,4},{1,5},{2,6},{3,7},{4,0},{5,1},{6,2},{7,3},{8,12},{9,13},{10,... | collective-permute-start | bytes 98312 | tf_op jit(solution)/shard_map/ppermute | solution.py:281
  22.0 3.9 %collective-permute-start.7 = (bf16[32,512]{1,0:T(8,128)(2,1)S(1)}, bf16[32,512]{1,0:T(8,128)(2,1)S(1)}, u32[]{:S(2)}, u32[]{:S(2)}) collective-permute-start(bf16[32,512]{1,0:T(8,128)(2,1)S(1)} %precondition.1.rest_0_), channel_id=1, source_target_pairs={{0,2},{1,3},{2,0},{3,1},{4,6},{5,7},{6,4},{7,5},{8,10},{9,11},{10,... | collective-permute-start | bytes 98312 | tf_op jit(solution)/shard_map/ppermute | solution.py:281
  23.4 3.4 %collective-permute-start.10 = (bf16[32,512]{1,0:T(8,128)(2,1)S(1)}, bf16[32,512]{1,0:T(8,128)(2,1)S(1)}, u32[]{:S(2)}, u32[]{:S(2)}) collective-permute-start(bf16[32,512]{1,0:T(8,128)(2,1)S(1)} %precondition.1.rest_0_), channel_id=1, source_target_pairs={{0,1},{1,0},{2,3},{3,2},{4,5},{5,4},{6,7},{7,6},{8,9},{9,8},{10,11... | collective-permute-start | bytes 98312 | tf_op jit(solution)/shard_map/ppermute | solution.py:281
  24.7 2.1 %collective-permute-start.13 = (bf16[32,512]{1,0:T(8,128)(2,1)S(1)}, bf16[32,512]{1,0:T(8,128)(2,1)S(1)}, u32[]{:S(2)}, u32[]{:S(2)}) collective-permute-start(bf16[32,512]{1,0:T(8,128)(2,1)S(1)} %collective-permute-done.9.rest_3_), channel_id=1, source_target_pairs={{0,1},{1,0},{2,3},{3,2},{4,5},{5,4},{6,7},{7,6},{8,9},{9,8},{10,11... | collective-permute-start | bytes 98312 | tf_op jit(solution)/shard_map/ppermute | solution.py:281
  25.3 1.5 %collective-permute-start.12 = (bf16[32,512]{1,0:T(8,128)(2,1)S(1)}, bf16[32,512]{1,0:T(8,128)(2,1)S(1)}, u32[]{:S(2)}, u32[]{:S(2)}) collective-permute-start(bf16[32,512]{1,0:T(8,128)(2,1)S(1)} %collective-permute-done.8.rest_2_), channel_id=1, source_target_pairs={{0,1},{1,0},{2,3},{3,2},{4,5},{5,4},{6,7},{7,6},{8,9},{9,8},{10,11... | collective-permute-start | bytes 98312 | tf_op jit(solution)/shard_map/ppermute | solution.py:281
  25.9 1.2 %collective-permute-start.11 = (bf16[32,512]{1,0:T(8,128)(2,1)S(1)}, bf16[32,512]{1,0:T(8,128)(2,1)S(1)}, u32[]{:S(2)}, u32[]{:S(2)}) collective-permute-start(bf16[32,512]{1,0:T(8,128)(2,1)S(1)} %collective-permute-done.7.rest_1_), channel_id=1, source_target_pairs={{0,1},{1,0},{2,3},{3,2},{4,5},{5,4},{6,7},{7,6},{8,9},{9,8},{10,11... | collective-permute-start | bytes 98312 | tf_op jit(solution)/shard_map/ppermute | solution.py:281
  28.1 5.7 %collective-permute-start.14 = (f32[8,768]{1,0:T(8,128)S(1)}, f32[8,768]{1,0:T(8,128)S(1)}, u32[]{:S(2)}, u32[]{:S(2)}) collective-permute-start(f32[8,768]{1,0:T(8,128)S(1)} %get-tuple-element.16), channel_id=1, source_target_pairs={{0,8},{8,24},{24,16},{16,0},{1,9},{9,25},{25,17},{17,1},{2,10},{10... | collective-permute-start | bytes 73736 | tf_op jit(solution)/shard_map/ppermute | solution.py:287
  29.7 5.7 %collective-permute-start.15 = (f32[8,768]{1,0:T(8,128)S(1)}, f32[8,768]{1,0:T(8,128)S(1)}, u32[]{:S(2)}, u32[]{:S(2)}) collective-permute-start(f32[8,768]{1,0:T(8,128)S(1)} %get-tuple-element.17), channel_id=1, source_target_pairs={{0,24},{8,16},{24,0},{16,8},{1,25},{9,17},{25,1},{17,9},{2,26},{10... | collective-permute-start | bytes 73736 | tf_op jit(solution)/shard_map/ppermute | solution.py:287
  32.2 3.8 %collective-permute-start.16 = (f32[8,768]{1,0:T(8,128)S(1)}, f32[8,768]{1,0:T(8,128)S(1)}, u32[]{:S(2)}, u32[]{:S(2)}) collective-permute-start(f32[8,768]{1,0:T(8,128)S(1)} %get-tuple-element.18), channel_id=1, source_target_pairs={{0,16},{8,0},{24,8},{16,24},{1,17},{9,1},{25,9},{17,25},{2,18},{10... | collective-permute-start | bytes 73736 | tf_op jit(solution)/shard_map/ppermute | solution.py:287

commit v7 on v6

--- a/solution.py
+++ b/solution.py
@@ -207,8 +207,11 @@
 def precondition_kernel(curvature_ref, placer_ref, *rest):
     piece_refs, out_ref, feature = rest[:-2], rest[-2], rest[-1]
     capacity = piece_refs[0].shape[0]
-    for place, piece_ref in enumerate(piece_refs):
-        feature[pl.ds(place * capacity, capacity), :] = piece_ref[...]
+    for place in range(0, len(piece_refs), 2):
+        both = [ref[...].astype(jnp.float32) for ref in piece_refs[place : place + 2]]
+        feature[pl.ds(place * capacity, 2 * capacity), :] = jnp.concatenate(
+            both, axis=0
+        ).astype(jnp.bfloat16)
     by_slot = contract_last(feature[...], curvature_ref[...]).astype(jnp.bfloat16)
     out_ref[...] = dot(placer_ref[...].astype(jnp.bfloat16), by_slot).astype(jnp.bfloat16)
 

time: 36.8 us -> 36.8 us (level)
  no operation moved by 1% of the time
where the time goes in v7:
time: 36.8 us; the launch traced here: 36.7 us
  starting transfers between devices  13.8 us (38%)
  Pallas kernels  11.9 us (32%)
  waiting for transfers between devices  10.2 us (28%)
  other arithmetic  0.62 us (2%)
    pallas_call x1, Pallas kernels, featurize(): pl.pallas_call(featurize_kernel, in_specs=[pl.BlockSpec(memory_space=pl.A...  8.42 us
    ppermute x14, starting transfers between devices, exchange(): return lax.ppermute(array, axis, [(i, i ^ distance) for i in range(count)])  8.15 us
    ppermute x14, waiting for transfers between devices, exchange(): return lax.ppermute(array, axis, [(i, i ^ distance) for i in range(count)])  7.99 us
    ppermute x3, starting transfers between devices, send_on(): lax.ppermute(array, axis, [(order[i], order[(i + places) % count]) for i...  5.69 us
    ppermute x3, waiting for transfers between devices, send_on(): lax.ppermute(array, axis, [(order[i], order[(i + places) % count]) for i...  2.24 us
    pallas_call x1, Pallas kernels, precondition(): pl.pallas_call(precondition_kernel, in_specs=[pl.BlockSpec(memory_space=p...  1.5 us
    pallas_call x1, Pallas kernels, score(): pl.pallas_call(functools.partial(score_kernel, late_places, parts), in_sp...  1.01 us
    pallas_call x1, Pallas kernels, score(): pl.pallas_call(functools.partial(early_score_kernel, early_places), in_sp...  0.95 us
  transfers between devices with their start and end apart: 17, of which 11 were waited for; matrix products, arithmetic and copies ran while one was open for 0% of the time, Pallas kernels for 3%

profile of v7, /device:TPU:0, one launch (start us, length us, event | category | flops | bytes accessed | tf_op | source)
XLA Modules:
  0.0 36.7 jit_solution(5655555181571227330)
XLA Ops:
  0.0 8.4 %featurize.1 = (bf16[8,4096]{1,0:T(8,128)(2,1)S(1)}, f32[32,64]{1,0:T(8,128)S(1)}, bf16[512,4096]{1,0:T(8,128)(2,1)S(1)}) custom-call(s32[32]{0:T(128)} %lengths_hbm.1, s32[32]{0:T(128)} %owners_hbm.1, bf16[512,4096]{1,0:T(8,128)(2,1)} %bitcast.12, bf16[1024,4096]{1,0:T(8,128)(2,1)} %bitcast.10, bf16[1024,4096]{1,0:T(8,128)(2,1)} %bitcast.11, ...), custom_call_target="tpu_custom_call" | custom-call | tf_op jit(solution)/shard_map/featurize/pallas_call | solution.py:176
  8.4 4.0 %collective-permute-start.5 = (bf16[8,4096]{1,0:T(8,128)(2,1)S(1)}, bf16[8,4096]{1,0:T(8,128)(2,1)S(1)}, u32[]{:S(2)}, u32[]{:S(2)}) collective-permute-start(bf16[8,4096]{1,0:T(8,128)(2,1)S(1)} %get-tuple-element.14.rest_0_), channel_id=1, source_target_pairs={{0,6},{1,7},{2,4},{3,5},{4,2},{5,3},{6,0},{7,1},{8,14},{9,15},{10,... | collective-permute-start | bytes 196616 | tf_op jit(solution)/shard_map/ppermute | solution.py:284
  12.4 0.5 %collective-permute-start.3 = (bf16[8,4096]{1,0:T(8,128)(2,1)S(1)}, bf16[8,4096]{1,0:T(8,128)(2,1)S(1)}, u32[]{:S(2)}, u32[]{:S(2)}) collective-permute-start(bf16[8,4096]{1,0:T(8,128)(2,1)S(1)} %get-tuple-element.14.rest_0_), channel_id=1, source_target_pairs={{0,4},{1,5},{2,6},{3,7},{4,0},{5,1},{6,2},{7,3},{8,12},{9,13},{10,... | collective-permute-start | bytes 196616 | tf_op jit(solution)/shard_map/ppermute | solution.py:284
  13.1 1.6 %collective-permute-done.5.rest_6_ = bf16[8,4096]{1,0:T(8,128)(2,1)S(1)} collective-permute-done((bf16[8,4096]{1,0:T(8,128)(2,1)S(1)}, bf16[8,4096]{1,0:T(8,128)(2,1)S(1)}, u32[]{:S(2)}, u32[]{:S(2)}) %collective-permute-start.5) | collective-permute-done | bytes 65568 | tf_op jit(solution)/shard_map/ppermute | solution.py:284
  14.7 2.0 %collective-permute-done.3.rest_4_ = bf16[8,4096]{1,0:T(8,128)(2,1)S(1)} collective-permute-done((bf16[8,4096]{1,0:T(8,128)(2,1)S(1)}, bf16[8,4096]{1,0:T(8,128)(2,1)S(1)}, u32[]{:S(2)}, u32[]{:S(2)}) %collective-permute-start.3) | collective-permute-done | bytes 65568 | tf_op jit(solution)/shard_map/ppermute | solution.py:284
  16.7 0.5 %collective-permute-done.1.rest_2_ = bf16[8,4096]{1,0:T(8,128)(2,1)S(1)} collective-permute-done((bf16[8,4096]{1,0:T(8,128)(2,1)S(1)}, bf16[8,4096]{1,0:T(8,128)(2,1)S(1)}, u32[]{:S(2)}, u32[]{:S(2)}) %collective-permute-start.1) | collective-permute-done | bytes 65568 | tf_op jit(solution)/shard_map/ppermute | solution.py:284
  17.2 0.7 %collective-permute-done.4.rest_5_ = bf16[8,4096]{1,0:T(8,128)(2,1)S(1)} collective-permute-done((bf16[8,4096]{1,0:T(8,128)(2,1)S(1)}, bf16[8,4096]{1,0:T(8,128)(2,1)S(1)}, u32[]{:S(2)}, u32[]{:S(2)}) %collective-permute-start.4) | collective-permute-done | bytes 65568 | tf_op jit(solution)/shard_map/ppermute | solution.py:284
  17.9 0.5 %collective-permute-done.2.rest_3_ = bf16[8,4096]{1,0:T(8,128)(2,1)S(1)} collective-permute-done((bf16[8,4096]{1,0:T(8,128)(2,1)S(1)}, bf16[8,4096]{1,0:T(8,128)(2,1)S(1)}, u32[]{:S(2)}, u32[]{:S(2)}) %collective-permute-start.2) | collective-permute-done | bytes 65568 | tf_op jit(solution)/shard_map/ppermute | solution.py:284
  18.4 1.5 %precondition.1.rest_0_ = bf16[32,512]{1,0:T(8,128)(2,1)S(1)} custom-call(bf16[512,4096]{1,0:T(8,128)(2,1)S(1)} %get-tuple-element.12.curvature_ref, f32[32,64]{1,0:T(8,128)S(1)} %get-tuple-element.13.placer_ref, bf16[8,4096]{1,0:T(8,128)(2,1)S(1)} %get-tuple-element.14.rest_0_, bf16[8,4096]{1,0:T(8,128)(2,1)S(1)} %collective-permute-done.rest_1_, ...), custom_call_target="tpu_custom_call" | custom-call | tf_op jit(solution)/shard_map/precondition/pallas_call | solution.py:221
  19.9 1.5 %collective-permute-start.9 = (bf16[32,512]{1,0:T(8,128)(2,1)S(1)}, bf16[32,512]{1,0:T(8,128)(2,1)S(1)}, u32[]{:S(2)}, u32[]{:S(2)}) collective-permute-start(bf16[32,512]{1,0:T(8,128)(2,1)S(1)} %precondition.1.rest_0_), channel_id=1, source_target_pairs={{0,6},{1,7},{2,4},{3,5},{4,2},{5,3},{6,0},{7,1},{8,14},{9,15},{10,... | collective-permute-start | bytes 98312 | tf_op jit(solution)/shard_map/ppermute | solution.py:284
  21.4 0.6 %collective-permute-start.8 = (bf16[32,512]{1,0:T(8,128)(2,1)S(1)}, bf16[32,512]{1,0:T(8,128)(2,1)S(1)}, u32[]{:S(2)}, u32[]{:S(2)}) collective-permute-start(bf16[32,512]{1,0:T(8,128)(2,1)S(1)} %precondition.1.rest_0_), channel_id=1, source_target_pairs={{0,4},{1,5},{2,6},{3,7},{4,0},{5,1},{6,2},{7,3},{8,12},{9,13},{10,... | collective-permute-start | bytes 98312 | tf_op jit(solution)/shard_map/ppermute | solution.py:284
  22.0 1.4 %collective-permute-start.7 = (bf16[32,512]{1,0:T(8,128)(2,1)S(1)}, bf16[32,512]{1,0:T(8,128)(2,1)S(1)}, u32[]{:S(2)}, u32[]{:S(2)}) collective-permute-start(bf16[32,512]{1,0:T(8,128)(2,1)S(1)} %precondition.1.rest_0_), channel_id=1, source_target_pairs={{0,2},{1,3},{2,0},{3,1},{4,6},{5,7},{6,4},{7,5},{8,10},{9,11},{10,... | collective-permute-start | bytes 98312 | tf_op jit(solution)/shard_map/ppermute | solution.py:284
  23.4 1.3 %collective-permute-done.9.rest_3_ = bf16[32,512]{1,0:T(8,128)(2,1)S(1)} collective-permute-done((bf16[32,512]{1,0:T(8,128)(2,1)S(1)}, bf16[32,512]{1,0:T(8,128)(2,1)S(1)}, u32[]{:S(2)}, u32[]{:S(2)}) %collective-permute-start.9) | collective-permute-done | bytes 32800 | tf_op jit(solution)/shard_map/ppermute | solution.py:284
  24.7 0.6 %collective-permute-done.8.rest_2_ = bf16[32,512]{1,0:T(8,128)(2,1)S(1)} collective-permute-done((bf16[32,512]{1,0:T(8,128)(2,1)S(1)}, bf16[32,512]{1,0:T(8,128)(2,1)S(1)}, u32[]{:S(2)}, u32[]{:S(2)}) %collective-permute-start.8) | collective-permute-done | bytes 32800 | tf_op jit(solution)/shard_map/ppermute | solution.py:284
  25.3 0.6 %collective-permute-done.7.rest_1_ = bf16[32,512]{1,0:T(8,128)(2,1)S(1)} collective-permute-done((bf16[32,512]{1,0:T(8,128)(2,1)S(1)}, bf16[32,512]{1,0:T(8,128)(2,1)S(1)}, u32[]{:S(2)}, u32[]{:S(2)}) %collective-permute-start.7) | collective-permute-done | bytes 32800 | tf_op jit(solution)/shard_map/ppermute | solution.py:284
  25.9 1.0 %early_score.1.early_ref = f32[768,32]{1,0:T(8,128)S(1)} custom-call(bf16[768,4096]{1,0:T(8,128)(2,1)S(1)} %bitcast.8, bf16[32,512]{1,0:T(8,128)(2,1)S(1)} %precondition.1.rest_0_, bf16[32,512]{1,0:T(8,128)(2,1)S(1)} %collective-permute-done.7.rest_1_, bf16[32,512]{1,0:T(8,128)(2,1)S(1)} %collective-permute-done.8.rest_2_, ...), custom_call_target="tpu_custom_call" | custom-call | tf_op jit(solution)/shard_map/early_score/pallas_call | solution.py:262
  26.9 0.2 collective-permute-done.11.rest_1_
  27.1 1.0 %score.1 = (f32[8,768]{1,0:T(8,128)S(1)}, f32[8,768]{1,0:T(8,128)S(1)}, f32[8,768]{1,0:T(8,128)S(1)}, f32[8,768]{1,0:T(8,128)S(1)}) custom-call(f32[768,32]{1,0:T(8,128)S(1)} %early_score.1.early_ref, bf16[768,4096]{1,0:T(8,128)(2,1)S(1)} %bitcast.9, bf16[32,512]{1,0:T(8,128)(2,1)S(1)} %collective-permute-done.10.rest_0_, ...), custom_call_target="tpu_custom_call" | custom-call | tf_op jit(solution)/shard_map/score/pallas_call | solution.py:271
  28.1 1.6 %collective-permute-start.14 = (f32[8,768]{1,0:T(8,128)S(1)}, f32[8,768]{1,0:T(8,128)S(1)}, u32[]{:S(2)}, u32[]{:S(2)}) collective-permute-start(f32[8,768]{1,0:T(8,128)S(1)} %get-tuple-element.16), channel_id=1, source_target_pairs={{0,8},{8,24},{24,16},{16,0},{1,9},{9,25},{25,17},{17,1},{2,10},{10... | collective-permute-start | bytes 73736 | tf_op jit(solution)/shard_map/ppermute | solution.py:290
  29.7 2.5 %collective-permute-start.15 = (f32[8,768]{1,0:T(8,128)S(1)}, f32[8,768]{1,0:T(8,128)S(1)}, u32[]{:S(2)}, u32[]{:S(2)}) collective-permute-start(f32[8,768]{1,0:T(8,128)S(1)} %get-tuple-element.17), channel_id=1, source_target_pairs={{0,24},{8,16},{24,0},{16,8},{1,25},{9,17},{25,1},{17,9},{2,26},{10... | collective-permute-start | bytes 73736 | tf_op jit(solution)/shard_map/ppermute | solution.py:290
  32.2 1.6 %collective-permute-start.16 = (f32[8,768]{1,0:T(8,128)S(1)}, f32[8,768]{1,0:T(8,128)S(1)}, u32[]{:S(2)}, u32[]{:S(2)}) collective-permute-start(f32[8,768]{1,0:T(8,128)S(1)} %get-tuple-element.18), channel_id=1, source_target_pairs={{0,16},{8,0},{24,8},{16,24},{1,17},{9,1},{25,9},{17,25},{2,18},{10... | collective-permute-start | bytes 73736 | tf_op jit(solution)/shard_map/ppermute | solution.py:290
  33.8 1.6 %collective-permute-done.15 = f32[8,768]{1,0:T(8,128)S(1)} collective-permute-done((f32[8,768]{1,0:T(8,128)S(1)}, f32[8,768]{1,0:T(8,128)S(1)}, u32[]{:S(2)}, u32[]{:S(2)}) %collective-permute-start.15) | collective-permute-done | bytes 24608 | tf_op jit(solution)/shard_map/ppermute | solution.py:290
  35.4 0.6 %collective-permute-done.16 = f32[8,768]{1,0:T(8,128)S(1)} collective-permute-done((f32[8,768]{1,0:T(8,128)S(1)}, f32[8,768]{1,0:T(8,128)S(1)}, u32[]{:S(2)}, u32[]{:S(2)}) %collective-permute-start.16) | collective-permute-done | bytes 24608 | tf_op jit(solution)/shard_map/ppermute | solution.py:290
  36.0 0.6 %add_add_fusion = f32[8,768]{1,0:T(8,128)} fusion(f32[8,768]{1,0:T(8,128)S(1)} %collective-permute-done.16, f32[8,768]{1,0:T(8,128)S(1)} %collective-permute-done.15, f32[8,768]{1,0:T(8,128)S(1)} %get-tuple-element.15, f32[8,768]{1,0:T(8,128)S(1)} %collective-permute-done.14), kind=kLoop, calls=%fused_computation | loop fusion | flops 18432 | bytes 122880 | tf_op jit(solution)/shard_map/add | solution.py:335
  (20 shorter events, 0.2 us)
Async XLA Ops:
  0.0 25.9 %slice-start = ((s8[6291456]{0:T(1024)(128)(4,1)}), s8[4194304]{0:T(1024)(128)(4,1)S(1)}, s32[]{:S(2)}) async-start(s8[6291456]{0:T(1024)(128)(4,1)} %bitcast.6), calls=%async_computation | async-start | bytes 8388608
  0.0 25.9 %slice-start.1 = ((s8[6291456]{0:T(1024)(128)(4,1)}), s8[2097152]{0:T(1024)(128)(4,1)S(1)}, s32[]{:S(2)}) async-start(s8[6291456]{0:T(1024)(128)(4,1)} %bitcast.6), calls=%async_computation.1 | async-start | bytes 4194304
  8.4 6.2 %collective-permute-start.5 = (bf16[8,4096]{1,0:T(8,128)(2,1)S(1)}, bf16[8,4096]{1,0:T(8,128)(2,1)S(1)}, u32[]{:S(2)}, u32[]{:S(2)}) collective-permute-start(bf16[8,4096]{1,0:T(8,128)(2,1)S(1)} %get-tuple-element.14.rest_0_), channel_id=1, source_target_pairs={{0,6},{1,7},{2,4},{3,5},{4,2},{5,3},{6,0},{7,1},{8,14},{9,15},{10,... | collective-permute-start | bytes 196616 | tf_op jit(solution)/shard_map/ppermute | solution.py:284
  12.4 4.3 %collective-permute-start.3 = (bf16[8,4096]{1,0:T(8,128)(2,1)S(1)}, bf16[8,4096]{1,0:T(8,128)(2,1)S(1)}, u32[]{:S(2)}, u32[]{:S(2)}) collective-permute-start(bf16[8,4096]{1,0:T(8,128)(2,1)S(1)} %get-tuple-element.14.rest_0_), channel_id=1, source_target_pairs={{0,4},{1,5},{2,6},{3,7},{4,0},{5,1},{6,2},{7,3},{8,12},{9,13},{10,... | collective-permute-start | bytes 196616 | tf_op jit(solution)/shard_map/ppermute | solution.py:284
  12.9 4.3 %collective-permute-start.1 = (bf16[8,4096]{1,0:T(8,128)(2,1)S(1)}, bf16[8,4096]{1,0:T(8,128)(2,1)S(1)}, u32[]{:S(2)}, u32[]{:S(2)}) collective-permute-start(bf16[8,4096]{1,0:T(8,128)(2,1)S(1)} %get-tuple-element.14.rest_0_), channel_id=1, source_target_pairs={{0,2},{1,3},{2,0},{3,1},{4,6},{5,7},{6,4},{7,5},{8,10},{9,11},{10,... | collective-permute-start | bytes 196616 | tf_op jit(solution)/shard_map/ppermute | solution.py:284
  13.0 4.1 %collective-permute-start = (bf16[8,4096]{1,0:T(8,128)(2,1)S(1)}, bf16[8,4096]{1,0:T(8,128)(2,1)S(1)}, u32[]{:S(2)}, u32[]{:S(2)}) collective-permute-start(bf16[8,4096]{1,0:T(8,128)(2,1)S(1)} %get-tuple-element.14.rest_0_), channel_id=1, source_target_pairs={{0,1},{1,0},{2,3},{3,2},{4,5},{5,4},{6,7},{7,6},{8,9},{9,8},{10,11... | collective-permute-start | bytes 196616 | tf_op jit(solution)/shard_map/ppermute | solution.py:284
  14.7 2.5 %collective-permute-start.6 = (bf16[8,4096]{1,0:T(8,128)(2,1)S(1)}, bf16[8,4096]{1,0:T(8,128)(2,1)S(1)}, u32[]{:S(2)}, u32[]{:S(2)}) collective-permute-start(bf16[8,4096]{1,0:T(8,128)(2,1)S(1)} %collective-permute-done.5.rest_6_), channel_id=1, source_target_pairs={{0,1},{1,0},{2,3},{3,2},{4,5},{5,4},{6,7},{7,6},{8,9},{9,8},{10,11... | collective-permute-start | bytes 196616 | tf_op jit(solution)/shard_map/ppermute | solution.py:284
  16.7 1.3 %collective-permute-start.4 = (bf16[8,4096]{1,0:T(8,128)(2,1)S(1)}, bf16[8,4096]{1,0:T(8,128)(2,1)S(1)}, u32[]{:S(2)}, u32[]{:S(2)}) collective-permute-start(bf16[8,4096]{1,0:T(8,128)(2,1)S(1)} %collective-permute-done.3.rest_4_), channel_id=1, source_target_pairs={{0,1},{1,0},{2,3},{3,2},{4,5},{5,4},{6,7},{7,6},{8,9},{9,8},{10,11... | collective-permute-start | bytes 196616 | tf_op jit(solution)/shard_map/ppermute | solution.py:284
  17.2 1.3 %collective-permute-start.2 = (bf16[8,4096]{1,0:T(8,128)(2,1)S(1)}, bf16[8,4096]{1,0:T(8,128)(2,1)S(1)}, u32[]{:S(2)}, u32[]{:S(2)}) collective-permute-start(bf16[8,4096]{1,0:T(8,128)(2,1)S(1)} %collective-permute-done.1.rest_2_), channel_id=1, source_target_pairs={{0,1},{1,0},{2,3},{3,2},{4,5},{5,4},{6,7},{7,6},{8,9},{9,8},{10,11... | collective-permute-start | bytes 196616 | tf_op jit(solution)/shard_map/ppermute | solution.py:284
  19.9 4.8 %collective-permute-start.9 = (bf16[32,512]{1,0:T(8,128)(2,1)S(1)}, bf16[32,512]{1,0:T(8,128)(2,1)S(1)}, u32[]{:S(2)}, u32[]{:S(2)}) collective-permute-start(bf16[32,512]{1,0:T(8,128)(2,1)S(1)} %precondition.1.rest_0_), channel_id=1, source_target_pairs={{0,6},{1,7},{2,4},{3,5},{4,2},{5,3},{6,0},{7,1},{8,14},{9,15},{10,... | collective-permute-start | bytes 98312 | tf_op jit(solution)/shard_map/ppermute | solution.py:284
  21.4 3.9 %collective-permute-start.8 = (bf16[32,512]{1,0:T(8,128)(2,1)S(1)}, bf16[32,512]{1,0:T(8,128)(2,1)S(1)}, u32[]{:S(2)}, u32[]{:S(2)}) collective-permute-start(bf16[32,512]{1,0:T(8,128)(2,1)S(1)} %precondition.1.rest_0_), channel_id=1, source_target_pairs={{0,4},{1,5},{2,6},{3,7},{4,0},{5,1},{6,2},{7,3},{8,12},{9,13},{10,... | collective-permute-start | bytes 98312 | tf_op jit(solution)/shard_map/ppermute | solution.py:284
  22.0 3.9 %collective-permute-start.7 = (bf16[32,512]{1,0:T(8,128)(2,1)S(1)}, bf16[32,512]{1,0:T(8,128)(2,1)S(1)}, u32[]{:S(2)}, u32[]{:S(2)}) collective-permute-start(bf16[32,512]{1,0:T(8,128)(2,1)S(1)} %precondition.1.rest_0_), channel_id=1, source_target_pairs={{0,2},{1,3},{2,0},{3,1},{4,6},{5,7},{6,4},{7,5},{8,10},{9,11},{10,... | collective-permute-start | bytes 98312 | tf_op jit(solution)/shard_map/ppermute | solution.py:284
  23.4 3.5 %collective-permute-start.10 = (bf16[32,512]{1,0:T(8,128)(2,1)S(1)}, bf16[32,512]{1,0:T(8,128)(2,1)S(1)}, u32[]{:S(2)}, u32[]{:S(2)}) collective-permute-start(bf16[32,512]{1,0:T(8,128)(2,1)S(1)} %precondition.1.rest_0_), channel_id=1, source_target_pairs={{0,1},{1,0},{2,3},{3,2},{4,5},{5,4},{6,7},{7,6},{8,9},{9,8},{10,11... | collective-permute-start | bytes 98312 | tf_op jit(solution)/shard_map/ppermute | solution.py:284
  24.7 2.1 %collective-permute-start.13 = (bf16[32,512]{1,0:T(8,128)(2,1)S(1)}, bf16[32,512]{1,0:T(8,128)(2,1)S(1)}, u32[]{:S(2)}, u32[]{:S(2)}) collective-permute-start(bf16[32,512]{1,0:T(8,128)(2,1)S(1)} %collective-permute-done.9.rest_3_), channel_id=1, source_target_pairs={{0,1},{1,0},{2,3},{3,2},{4,5},{5,4},{6,7},{7,6},{8,9},{9,8},{10,11... | collective-permute-start | bytes 98312 | tf_op jit(solution)/shard_map/ppermute | solution.py:284
  25.3 1.6 %collective-permute-start.12 = (bf16[32,512]{1,0:T(8,128)(2,1)S(1)}, bf16[32,512]{1,0:T(8,128)(2,1)S(1)}, u32[]{:S(2)}, u32[]{:S(2)}) collective-permute-start(bf16[32,512]{1,0:T(8,128)(2,1)S(1)} %collective-permute-done.8.rest_2_), channel_id=1, source_target_pairs={{0,1},{1,0},{2,3},{3,2},{4,5},{5,4},{6,7},{7,6},{8,9},{9,8},{10,11... | collective-permute-start | bytes 98312 | tf_op jit(solution)/shard_map/ppermute | solution.py:284
  25.9 1.2 %collective-permute-start.11 = (bf16[32,512]{1,0:T(8,128)(2,1)S(1)}, bf16[32,512]{1,0:T(8,128)(2,1)S(1)}, u32[]{:S(2)}, u32[]{:S(2)}) collective-permute-start(bf16[32,512]{1,0:T(8,128)(2,1)S(1)} %collective-permute-done.7.rest_1_), channel_id=1, source_target_pairs={{0,1},{1,0},{2,3},{3,2},{4,5},{5,4},{6,7},{7,6},{8,9},{9,8},{10,11... | collective-permute-start | bytes 98312 | tf_op jit(solution)/shard_map/ppermute | solution.py:284
  28.1 5.7 %collective-permute-start.14 = (f32[8,768]{1,0:T(8,128)S(1)}, f32[8,768]{1,0:T(8,128)S(1)}, u32[]{:S(2)}, u32[]{:S(2)}) collective-permute-start(f32[8,768]{1,0:T(8,128)S(1)} %get-tuple-element.16), channel_id=1, source_target_pairs={{0,8},{8,24},{24,16},{16,0},{1,9},{9,25},{25,17},{17,1},{2,10},{10... | collective-permute-start | bytes 73736 | tf_op jit(solution)/shard_map/ppermute | solution.py:290
  29.7 5.7 %collective-permute-start.15 = (f32[8,768]{1,0:T(8,128)S(1)}, f32[8,768]{1,0:T(8,128)S(1)}, u32[]{:S(2)}, u32[]{:S(2)}) collective-permute-start(f32[8,768]{1,0:T(8,128)S(1)} %get-tuple-element.17), channel_id=1, source_target_pairs={{0,24},{8,16},{24,0},{16,8},{1,25},{9,17},{25,1},{17,9},{2,26},{10... | collective-permute-start | bytes 73736 | tf_op jit(solution)/shard_map/ppermute | solution.py:290
  32.2 3.8 %collective-permute-start.16 = (f32[8,768]{1,0:T(8,128)S(1)}, f32[8,768]{1,0:T(8,128)S(1)}, u32[]{:S(2)}, u32[]{:S(2)}) collective-permute-start(f32[8,768]{1,0:T(8,128)S(1)} %get-tuple-element.18), channel_id=1, source_target_pairs={{0,16},{8,0},{24,8},{16,24},{1,17},{9,1},{25,9},{17,25},{2,18},{10... | collective-permute-start | bytes 73736 | tf_op jit(solution)/shard_map/ppermute | solution.py:290

commit v8 on v7

--- a/solution.py
+++ b/solution.py
@@ -34,10 +34,6 @@
 
 def dot(left, right):
     return jnp.dot(left, right, preferred_element_type=jnp.float32)
-
-
-def chunks_of(units):
-    return [(first, min(2, units - first)) for first in range(0, units, 2)]
 
 
 def featurize_kernel(
@@ -72,11 +68,11 @@
     capacity = feature_ref.shape[0]
     queries, slots = placer_ref.shape
     unit = tokens // capacity
-    chunks = chunks_of(capacity)
+    chunks = act_sems.shape[0]
+    size = tokens // chunks
 
     def copies(index):
-        first, size = chunks[index]
-        rows = pl.ds(first * unit, size * unit)
+        rows = pl.ds(pl.multiple_of(index * size, size), size)
         return (
             pltpu.make_async_copy(act_hbm.at[rows], act.at[rows], act_sems.at[index]),
             pltpu.make_async_copy(grad_hbm.at[rows], grad.at[rows], grad_sems.at[index]),
@@ -95,7 +91,7 @@
     ]
     for copy in first_copies:
         copy.start()
-    for index in range(len(chunks)):
+    for index in range(chunks):
         for copy in copies(index):
             copy.start()
 
@@ -133,28 +129,30 @@
 
     for copy in first_copies[:2]:
         copy.wait()
-    for index, (first, size) in enumerate(chunks):
+    @pl.loop(0, chunks)
+    def _(index):
         for copy in copies(index):
             copy.wait()
-        rows = pl.ds(first * unit, size * unit)
-        padded = pl.ds((first + 1) * unit, size * unit)
+        rows = pl.ds(pl.multiple_of(index * size, size), size)
+        padded = pl.ds(pl.multiple_of(index * size + unit, unit), size)
         in_feat[padded, :] = contract_last(act[rows, :], in_proj[...])
         out_feat[:, padded] = contract_last(grad[rows, :], out_proj[...]).T
-    for slot in range(capacity):
+
+    @pl.loop(0, capacity, unroll=capacity)
+    def _(slot):
         start, stop = starts[slot], stops[slot]
         window = jnp.maximum((stop + unit - 1) // unit - 1, 0) * unit
         window = pl.multiple_of(window, unit)
-        position = (
-            window - unit + lax.broadcasted_iota(jnp.int32, (rank, 2 * unit), 1)
-        )
+        position = window - unit + lax.broadcasted_iota(jnp.int32, (rank, 2 * unit), 1)
         member = (position >= start) & (position < stop)
         out_high, out_low = split_two(
             jnp.where(member, out_feat[:, pl.ds(window, 2 * unit)], 0.0)
         )
         in_high, in_low = split_two(in_feat[pl.ds(window, 2 * unit), :])
-        total[pl.ds(slot * rank, rank), :] = (
+        total[pl.ds(pl.multiple_of(slot * rank, rank), rank), :] = (
             dot(out_high, in_high) + dot(out_high, in_low) + dot(out_low, in_high)
         )
+
     for first in range(0, rank, 2):
         pair = [
             total[pl.ds(first + k, capacity, stride=rank), :] for k in range(2)
@@ -172,7 +170,7 @@
     rank = in_projection.shape[0]
     queries = lengths.shape[0]
     unit = tokens // capacity
-    chunks = len(chunks_of(capacity))
+    chunks = max(capacity // 2, 1)
     return pl.pallas_call(
         featurize_kernel,
         in_specs=[pl.BlockSpec(memory_space=pl.ANY)] * 7,
@@ -212,7 +210,7 @@
         feature[pl.ds(place * capacity, 2 * capacity), :] = jnp.concatenate(
             both, axis=0
         ).astype(jnp.bfloat16)
-    by_slot = contract_last(feature[...], curvature_ref[...]).astype(jnp.bfloat16)
+    by_slot = contract_last(curvature_ref[...], feature[...]).T.astype(jnp.bfloat16)
     out_ref[...] = dot(placer_ref[...].astype(jnp.bfloat16), by_slot).astype(jnp.bfloat16)
 
 

time: 36.8 us -> 36.8 us (level)
  no operation moved by 1% of the time
where the time goes in v8:
time: 36.8 us; the launch traced here: 36.7 us
  starting transfers between devices  13.8 us (38%)
  Pallas kernels  11.8 us (32%)
  waiting for transfers between devices  10.3 us (28%)
  other arithmetic  0.62 us (2%)
    pallas_call x1, Pallas kernels, featurize(): pl.pallas_call(featurize_kernel, in_specs=[pl.BlockSpec(memory_space=pl.A...  8.42 us
    ppermute x14, starting transfers between devices, exchange(): return lax.ppermute(array, axis, [(i, i ^ distance) for i in range(count)])  8.18 us
    ppermute x14, waiting for transfers between devices, exchange(): return lax.ppermute(array, axis, [(i, i ^ distance) for i in range(count)])  8.01 us
    ppermute x3, starting transfers between devices, send_on(): lax.ppermute(array, axis, [(order[i], order[(i + places) % count]) for i...  5.67 us
    ppermute x3, waiting for transfers between devices, send_on(): lax.ppermute(array, axis, [(order[i], order[(i + places) % count]) for i...  2.26 us
    pallas_call x1, Pallas kernels, precondition(): pl.pallas_call(precondition_kernel, in_specs=[pl.BlockSpec(memory_space=p...  1.45 us
    pallas_call x1, Pallas kernels, score(): pl.pallas_call(functools.partial(score_kernel, late_places, parts), in_sp...  1.01 us
    pallas_call x1, Pallas kernels, score(): pl.pallas_call(functools.partial(early_score_kernel, early_places), in_sp...  0.96 us
  transfers between devices with their start and end apart: 17, of which 11 were waited for; matrix products, arithmetic and copies ran while one was open for 0% of the time, Pallas kernels for 3%

profile of v8, /device:TPU:0, one launch (start us, length us, event | category | flops | bytes accessed | tf_op | source)
XLA Modules:
  0.0 36.7 jit_solution(13982503200527960787)
XLA Ops:
  0.0 8.4 %featurize.1 = (bf16[8,4096]{1,0:T(8,128)(2,1)S(1)}, f32[32,64]{1,0:T(8,128)S(1)}, bf16[512,4096]{1,0:T(8,128)(2,1)S(1)}) custom-call(s32[32]{0:T(128)} %lengths_hbm.1, s32[32]{0:T(128)} %owners_hbm.1, bf16[512,4096]{1,0:T(8,128)(2,1)} %bitcast.12, bf16[1024,4096]{1,0:T(8,128)(2,1)} %bitcast.10, bf16[1024,4096]{1,0:T(8,128)(2,1)} %bitcast.11, ...), custom_call_target="tpu_custom_call" | custom-call | tf_op jit(solution)/shard_map/featurize/pallas_call | solution.py:174
  8.4 4.0 %collective-permute-start.5 = (bf16[8,4096]{1,0:T(8,128)(2,1)S(1)}, bf16[8,4096]{1,0:T(8,128)(2,1)S(1)}, u32[]{:S(2)}, u32[]{:S(2)}) collective-permute-start(bf16[8,4096]{1,0:T(8,128)(2,1)S(1)} %get-tuple-element.14.rest_0_), channel_id=1, source_target_pairs={{0,6},{1,7},{2,4},{3,5},{4,2},{5,3},{6,0},{7,1},{8,14},{9,15},{10,... | collective-permute-start | bytes 196616 | tf_op jit(solution)/shard_map/ppermute | solution.py:282
  12.4 0.5 %collective-permute-start.3 = (bf16[8,4096]{1,0:T(8,128)(2,1)S(1)}, bf16[8,4096]{1,0:T(8,128)(2,1)S(1)}, u32[]{:S(2)}, u32[]{:S(2)}) collective-permute-start(bf16[8,4096]{1,0:T(8,128)(2,1)S(1)} %get-tuple-element.14.rest_0_), channel_id=1, source_target_pairs={{0,4},{1,5},{2,6},{3,7},{4,0},{5,1},{6,2},{7,3},{8,12},{9,13},{10,... | collective-permute-start | bytes 196616 | tf_op jit(solution)/shard_map/ppermute | solution.py:282
  13.0 1.6 %collective-permute-done.5.rest_6_ = bf16[8,4096]{1,0:T(8,128)(2,1)S(1)} collective-permute-done((bf16[8,4096]{1,0:T(8,128)(2,1)S(1)}, bf16[8,4096]{1,0:T(8,128)(2,1)S(1)}, u32[]{:S(2)}, u32[]{:S(2)}) %collective-permute-start.5) | collective-permute-done | bytes 65568 | tf_op jit(solution)/shard_map/ppermute | solution.py:282
  14.6 2.0 %collective-permute-done.3.rest_4_ = bf16[8,4096]{1,0:T(8,128)(2,1)S(1)} collective-permute-done((bf16[8,4096]{1,0:T(8,128)(2,1)S(1)}, bf16[8,4096]{1,0:T(8,128)(2,1)S(1)}, u32[]{:S(2)}, u32[]{:S(2)}) %collective-permute-start.3) | collective-permute-done | bytes 65568 | tf_op jit(solution)/shard_map/ppermute | solution.py:282
  16.7 0.5 %collective-permute-done.1.rest_2_ = bf16[8,4096]{1,0:T(8,128)(2,1)S(1)} collective-permute-done((bf16[8,4096]{1,0:T(8,128)(2,1)S(1)}, bf16[8,4096]{1,0:T(8,128)(2,1)S(1)}, u32[]{:S(2)}, u32[]{:S(2)}) %collective-permute-start.1) | collective-permute-done | bytes 65568 | tf_op jit(solution)/shard_map/ppermute | solution.py:282
  17.2 0.7 %collective-permute-done.4.rest_5_ = bf16[8,4096]{1,0:T(8,128)(2,1)S(1)} collective-permute-done((bf16[8,4096]{1,0:T(8,128)(2,1)S(1)}, bf16[8,4096]{1,0:T(8,128)(2,1)S(1)}, u32[]{:S(2)}, u32[]{:S(2)}) %collective-permute-start.4) | collective-permute-done | bytes 65568 | tf_op jit(solution)/shard_map/ppermute | solution.py:282
  17.9 0.5 %collective-permute-done.2.rest_3_ = bf16[8,4096]{1,0:T(8,128)(2,1)S(1)} collective-permute-done((bf16[8,4096]{1,0:T(8,128)(2,1)S(1)}, bf16[8,4096]{1,0:T(8,128)(2,1)S(1)}, u32[]{:S(2)}, u32[]{:S(2)}) %collective-permute-start.2) | collective-permute-done | bytes 65568 | tf_op jit(solution)/shard_map/ppermute | solution.py:282
  18.4 1.4 %precondition.1.rest_0_ = bf16[32,512]{1,0:T(8,128)(2,1)S(1)} custom-call(bf16[512,4096]{1,0:T(8,128)(2,1)S(1)} %get-tuple-element.12.curvature_ref, f32[32,64]{1,0:T(8,128)S(1)} %get-tuple-element.13.placer_ref, bf16[8,4096]{1,0:T(8,128)(2,1)S(1)} %get-tuple-element.14.rest_0_, bf16[8,4096]{1,0:T(8,128)(2,1)S(1)} %collective-permute-done.rest_1_, ...), custom_call_target="tpu_custom_call" | custom-call | tf_op jit(solution)/shard_map/precondition/pallas_call | solution.py:219
  19.9 1.5 %collective-permute-start.9 = (bf16[32,512]{1,0:T(8,128)(2,1)S(1)}, bf16[32,512]{1,0:T(8,128)(2,1)S(1)}, u32[]{:S(2)}, u32[]{:S(2)}) collective-permute-start(bf16[32,512]{1,0:T(8,128)(2,1)S(1)} %precondition.1.rest_0_), channel_id=1, source_target_pairs={{0,6},{1,7},{2,4},{3,5},{4,2},{5,3},{6,0},{7,1},{8,14},{9,15},{10,... | collective-permute-start | bytes 98312 | tf_op jit(solution)/shard_map/ppermute | solution.py:282
  21.4 0.5 %collective-permute-start.8 = (bf16[32,512]{1,0:T(8,128)(2,1)S(1)}, bf16[32,512]{1,0:T(8,128)(2,1)S(1)}, u32[]{:S(2)}, u32[]{:S(2)}) collective-permute-start(bf16[32,512]{1,0:T(8,128)(2,1)S(1)} %precondition.1.rest_0_), channel_id=1, source_target_pairs={{0,4},{1,5},{2,6},{3,7},{4,0},{5,1},{6,2},{7,3},{8,12},{9,13},{10,... | collective-permute-start | bytes 98312 | tf_op jit(solution)/shard_map/ppermute | solution.py:282
  22.0 1.5 %collective-permute-start.7 = (bf16[32,512]{1,0:T(8,128)(2,1)S(1)}, bf16[32,512]{1,0:T(8,128)(2,1)S(1)}, u32[]{:S(2)}, u32[]{:S(2)}) collective-permute-start(bf16[32,512]{1,0:T(8,128)(2,1)S(1)} %precondition.1.rest_0_), channel_id=1, source_target_pairs={{0,2},{1,3},{2,0},{3,1},{4,6},{5,7},{6,4},{7,5},{8,10},{9,11},{10,... | collective-permute-start | bytes 98312 | tf_op jit(solution)/shard_map/ppermute | solution.py:282
  23.5 1.3 %collective-permute-done.9.rest_3_ = bf16[32,512]{1,0:T(8,128)(2,1)S(1)} collective-permute-done((bf16[32,512]{1,0:T(8,128)(2,1)S(1)}, bf16[32,512]{1,0:T(8,128)(2,1)S(1)}, u32[]{:S(2)}, u32[]{:S(2)}) %collective-permute-start.9) | collective-permute-done | bytes 32800 | tf_op jit(solution)/shard_map/ppermute | solution.py:282
  24.8 0.6 %collective-permute-done.8.rest_2_ = bf16[32,512]{1,0:T(8,128)(2,1)S(1)} collective-permute-done((bf16[32,512]{1,0:T(8,128)(2,1)S(1)}, bf16[32,512]{1,0:T(8,128)(2,1)S(1)}, u32[]{:S(2)}, u32[]{:S(2)}) %collective-permute-start.8) | collective-permute-done | bytes 32800 | tf_op jit(solution)/shard_map/ppermute | solution.py:282
  25.4 0.5 %collective-permute-done.7.rest_1_ = bf16[32,512]{1,0:T(8,128)(2,1)S(1)} collective-permute-done((bf16[32,512]{1,0:T(8,128)(2,1)S(1)}, bf16[32,512]{1,0:T(8,128)(2,1)S(1)}, u32[]{:S(2)}, u32[]{:S(2)}) %collective-permute-start.7) | collective-permute-done | bytes 32800 | tf_op jit(solution)/shard_map/ppermute | solution.py:282
  25.9 1.0 %early_score.1.early_ref = f32[768,32]{1,0:T(8,128)S(1)} custom-call(bf16[768,4096]{1,0:T(8,128)(2,1)S(1)} %bitcast.8, bf16[32,512]{1,0:T(8,128)(2,1)S(1)} %precondition.1.rest_0_, bf16[32,512]{1,0:T(8,128)(2,1)S(1)} %collective-permute-done.7.rest_1_, bf16[32,512]{1,0:T(8,128)(2,1)S(1)} %collective-permute-done.8.rest_2_, ...), custom_call_target="tpu_custom_call" | custom-call | tf_op jit(solution)/shard_map/early_score/pallas_call | solution.py:260
  26.9 0.2 collective-permute-done.11.rest_1_
  27.1 1.0 %score.1 = (f32[8,768]{1,0:T(8,128)S(1)}, f32[8,768]{1,0:T(8,128)S(1)}, f32[8,768]{1,0:T(8,128)S(1)}, f32[8,768]{1,0:T(8,128)S(1)}) custom-call(f32[768,32]{1,0:T(8,128)S(1)} %early_score.1.early_ref, bf16[768,4096]{1,0:T(8,128)(2,1)S(1)} %bitcast.9, bf16[32,512]{1,0:T(8,128)(2,1)S(1)} %collective-permute-done.10.rest_0_, ...), custom_call_target="tpu_custom_call" | custom-call | tf_op jit(solution)/shard_map/score/pallas_call | solution.py:269
  28.1 1.6 %collective-permute-start.14 = (f32[8,768]{1,0:T(8,128)S(1)}, f32[8,768]{1,0:T(8,128)S(1)}, u32[]{:S(2)}, u32[]{:S(2)}) collective-permute-start(f32[8,768]{1,0:T(8,128)S(1)} %get-tuple-element.16), channel_id=1, source_target_pairs={{0,8},{8,24},{24,16},{16,0},{1,9},{9,25},{25,17},{17,1},{2,10},{10... | collective-permute-start | bytes 73736 | tf_op jit(solution)/shard_map/ppermute | solution.py:288
  29.8 2.5 %collective-permute-start.15 = (f32[8,768]{1,0:T(8,128)S(1)}, f32[8,768]{1,0:T(8,128)S(1)}, u32[]{:S(2)}, u32[]{:S(2)}) collective-permute-start(f32[8,768]{1,0:T(8,128)S(1)} %get-tuple-element.17), channel_id=1, source_target_pairs={{0,24},{8,16},{24,0},{16,8},{1,25},{9,17},{25,1},{17,9},{2,26},{10... | collective-permute-start | bytes 73736 | tf_op jit(solution)/shard_map/ppermute | solution.py:288
  32.2 1.6 %collective-permute-start.16 = (f32[8,768]{1,0:T(8,128)S(1)}, f32[8,768]{1,0:T(8,128)S(1)}, u32[]{:S(2)}, u32[]{:S(2)}) collective-permute-start(f32[8,768]{1,0:T(8,128)S(1)} %get-tuple-element.18), channel_id=1, source_target_pairs={{0,16},{8,0},{24,8},{16,24},{1,17},{9,1},{25,9},{17,25},{2,18},{10... | collective-permute-start | bytes 73736 | tf_op jit(solution)/shard_map/ppermute | solution.py:288
  33.8 1.7 %collective-permute-done.15 = f32[8,768]{1,0:T(8,128)S(1)} collective-permute-done((f32[8,768]{1,0:T(8,128)S(1)}, f32[8,768]{1,0:T(8,128)S(1)}, u32[]{:S(2)}, u32[]{:S(2)}) %collective-permute-start.15) | collective-permute-done | bytes 24608 | tf_op jit(solution)/shard_map/ppermute | solution.py:288
  35.5 0.6 %collective-permute-done.16 = f32[8,768]{1,0:T(8,128)S(1)} collective-permute-done((f32[8,768]{1,0:T(8,128)S(1)}, f32[8,768]{1,0:T(8,128)S(1)}, u32[]{:S(2)}, u32[]{:S(2)}) %collective-permute-start.16) | collective-permute-done | bytes 24608 | tf_op jit(solution)/shard_map/ppermute | solution.py:288
  36.1 0.6 %add_add_fusion = f32[8,768]{1,0:T(8,128)} fusion(f32[8,768]{1,0:T(8,128)S(1)} %collective-permute-done.16, f32[8,768]{1,0:T(8,128)S(1)} %collective-permute-done.15, f32[8,768]{1,0:T(8,128)S(1)} %get-tuple-element.15, f32[8,768]{1,0:T(8,128)S(1)} %collective-permute-done.14), kind=kLoop, calls=%fused_computation | loop fusion | flops 18432 | bytes 122880 | tf_op jit(solution)/shard_map/add | solution.py:333
  (20 shorter events, 0.2 us)
Async XLA Ops:
  0.0 25.9 %slice-start = ((s8[6291456]{0:T(1024)(128)(4,1)}), s8[4194304]{0:T(1024)(128)(4,1)S(1)}, s32[]{:S(2)}) async-start(s8[6291456]{0:T(1024)(128)(4,1)} %bitcast.6), calls=%async_computation | async-start | bytes 8388608
  0.0 25.9 %slice-start.1 = ((s8[6291456]{0:T(1024)(128)(4,1)}), s8[2097152]{0:T(1024)(128)(4,1)S(1)}, s32[]{:S(2)}) async-start(s8[6291456]{0:T(1024)(128)(4,1)} %bitcast.6), calls=%async_computation.1 | async-start | bytes 4194304
  8.4 6.2 %collective-permute-start.5 = (bf16[8,4096]{1,0:T(8,128)(2,1)S(1)}, bf16[8,4096]{1,0:T(8,128)(2,1)S(1)}, u32[]{:S(2)}, u32[]{:S(2)}) collective-permute-start(bf16[8,4096]{1,0:T(8,128)(2,1)S(1)} %get-tuple-element.14.rest_0_), channel_id=1, source_target_pairs={{0,6},{1,7},{2,4},{3,5},{4,2},{5,3},{6,0},{7,1},{8,14},{9,15},{10,... | collective-permute-start | bytes 196616 | tf_op jit(solution)/shard_map/ppermute | solution.py:282
  12.4 4.3 %collective-permute-start.3 = (bf16[8,4096]{1,0:T(8,128)(2,1)S(1)}, bf16[8,4096]{1,0:T(8,128)(2,1)S(1)}, u32[]{:S(2)}, u32[]{:S(2)}) collective-permute-start(bf16[8,4096]{1,0:T(8,128)(2,1)S(1)} %get-tuple-element.14.rest_0_), channel_id=1, source_target_pairs={{0,4},{1,5},{2,6},{3,7},{4,0},{5,1},{6,2},{7,3},{8,12},{9,13},{10,... | collective-permute-start | bytes 196616 | tf_op jit(solution)/shard_map/ppermute | solution.py:282
  12.9 4.3 %collective-permute-start.1 = (bf16[8,4096]{1,0:T(8,128)(2,1)S(1)}, bf16[8,4096]{1,0:T(8,128)(2,1)S(1)}, u32[]{:S(2)}, u32[]{:S(2)}) collective-permute-start(bf16[8,4096]{1,0:T(8,128)(2,1)S(1)} %get-tuple-element.14.rest_0_), channel_id=1, source_target_pairs={{0,2},{1,3},{2,0},{3,1},{4,6},{5,7},{6,4},{7,5},{8,10},{9,11},{10,... | collective-permute-start | bytes 196616 | tf_op jit(solution)/shard_map/ppermute | solution.py:282
  13.0 4.2 %collective-permute-start = (bf16[8,4096]{1,0:T(8,128)(2,1)S(1)}, bf16[8,4096]{1,0:T(8,128)(2,1)S(1)}, u32[]{:S(2)}, u32[]{:S(2)}) collective-permute-start(bf16[8,4096]{1,0:T(8,128)(2,1)S(1)} %get-tuple-element.14.rest_0_), channel_id=1, source_target_pairs={{0,1},{1,0},{2,3},{3,2},{4,5},{5,4},{6,7},{7,6},{8,9},{9,8},{10,11... | collective-permute-start | bytes 196616 | tf_op jit(solution)/shard_map/ppermute | solution.py:282
  14.6 2.5 %collective-permute-start.6 = (bf16[8,4096]{1,0:T(8,128)(2,1)S(1)}, bf16[8,4096]{1,0:T(8,128)(2,1)S(1)}, u32[]{:S(2)}, u32[]{:S(2)}) collective-permute-start(bf16[8,4096]{1,0:T(8,128)(2,1)S(1)} %collective-permute-done.5.rest_6_), channel_id=1, source_target_pairs={{0,1},{1,0},{2,3},{3,2},{4,5},{5,4},{6,7},{7,6},{8,9},{9,8},{10,11... | collective-permute-start | bytes 196616 | tf_op jit(solution)/shard_map/ppermute | solution.py:282
  16.7 1.3 %collective-permute-start.4 = (bf16[8,4096]{1,0:T(8,128)(2,1)S(1)}, bf16[8,4096]{1,0:T(8,128)(2,1)S(1)}, u32[]{:S(2)}, u32[]{:S(2)}) collective-permute-start(bf16[8,4096]{1,0:T(8,128)(2,1)S(1)} %collective-permute-done.3.rest_4_), channel_id=1, source_target_pairs={{0,1},{1,0},{2,3},{3,2},{4,5},{5,4},{6,7},{7,6},{8,9},{9,8},{10,11... | collective-permute-start | bytes 196616 | tf_op jit(solution)/shard_map/ppermute | solution.py:282
  17.2 1.3 %collective-permute-start.2 = (bf16[8,4096]{1,0:T(8,128)(2,1)S(1)}, bf16[8,4096]{1,0:T(8,128)(2,1)S(1)}, u32[]{:S(2)}, u32[]{:S(2)}) collective-permute-start(bf16[8,4096]{1,0:T(8,128)(2,1)S(1)} %collective-permute-done.1.rest_2_), channel_id=1, source_target_pairs={{0,1},{1,0},{2,3},{3,2},{4,5},{5,4},{6,7},{7,6},{8,9},{9,8},{10,11... | collective-permute-start | bytes 196616 | tf_op jit(solution)/shard_map/ppermute | solution.py:282
  19.9 4.9 %collective-permute-start.9 = (bf16[32,512]{1,0:T(8,128)(2,1)S(1)}, bf16[32,512]{1,0:T(8,128)(2,1)S(1)}, u32[]{:S(2)}, u32[]{:S(2)}) collective-permute-start(bf16[32,512]{1,0:T(8,128)(2,1)S(1)} %precondition.1.rest_0_), channel_id=1, source_target_pairs={{0,6},{1,7},{2,4},{3,5},{4,2},{5,3},{6,0},{7,1},{8,14},{9,15},{10,... | collective-permute-start | bytes 98312 | tf_op jit(solution)/shard_map/ppermute | solution.py:282
  21.4 3.9 %collective-permute-start.8 = (bf16[32,512]{1,0:T(8,128)(2,1)S(1)}, bf16[32,512]{1,0:T(8,128)(2,1)S(1)}, u32[]{:S(2)}, u32[]{:S(2)}) collective-permute-start(bf16[32,512]{1,0:T(8,128)(2,1)S(1)} %precondition.1.rest_0_), channel_id=1, source_target_pairs={{0,4},{1,5},{2,6},{3,7},{4,0},{5,1},{6,2},{7,3},{8,12},{9,13},{10,... | collective-permute-start | bytes 98312 | tf_op jit(solution)/shard_map/ppermute | solution.py:282
  22.0 3.9 %collective-permute-start.7 = (bf16[32,512]{1,0:T(8,128)(2,1)S(1)}, bf16[32,512]{1,0:T(8,128)(2,1)S(1)}, u32[]{:S(2)}, u32[]{:S(2)}) collective-permute-start(bf16[32,512]{1,0:T(8,128)(2,1)S(1)} %precondition.1.rest_0_), channel_id=1, source_target_pairs={{0,2},{1,3},{2,0},{3,1},{4,6},{5,7},{6,4},{7,5},{8,10},{9,11},{10,... | collective-permute-start | bytes 98312 | tf_op jit(solution)/shard_map/ppermute | solution.py:282
  23.4 3.4 %collective-permute-start.10 = (bf16[32,512]{1,0:T(8,128)(2,1)S(1)}, bf16[32,512]{1,0:T(8,128)(2,1)S(1)}, u32[]{:S(2)}, u32[]{:S(2)}) collective-permute-start(bf16[32,512]{1,0:T(8,128)(2,1)S(1)} %precondition.1.rest_0_), channel_id=1, source_target_pairs={{0,1},{1,0},{2,3},{3,2},{4,5},{5,4},{6,7},{7,6},{8,9},{9,8},{10,11... | collective-permute-start | bytes 98312 | tf_op jit(solution)/shard_map/ppermute | solution.py:282
  24.8 2.1 %collective-permute-start.13 = (bf16[32,512]{1,0:T(8,128)(2,1)S(1)}, bf16[32,512]{1,0:T(8,128)(2,1)S(1)}, u32[]{:S(2)}, u32[]{:S(2)}) collective-permute-start(bf16[32,512]{1,0:T(8,128)(2,1)S(1)} %collective-permute-done.9.rest_3_), channel_id=1, source_target_pairs={{0,1},{1,0},{2,3},{3,2},{4,5},{5,4},{6,7},{7,6},{8,9},{9,8},{10,11... | collective-permute-start | bytes 98312 | tf_op jit(solution)/shard_map/ppermute | solution.py:282
  25.4 1.6 %collective-permute-start.12 = (bf16[32,512]{1,0:T(8,128)(2,1)S(1)}, bf16[32,512]{1,0:T(8,128)(2,1)S(1)}, u32[]{:S(2)}, u32[]{:S(2)}) collective-permute-start(bf16[32,512]{1,0:T(8,128)(2,1)S(1)} %collective-permute-done.8.rest_2_), channel_id=1, source_target_pairs={{0,1},{1,0},{2,3},{3,2},{4,5},{5,4},{6,7},{7,6},{8,9},{9,8},{10,11... | collective-permute-start | bytes 98312 | tf_op jit(solution)/shard_map/ppermute | solution.py:282
  25.9 1.2 %collective-permute-start.11 = (bf16[32,512]{1,0:T(8,128)(2,1)S(1)}, bf16[32,512]{1,0:T(8,128)(2,1)S(1)}, u32[]{:S(2)}, u32[]{:S(2)}) collective-permute-start(bf16[32,512]{1,0:T(8,128)(2,1)S(1)} %collective-permute-done.7.rest_1_), channel_id=1, source_target_pairs={{0,1},{1,0},{2,3},{3,2},{4,5},{5,4},{6,7},{7,6},{8,9},{9,8},{10,11... | collective-permute-start | bytes 98312 | tf_op jit(solution)/shard_map/ppermute | solution.py:282
  28.1 5.7 %collective-permute-start.14 = (f32[8,768]{1,0:T(8,128)S(1)}, f32[8,768]{1,0:T(8,128)S(1)}, u32[]{:S(2)}, u32[]{:S(2)}) collective-permute-start(f32[8,768]{1,0:T(8,128)S(1)} %get-tuple-element.16), channel_id=1, source_target_pairs={{0,8},{8,24},{24,16},{16,0},{1,9},{9,25},{25,17},{17,1},{2,10},{10... | collective-permute-start | bytes 73736 | tf_op jit(solution)/shard_map/ppermute | solution.py:288
  29.8 5.7 %collective-permute-start.15 = (f32[8,768]{1,0:T(8,128)S(1)}, f32[8,768]{1,0:T(8,128)S(1)}, u32[]{:S(2)}, u32[]{:S(2)}) collective-permute-start(f32[8,768]{1,0:T(8,128)S(1)} %get-tuple-element.17), channel_id=1, source_target_pairs={{0,24},{8,16},{24,0},{16,8},{1,25},{9,17},{25,1},{17,9},{2,26},{10... | collective-permute-start | bytes 73736 | tf_op jit(solution)/shard_map/ppermute | solution.py:288
  32.2 3.8 %collective-permute-start.16 = (f32[8,768]{1,0:T(8,128)S(1)}, f32[8,768]{1,0:T(8,128)S(1)}, u32[]{:S(2)}, u32[]{:S(2)}) collective-permute-start(f32[8,768]{1,0:T(8,128)S(1)} %get-tuple-element.18), channel_id=1, source_target_pairs={{0,16},{8,0},{24,8},{16,24},{1,17},{9,1},{25,9},{17,25},{2,18},{10... | collective-permute-start | bytes 73736 | tf_op jit(solution)/shard_map/ppermute | solution.py:288

commit v9 on v8

--- a/solution.py
+++ b/solution.py
@@ -301,6 +301,20 @@
     return pieces
 
 
+def add_up_kernel(*refs):
+    refs[-1][...] = sum(ref[...] for ref in refs[1:-1]) + refs[0][...]
+
+
+def add_up(arrays):
+    return pl.pallas_call(
+        add_up_kernel,
+        in_specs=[pl.BlockSpec(memory_space=pltpu.VMEM)] * len(arrays),
+        out_specs=pl.BlockSpec(memory_space=pltpu.VMEM),
+        out_shape=jax.ShapeDtypeStruct(arrays[0].shape, arrays[0].dtype),
+        name="add_up",
+    )(*arrays)
+
+
 def on_device(
     activations,
     out_grads,
@@ -328,10 +342,8 @@
     )
     column_part = precondition(pieces_of_all(feature, "row"), curvature, placer)
     shares = score(pieces_of_all(column_part, "row"), store_grads[0], queries, mod_count)
-    total = shares[0]
-    for places in range(1, mod_count):
-        total = total + send_on(shares[places], "mod", places)
-    return total
+    arrived = [send_on(shares[places], "mod", places) for places in range(1, mod_count)]
+    return add_up([shares[0], *arrived])
 
 
 def solution(mesh):

time: 36.8 us -> 38.8 us (1.054)
  Pallas kernels: 11.8 us -> 13.2 us
  local copies, waits for them, and re-layouts: 0.01 us -> 1.23 us
  other arithmetic: 0.62 us -> 0.01 us
    pallas_call x0 -> x1, Pallas kernels: none -> 1.41 us  [add_up(): pl.pallas_call(add_up_kernel, in_specs=[pl.BlockSpec(memory_space=pltpu.V...]
    unnamed x4 -> x12, local copies, waits for them, and re-layouts: 0.01 us -> 1.23 us
    add x1 -> x0, other arithmetic: 0.62 us -> none  [on_device(): total = total + send_on(shares[places], 'mod', places)]
  transfers between devices with their start and end apart: 17 -> 17, of which waited for: 11 -> 11; matrix products, arithmetic and copies ran while one was open for 0% -> 0% of each run, Pallas kernels for 3% -> 2%
where the time goes in v9:
time: 38.8 us; the launch traced here: 38.6 us
  starting transfers between devices  13.8 us (36%)
  Pallas kernels  13.2 us (34%)
  waiting for transfers between devices  10.3 us (27%)
  local copies, waits for them, and re-layouts  1.23 us (3%)
    pallas_call x1, Pallas kernels, featurize(): pl.pallas_call(featurize_kernel, in_specs=[pl.BlockSpec(memory_space=pl.A...  8.42 us
    ppermute x14, starting transfers between devices, exchange(): return lax.ppermute(array, axis, [(i, i ^ distance) for i in range(count)])  8.18 us
    ppermute x14, waiting for transfers between devices, exchange(): return lax.ppermute(array, axis, [(i, i ^ distance) for i in range(count)])  8.03 us
    ppermute x3, starting transfers between devices, send_on(): lax.ppermute(array, axis, [(order[i], order[(i + places) % count]) for i...  5.62 us
    ppermute x3, waiting for transfers between devices, send_on(): lax.ppermute(array, axis, [(order[i], order[(i + places) % count]) for i...  2.25 us
    pallas_call x1, Pallas kernels, precondition(): pl.pallas_call(precondition_kernel, in_specs=[pl.BlockSpec(memory_space=p...  1.45 us
    pallas_call x1, Pallas kernels, add_up(): pl.pallas_call(add_up_kernel, in_specs=[pl.BlockSpec(memory_space=pltpu.V...  1.41 us
    unnamed x12, local copies, waits for them, and re-layouts  1.23 us
  transfers between devices with their start and end apart: 17, of which 11 were waited for; matrix products, arithmetic and copies ran while one was open for 0% of the time, Pallas kernels for 2%

profile of v9, /device:TPU:0, one launch (start us, length us, event | category | flops | bytes accessed | tf_op | source)
XLA Modules:
  0.0 38.6 jit_solution(305682776032309844)
XLA Ops:
  0.0 8.4 %featurize.1 = (bf16[8,4096]{1,0:T(8,128)(2,1)S(1)}, f32[32,64]{1,0:T(8,128)S(1)}, bf16[512,4096]{1,0:T(8,128)(2,1)S(1)}) custom-call(s32[32]{0:T(128)} %lengths_hbm.1, s32[32]{0:T(128)} %owners_hbm.1, bf16[512,4096]{1,0:T(8,128)(2,1)} %bitcast.12, bf16[1024,4096]{1,0:T(8,128)(2,1)} %bitcast.10, bf16[1024,4096]{1,0:T(8,128)(2,1)} %bitcast.11, ...), custom_call_target="tpu_custom_call" | custom-call | tf_op jit(solution)/shard_map/featurize/pallas_call | solution.py:174
  8.4 4.0 %collective-permute-start.5 = (bf16[8,4096]{1,0:T(8,128)(2,1)S(1)}, bf16[8,4096]{1,0:T(8,128)(2,1)S(1)}, u32[]{:S(2)}, u32[]{:S(2)}) collective-permute-start(bf16[8,4096]{1,0:T(8,128)(2,1)S(1)} %get-tuple-element.14.rest_0_), channel_id=1, source_target_pairs={{0,6},{1,7},{2,4},{3,5},{4,2},{5,3},{6,0},{7,1},{8,14},{9,15},{10,... | collective-permute-start | bytes 196616 | tf_op jit(solution)/shard_map/ppermute | solution.py:282
  12.4 0.5 %collective-permute-start.3 = (bf16[8,4096]{1,0:T(8,128)(2,1)S(1)}, bf16[8,4096]{1,0:T(8,128)(2,1)S(1)}, u32[]{:S(2)}, u32[]{:S(2)}) collective-permute-start(bf16[8,4096]{1,0:T(8,128)(2,1)S(1)} %get-tuple-element.14.rest_0_), channel_id=1, source_target_pairs={{0,4},{1,5},{2,6},{3,7},{4,0},{5,1},{6,2},{7,3},{8,12},{9,13},{10,... | collective-permute-start | bytes 196616 | tf_op jit(solution)/shard_map/ppermute | solution.py:282
  13.0 1.6 %collective-permute-done.5.rest_6_ = bf16[8,4096]{1,0:T(8,128)(2,1)S(1)} collective-permute-done((bf16[8,4096]{1,0:T(8,128)(2,1)S(1)}, bf16[8,4096]{1,0:T(8,128)(2,1)S(1)}, u32[]{:S(2)}, u32[]{:S(2)}) %collective-permute-start.5) | collective-permute-done | bytes 65568 | tf_op jit(solution)/shard_map/ppermute | solution.py:282
  14.7 2.0 %collective-permute-done.3.rest_4_ = bf16[8,4096]{1,0:T(8,128)(2,1)S(1)} collective-permute-done((bf16[8,4096]{1,0:T(8,128)(2,1)S(1)}, bf16[8,4096]{1,0:T(8,128)(2,1)S(1)}, u32[]{:S(2)}, u32[]{:S(2)}) %collective-permute-start.3) | collective-permute-done | bytes 65568 | tf_op jit(solution)/shard_map/ppermute | solution.py:282
  17.2 0.7 %collective-permute-done.4.rest_5_ = bf16[8,4096]{1,0:T(8,128)(2,1)S(1)} collective-permute-done((bf16[8,4096]{1,0:T(8,128)(2,1)S(1)}, bf16[8,4096]{1,0:T(8,128)(2,1)S(1)}, u32[]{:S(2)}, u32[]{:S(2)}) %collective-permute-start.4) | collective-permute-done | bytes 65568 | tf_op jit(solution)/shard_map/ppermute | solution.py:282
  17.9 0.5 %collective-permute-done.2.rest_3_ = bf16[8,4096]{1,0:T(8,128)(2,1)S(1)} collective-permute-done((bf16[8,4096]{1,0:T(8,128)(2,1)S(1)}, bf16[8,4096]{1,0:T(8,128)(2,1)S(1)}, u32[]{:S(2)}, u32[]{:S(2)}) %collective-permute-start.2) | collective-permute-done | bytes 65568 | tf_op jit(solution)/shard_map/ppermute | solution.py:282
  18.4 1.4 %precondition.1.rest_0_ = bf16[32,512]{1,0:T(8,128)(2,1)S(1)} custom-call(bf16[512,4096]{1,0:T(8,128)(2,1)S(1)} %get-tuple-element.12.curvature_ref, f32[32,64]{1,0:T(8,128)S(1)} %get-tuple-element.13.placer_ref, bf16[8,4096]{1,0:T(8,128)(2,1)S(1)} %get-tuple-element.14.rest_0_, bf16[8,4096]{1,0:T(8,128)(2,1)S(1)} %collective-permute-done.rest_1_, ...), custom_call_target="tpu_custom_call" | custom-call | tf_op jit(solution)/shard_map/precondition/pallas_call | solution.py:219
  19.9 1.5 %collective-permute-start.9 = (bf16[32,512]{1,0:T(8,128)(2,1)S(1)}, bf16[32,512]{1,0:T(8,128)(2,1)S(1)}, u32[]{:S(2)}, u32[]{:S(2)}) collective-permute-start(bf16[32,512]{1,0:T(8,128)(2,1)S(1)} %precondition.1.rest_0_), channel_id=1, source_target_pairs={{0,6},{1,7},{2,4},{3,5},{4,2},{5,3},{6,0},{7,1},{8,14},{9,15},{10,... | collective-permute-start | bytes 98312 | tf_op jit(solution)/shard_map/ppermute | solution.py:282
  21.4 0.6 %collective-permute-start.8 = (bf16[32,512]{1,0:T(8,128)(2,1)S(1)}, bf16[32,512]{1,0:T(8,128)(2,1)S(1)}, u32[]{:S(2)}, u32[]{:S(2)}) collective-permute-start(bf16[32,512]{1,0:T(8,128)(2,1)S(1)} %precondition.1.rest_0_), channel_id=1, source_target_pairs={{0,4},{1,5},{2,6},{3,7},{4,0},{5,1},{6,2},{7,3},{8,12},{9,13},{10,... | collective-permute-start | bytes 98312 | tf_op jit(solution)/shard_map/ppermute | solution.py:282
  22.0 1.4 %collective-permute-start.7 = (bf16[32,512]{1,0:T(8,128)(2,1)S(1)}, bf16[32,512]{1,0:T(8,128)(2,1)S(1)}, u32[]{:S(2)}, u32[]{:S(2)}) collective-permute-start(bf16[32,512]{1,0:T(8,128)(2,1)S(1)} %precondition.1.rest_0_), channel_id=1, source_target_pairs={{0,2},{1,3},{2,0},{3,1},{4,6},{5,7},{6,4},{7,5},{8,10},{9,11},{10,... | collective-permute-start | bytes 98312 | tf_op jit(solution)/shard_map/ppermute | solution.py:282
  23.4 1.3 %collective-permute-done.9.rest_3_ = bf16[32,512]{1,0:T(8,128)(2,1)S(1)} collective-permute-done((bf16[32,512]{1,0:T(8,128)(2,1)S(1)}, bf16[32,512]{1,0:T(8,128)(2,1)S(1)}, u32[]{:S(2)}, u32[]{:S(2)}) %collective-permute-start.9) | collective-permute-done | bytes 32800 | tf_op jit(solution)/shard_map/ppermute | solution.py:282
  24.8 0.6 %collective-permute-done.8.rest_2_ = bf16[32,512]{1,0:T(8,128)(2,1)S(1)} collective-permute-done((bf16[32,512]{1,0:T(8,128)(2,1)S(1)}, bf16[32,512]{1,0:T(8,128)(2,1)S(1)}, u32[]{:S(2)}, u32[]{:S(2)}) %collective-permute-start.8) | collective-permute-done | bytes 32800 | tf_op jit(solution)/shard_map/ppermute | solution.py:282
  25.3 0.6 %collective-permute-done.7.rest_1_ = bf16[32,512]{1,0:T(8,128)(2,1)S(1)} collective-permute-done((bf16[32,512]{1,0:T(8,128)(2,1)S(1)}, bf16[32,512]{1,0:T(8,128)(2,1)S(1)}, u32[]{:S(2)}, u32[]{:S(2)}) %collective-permute-start.7) | collective-permute-done | bytes 32800 | tf_op jit(solution)/shard_map/ppermute | solution.py:282
  25.9 1.0 %early_score.1.early_ref = f32[768,32]{1,0:T(8,128)S(1)} custom-call(bf16[768,4096]{1,0:T(8,128)(2,1)S(1)} %bitcast.8, bf16[32,512]{1,0:T(8,128)(2,1)S(1)} %precondition.1.rest_0_, bf16[32,512]{1,0:T(8,128)(2,1)S(1)} %collective-permute-done.7.rest_1_, bf16[32,512]{1,0:T(8,128)(2,1)S(1)} %collective-permute-done.8.rest_2_, ...), custom_call_target="tpu_custom_call" | custom-call | tf_op jit(solution)/shard_map/early_score/pallas_call | solution.py:260
  27.1 1.0 %score.1 = (f32[8,768]{1,0:T(8,128)S(1)}, f32[8,768]{1,0:T(8,128)S(1)}, f32[8,768]{1,0:T(8,128)S(1)}, f32[8,768]{1,0:T(8,128)S(1)}) custom-call(f32[768,32]{1,0:T(8,128)S(1)} %early_score.1.early_ref, bf16[768,4096]{1,0:T(8,128)(2,1)S(1)} %bitcast.9, bf16[32,512]{1,0:T(8,128)(2,1)S(1)} %collective-permute-done.10.rest_0_, ...), custom_call_target="tpu_custom_call" | custom-call | tf_op jit(solution)/shard_map/score/pallas_call | solution.py:269
  28.1 0.6 %copy-done = f32[8,768]{1,0:T(8,128)} copy-done((f32[8,768]{1,0:T(8,128)}, f32[8,768]{1,0:T(8,128)S(1)}, u32[]{:S(2)}) %copy-start) | copy-done | bytes 24600
  28.7 1.6 %collective-permute-start.14 = (f32[8,768]{1,0:T(8,128)S(1)}, f32[8,768]{1,0:T(8,128)S(1)}, u32[]{:S(2)}, u32[]{:S(2)}) collective-permute-start(f32[8,768]{1,0:T(8,128)S(1)} %get-tuple-element.16), channel_id=1, source_target_pairs={{0,8},{8,24},{24,16},{16,0},{1,9},{9,25},{25,17},{17,1},{2,10},{10... | collective-permute-start | bytes 73736 | tf_op jit(solution)/shard_map/ppermute | solution.py:288
  30.3 2.5 %collective-permute-start.15 = (f32[8,768]{1,0:T(8,128)S(1)}, f32[8,768]{1,0:T(8,128)S(1)}, u32[]{:S(2)}, u32[]{:S(2)}) collective-permute-start(f32[8,768]{1,0:T(8,128)S(1)} %get-tuple-element.17), channel_id=1, source_target_pairs={{0,24},{8,16},{24,0},{16,8},{1,25},{9,17},{25,1},{17,9},{2,26},{10... | collective-permute-start | bytes 73736 | tf_op jit(solution)/shard_map/ppermute | solution.py:288
  32.8 1.6 %collective-permute-start.16 = (f32[8,768]{1,0:T(8,128)S(1)}, f32[8,768]{1,0:T(8,128)S(1)}, u32[]{:S(2)}, u32[]{:S(2)}) collective-permute-start(f32[8,768]{1,0:T(8,128)S(1)} %get-tuple-element.18), channel_id=1, source_target_pairs={{0,16},{8,0},{24,8},{16,24},{1,17},{9,1},{25,9},{17,25},{2,18},{10... | collective-permute-start | bytes 73736 | tf_op jit(solution)/shard_map/ppermute | solution.py:288
  34.4 1.7 %collective-permute-done.15.refs_2_ = f32[8,768]{1,0:T(8,128)S(1)} collective-permute-done((f32[8,768]{1,0:T(8,128)S(1)}, f32[8,768]{1,0:T(8,128)S(1)}, u32[]{:S(2)}, u32[]{:S(2)}) %collective-permute-start.15) | collective-permute-done | bytes 24608 | tf_op jit(solution)/shard_map/ppermute | solution.py:288
  36.0 0.6 %collective-permute-done.16.refs_3_ = f32[8,768]{1,0:T(8,128)S(1)} collective-permute-done((f32[8,768]{1,0:T(8,128)S(1)}, f32[8,768]{1,0:T(8,128)S(1)}, u32[]{:S(2)}, u32[]{:S(2)}) %collective-permute-start.16) | collective-permute-done | bytes 24608 | tf_op jit(solution)/shard_map/ppermute | solution.py:288
  36.6 0.6 %copy-done.3 = f32[8,768]{1,0:T(8,128)} copy-done((f32[8,768]{1,0:T(8,128)}, f32[8,768]{1,0:T(8,128)S(1)}, u32[]{:S(2)}) %copy-start.3) | copy-done | bytes 24600
  37.2 1.4 %add_up.1 = f32[8,768]{1,0:T(8,128)} custom-call(f32[8,768]{1,0:T(8,128)} %copy-done, f32[8,768]{1,0:T(8,128)} %copy-done.1, f32[8,768]{1,0:T(8,128)} %copy-done.2, f32[8,768]{1,0:T(8,128)} %copy-done.3), custom_call_target="tpu_custom_call" | custom-call | tf_op jit(solution)/shard_map/add_up/pallas_call | solution.py:309
  (28 shorter events, 0.9 us)
Async XLA Ops:
  0.0 25.9 %slice-start = ((s8[6291456]{0:T(1024)(128)(4,1)}), s8[4194304]{0:T(1024)(128)(4,1)S(1)}, s32[]{:S(2)}) async-start(s8[6291456]{0:T(1024)(128)(4,1)} %bitcast.6), calls=%async_computation | async-start | bytes 8388608
  0.0 25.9 %slice-start.1 = ((s8[6291456]{0:T(1024)(128)(4,1)}), s8[2097152]{0:T(1024)(128)(4,1)S(1)}, s32[]{:S(2)}) async-start(s8[6291456]{0:T(1024)(128)(4,1)} %bitcast.6), calls=%async_computation.1 | async-start | bytes 4194304
  8.4 6.2 %collective-permute-start.5 = (bf16[8,4096]{1,0:T(8,128)(2,1)S(1)}, bf16[8,4096]{1,0:T(8,128)(2,1)S(1)}, u32[]{:S(2)}, u32[]{:S(2)}) collective-permute-start(bf16[8,4096]{1,0:T(8,128)(2,1)S(1)} %get-tuple-element.14.rest_0_), channel_id=1, source_target_pairs={{0,6},{1,7},{2,4},{3,5},{4,2},{5,3},{6,0},{7,1},{8,14},{9,15},{10,... | collective-permute-start | bytes 196616 | tf_op jit(solution)/shard_map/ppermute | solution.py:282
  12.4 4.3 %collective-permute-start.3 = (bf16[8,4096]{1,0:T(8,128)(2,1)S(1)}, bf16[8,4096]{1,0:T(8,128)(2,1)S(1)}, u32[]{:S(2)}, u32[]{:S(2)}) collective-permute-start(bf16[8,4096]{1,0:T(8,128)(2,1)S(1)} %get-tuple-element.14.rest_0_), channel_id=1, source_target_pairs={{0,4},{1,5},{2,6},{3,7},{4,0},{5,1},{6,2},{7,3},{8,12},{9,13},{10,... | collective-permute-start | bytes 196616 | tf_op jit(solution)/shard_map/ppermute | solution.py:282
  12.9 4.3 %collective-permute-start.1 = (bf16[8,4096]{1,0:T(8,128)(2,1)S(1)}, bf16[8,4096]{1,0:T(8,128)(2,1)S(1)}, u32[]{:S(2)}, u32[]{:S(2)}) collective-permute-start(bf16[8,4096]{1,0:T(8,128)(2,1)S(1)} %get-tuple-element.14.rest_0_), channel_id=1, source_target_pairs={{0,2},{1,3},{2,0},{3,1},{4,6},{5,7},{6,4},{7,5},{8,10},{9,11},{10,... | collective-permute-start | bytes 196616 | tf_op jit(solution)/shard_map/ppermute | solution.py:282
  13.0 4.1 %collective-permute-start = (bf16[8,4096]{1,0:T(8,128)(2,1)S(1)}, bf16[8,4096]{1,0:T(8,128)(2,1)S(1)}, u32[]{:S(2)}, u32[]{:S(2)}) collective-permute-start(bf16[8,4096]{1,0:T(8,128)(2,1)S(1)} %get-tuple-element.14.rest_0_), channel_id=1, source_target_pairs={{0,1},{1,0},{2,3},{3,2},{4,5},{5,4},{6,7},{7,6},{8,9},{9,8},{10,11... | collective-permute-start | bytes 196616 | tf_op jit(solution)/shard_map/ppermute | solution.py:282
  14.7 2.5 %collective-permute-start.6 = (bf16[8,4096]{1,0:T(8,128)(2,1)S(1)}, bf16[8,4096]{1,0:T(8,128)(2,1)S(1)}, u32[]{:S(2)}, u32[]{:S(2)}) collective-permute-start(bf16[8,4096]{1,0:T(8,128)(2,1)S(1)} %collective-permute-done.5.rest_6_), channel_id=1, source_target_pairs={{0,1},{1,0},{2,3},{3,2},{4,5},{5,4},{6,7},{7,6},{8,9},{9,8},{10,11... | collective-permute-start | bytes 196616 | tf_op jit(solution)/shard_map/ppermute | solution.py:282
  16.7 1.3 %collective-permute-start.4 = (bf16[8,4096]{1,0:T(8,128)(2,1)S(1)}, bf16[8,4096]{1,0:T(8,128)(2,1)S(1)}, u32[]{:S(2)}, u32[]{:S(2)}) collective-permute-start(bf16[8,4096]{1,0:T(8,128)(2,1)S(1)} %collective-permute-done.3.rest_4_), channel_id=1, source_target_pairs={{0,1},{1,0},{2,3},{3,2},{4,5},{5,4},{6,7},{7,6},{8,9},{9,8},{10,11... | collective-permute-start | bytes 196616 | tf_op jit(solution)/shard_map/ppermute | solution.py:282
  17.2 1.3 %collective-permute-start.2 = (bf16[8,4096]{1,0:T(8,128)(2,1)S(1)}, bf16[8,4096]{1,0:T(8,128)(2,1)S(1)}, u32[]{:S(2)}, u32[]{:S(2)}) collective-permute-start(bf16[8,4096]{1,0:T(8,128)(2,1)S(1)} %collective-permute-done.1.rest_2_), channel_id=1, source_target_pairs={{0,1},{1,0},{2,3},{3,2},{4,5},{5,4},{6,7},{7,6},{8,9},{9,8},{10,11... | collective-permute-start | bytes 196616 | tf_op jit(solution)/shard_map/ppermute | solution.py:282
  19.9 4.9 %collective-permute-start.9 = (bf16[32,512]{1,0:T(8,128)(2,1)S(1)}, bf16[32,512]{1,0:T(8,128)(2,1)S(1)}, u32[]{:S(2)}, u32[]{:S(2)}) collective-permute-start(bf16[32,512]{1,0:T(8,128)(2,1)S(1)} %precondition.1.rest_0_), channel_id=1, source_target_pairs={{0,6},{1,7},{2,4},{3,5},{4,2},{5,3},{6,0},{7,1},{8,14},{9,15},{10,... | collective-permute-start | bytes 98312 | tf_op jit(solution)/shard_map/ppermute | solution.py:282
  21.4 3.9 %collective-permute-start.8 = (bf16[32,512]{1,0:T(8,128)(2,1)S(1)}, bf16[32,512]{1,0:T(8,128)(2,1)S(1)}, u32[]{:S(2)}, u32[]{:S(2)}) collective-permute-start(bf16[32,512]{1,0:T(8,128)(2,1)S(1)} %precondition.1.rest_0_), channel_id=1, source_target_pairs={{0,4},{1,5},{2,6},{3,7},{4,0},{5,1},{6,2},{7,3},{8,12},{9,13},{10,... | collective-permute-start | bytes 98312 | tf_op jit(solution)/shard_map/ppermute | solution.py:282
  22.0 3.9 %collective-permute-start.7 = (bf16[32,512]{1,0:T(8,128)(2,1)S(1)}, bf16[32,512]{1,0:T(8,128)(2,1)S(1)}, u32[]{:S(2)}, u32[]{:S(2)}) collective-permute-start(bf16[32,512]{1,0:T(8,128)(2,1)S(1)} %precondition.1.rest_0_), channel_id=1, source_target_pairs={{0,2},{1,3},{2,0},{3,1},{4,6},{5,7},{6,4},{7,5},{8,10},{9,11},{10,... | collective-permute-start | bytes 98312 | tf_op jit(solution)/shard_map/ppermute | solution.py:282
  23.4 3.5 %collective-permute-start.10 = (bf16[32,512]{1,0:T(8,128)(2,1)S(1)}, bf16[32,512]{1,0:T(8,128)(2,1)S(1)}, u32[]{:S(2)}, u32[]{:S(2)}) collective-permute-start(bf16[32,512]{1,0:T(8,128)(2,1)S(1)} %precondition.1.rest_0_), channel_id=1, source_target_pairs={{0,1},{1,0},{2,3},{3,2},{4,5},{5,4},{6,7},{7,6},{8,9},{9,8},{10,11... | collective-permute-start | bytes 98312 | tf_op jit(solution)/shard_map/ppermute | solution.py:282
  24.8 2.1 %collective-permute-start.13 = (bf16[32,512]{1,0:T(8,128)(2,1)S(1)}, bf16[32,512]{1,0:T(8,128)(2,1)S(1)}, u32[]{:S(2)}, u32[]{:S(2)}) collective-permute-start(bf16[32,512]{1,0:T(8,128)(2,1)S(1)} %collective-permute-done.9.rest_3_), channel_id=1, source_target_pairs={{0,1},{1,0},{2,3},{3,2},{4,5},{5,4},{6,7},{7,6},{8,9},{9,8},{10,11... | collective-permute-start | bytes 98312 | tf_op jit(solution)/shard_map/ppermute | solution.py:282
  25.3 1.6 %collective-permute-start.12 = (bf16[32,512]{1,0:T(8,128)(2,1)S(1)}, bf16[32,512]{1,0:T(8,128)(2,1)S(1)}, u32[]{:S(2)}, u32[]{:S(2)}) collective-permute-start(bf16[32,512]{1,0:T(8,128)(2,1)S(1)} %collective-permute-done.8.rest_2_), channel_id=1, source_target_pairs={{0,1},{1,0},{2,3},{3,2},{4,5},{5,4},{6,7},{7,6},{8,9},{9,8},{10,11... | collective-permute-start | bytes 98312 | tf_op jit(solution)/shard_map/ppermute | solution.py:282
  25.9 1.2 %collective-permute-start.11 = (bf16[32,512]{1,0:T(8,128)(2,1)S(1)}, bf16[32,512]{1,0:T(8,128)(2,1)S(1)}, u32[]{:S(2)}, u32[]{:S(2)}) collective-permute-start(bf16[32,512]{1,0:T(8,128)(2,1)S(1)} %collective-permute-done.7.rest_1_), channel_id=1, source_target_pairs={{0,1},{1,0},{2,3},{3,2},{4,5},{5,4},{6,7},{7,6},{8,9},{9,8},{10,11... | collective-permute-start | bytes 98312 | tf_op jit(solution)/shard_map/ppermute | solution.py:282
  28.1 0.6 %copy-start = (f32[8,768]{1,0:T(8,128)}, f32[8,768]{1,0:T(8,128)S(1)}, u32[]{:S(2)}) copy-start(f32[8,768]{1,0:T(8,128)S(1)} %get-tuple-element.15.refs_0_) | copy-start | bytes 73732
  28.7 5.6 %collective-permute-start.14 = (f32[8,768]{1,0:T(8,128)S(1)}, f32[8,768]{1,0:T(8,128)S(1)}, u32[]{:S(2)}, u32[]{:S(2)}) collective-permute-start(f32[8,768]{1,0:T(8,128)S(1)} %get-tuple-element.16), channel_id=1, source_target_pairs={{0,8},{8,24},{24,16},{16,0},{1,9},{9,25},{25,17},{17,1},{2,10},{10... | collective-permute-start | bytes 73736 | tf_op jit(solution)/shard_map/ppermute | solution.py:288
  30.3 5.7 %collective-permute-start.15 = (f32[8,768]{1,0:T(8,128)S(1)}, f32[8,768]{1,0:T(8,128)S(1)}, u32[]{:S(2)}, u32[]{:S(2)}) collective-permute-start(f32[8,768]{1,0:T(8,128)S(1)} %get-tuple-element.17), channel_id=1, source_target_pairs={{0,24},{8,16},{24,0},{16,8},{1,25},{9,17},{25,1},{17,9},{2,26},{10... | collective-permute-start | bytes 73736 | tf_op jit(solution)/shard_map/ppermute | solution.py:288
  32.8 3.8 %collective-permute-start.16 = (f32[8,768]{1,0:T(8,128)S(1)}, f32[8,768]{1,0:T(8,128)S(1)}, u32[]{:S(2)}, u32[]{:S(2)}) collective-permute-start(f32[8,768]{1,0:T(8,128)S(1)} %get-tuple-element.18), channel_id=1, source_target_pairs={{0,16},{8,0},{24,8},{16,24},{1,17},{9,1},{25,9},{17,25},{2,18},{10... | collective-permute-start | bytes 73736 | tf_op jit(solution)/shard_map/ppermute | solution.py:288
  34.4 2.3 %copy-start.1 = (f32[8,768]{1,0:T(8,128)}, f32[8,768]{1,0:T(8,128)S(1)}, u32[]{:S(2)}) copy-start(f32[8,768]{1,0:T(8,128)S(1)} %collective-permute-done.14.refs_1_) | copy-start | bytes 73732
  36.0 0.6 %copy-start.2 = (f32[8,768]{1,0:T(8,128)}, f32[8,768]{1,0:T(8,128)S(1)}, u32[]{:S(2)}) copy-start(f32[8,768]{1,0:T(8,128)S(1)} %collective-permute-done.15.refs_2_) | copy-start | bytes 73732
  36.6 0.6 %copy-start.3 = (f32[8,768]{1,0:T(8,128)}, f32[8,768]{1,0:T(8,128)S(1)}, u32[]{:S(2)}) copy-start(f32[8,768]{1,0:T(8,128)S(1)} %collective-permute-done.16.refs_3_) | copy-start | bytes 73732
